TPU v7x, 128 devices: a whole 4x4x4 slice. The times are simulated.
128 devices in a mesh: sub: 32 (over x, z, core), body: 4 (over y).
Axes of the slice: x: 4, y: 4, z: 4, core: 2. Of those that a mesh axis runs over, the one named last changes fastest.
Arguments:
- compliance: float32 [4, 32, 2400, 2400], P('body', 'sub'), may hold values from -1 to 4, as said below
- mortar: float32 [4, 32, 16, 64, 64], P('body', 'sub'), may hold values from -0.75 to 0.75
- rhs_glue: float32 [4, 32, 176, 128], P('body', 'sub'), may hold values from -6 to 6
- rhs_contact: float32 [4, 32, 16, 64, 128], P('body', 'sub'), may hold values from -6 to 6
- owner_sub: int32 [4, 32, 16, 1], P('body', 'sub'), may hold values from 0 to 31, as said below
- master_slot: int32 [4, 32, 16], P('body', 'sub'), may hold values from 0 to 15
- active_set: int32 [4, 32, 16, 64], P('body', 'sub'), may hold values 0 or 1
Outputs:
- multipliers_glue: float32 [4, 32, 176, 128], P('body', 'sub')
- multipliers_contact: float32 [4, 32, 16, 64, 128], P('body', 'sub')
- residual_glue: float32 [4, 32, 176, 128], P('body', 'sub')
- residual_contact: float32 [4, 32, 16, 64, 128], P('body', 'sub')
Inputs may be any that keep to these rules, and one draw needn't show every extreme that they name: `compliance`: symmetric positive definite for every subdomain. `owner_sub`: the master subdomain of a slave segment of subdomain (b, s) is (s + o) mod 32 with o in 0 .. 3. At most 8 slave segments of one subdomain name the same master subdomain, and every subdomain names one master subdomain exactly 8 times.
All inputs are finite; a program needn't handle non-finite values. No bound on the sum of `active_set` on one device may be relied on, other than what follows from the above.
Results may differ from a plain program's by a relative error of at most 0.00015.
Values sent between devices are 32-bit elements; how exact they have to be, the bound alone decides.
No kernel may reach another device: no remote copies, remote signals or barrier semaphores. Data moves between devices by JAX's collectives and lax.ppermute only.
A program may use at most 128 MiB of HBM per device.

v0:
```python
import jax
import jax.numpy as jnp
from jax import lax
from jax.sharding import PartitionSpec as P

W = 4
CAP = 8
ITERS = 2


highest = lax.Precision.HIGHEST


def shifted(value, axis, by):
    peers = lax.axis_size(axis)
    return lax.ppermute(value, axis, [(i, (i + by) % peers) for i in range(peers)])


def passed_along(value, axis, steps):
    count = lax.axis_size(axis)
    first, last = (max(0, -steps), min(count, count - steps))
    return lax.ppermute(value, axis, [(source, source + steps) for source in range(first, last)])


def window_send(hopped, window, per_peer):
    pieces = [hopped[:per_peer]]
    for offset in range(1, window):
        piece = hopped[offset * per_peer : (offset + 1) * per_peer]
        pieces.append(shifted(piece, "sub", offset))
    return jnp.concatenate(pieces, axis=0)


def window_slots(hopped, window, per_peer):
    pieces = [hopped[:per_peer]]
    for offset in range(1, window):
        piece = hopped[offset * per_peer : (offset + 1) * per_peer]
        pieces.append(shifted(piece, "sub", offset))
    return jnp.concatenate(pieces, axis=0)


def window_reply(reply, window, per_peer):
    pieces = [reply[:per_peer]]
    for offset in range(1, window):
        piece = reply[offset * per_peer : (offset + 1) * per_peer]
        pieces.append(shifted(piece, "sub", -offset))
    return jnp.concatenate(pieces, axis=0)


def route_slots(slot_out, window):
    hopped = shifted(slot_out, "body", 1)
    return window_slots(hopped, window, CAP)


def route_out(outgoing, window):
    hopped = shifted(outgoing, "body", 1)
    return window_send(hopped, window, CAP)


def route_back(reply, window):
    spread = window_reply(reply, window, CAP)
    return shifted(spread, "body", -1)


def column_sum(glue_part, contact_part):
    return jnp.sum(glue_part, axis=0) + jnp.sum(contact_part, axis=(0, 1))


def squares(res_glue, res_contact):
    return lax.psum(column_sum(res_glue * res_glue, res_contact * res_contact), ("sub", "body"))


def per_device(compliance, mortar, rhs_glue, rhs_contact, owner_sub, master_slot, active_set):
    schur_block = compliance[0, 0]
    blocks = mortar[0, 0]
    face_rows = rhs_glue.shape[2]
    seg_count = rhs_contact.shape[2]
    seg_dofs = rhs_contact.shape[3]
    load_cases = rhs_contact.shape[4]
    contact_rows = seg_count * seg_dofs
    owners = owner_sub[0, 0, :, 0]
    slots = master_slot[0, 0]
    mask = active_set[0, 0].astype(jnp.float32)[:, :, None]
    sub_count = lax.axis_size("sub")
    window = W
    seg_index = jnp.arange(seg_count, dtype=jnp.int32)
    earlier = (owners[:, None] == owners[None, :]) & (seg_index[None, :] < seg_index[:, None])
    ranks = jnp.sum(earlier.astype(jnp.int32), axis=1)
    peers = (owners - lax.axis_index("sub")) % sub_count
    position = peers * CAP + ranks
    buffer_rows = jnp.arange(window * CAP, dtype=jnp.int32)
    send_match = buffer_rows[:, None] == position[None, :]
    send_hot = send_match.astype(jnp.float32)
    slot_out = jnp.sum(jnp.where(send_match, slots[None, :] + 1, 0), axis=1) - 1
    recv_slots = route_slots(slot_out, window)
    recv_hot = (recv_slots[:, None] == seg_index[None, :]).astype(jnp.float32)
    res_glue = rhs_glue[0, 0]
    res_contact = rhs_contact[0, 0] * mask
    mult_glue = jnp.zeros_like(res_glue)
    mult_contact = jnp.zeros_like(res_contact)
    dir_glue, dir_contact = (res_glue, res_contact)
    norm_now = squares(res_glue, res_contact)
    for iteration in range(ITERS):
        payload = dir_contact.reshape(seg_count, seg_dofs * load_cases)
        outgoing = jnp.dot(send_hot, payload, precision=highest)
        incoming = route_out(outgoing, window)
        gathered = jnp.dot(recv_hot.T, incoming, precision=highest).reshape(
            seg_count, seg_dofs, load_cases
        )
        master_term = -jnp.einsum("jed,jel->jdl", blocks, gathered, precision=highest)
        left_glue = passed_along(dir_glue, "sub", 1)
        loads = jnp.concatenate(
            [
                -left_glue,
                dir_contact.reshape(contact_rows, load_cases),
                master_term.reshape(contact_rows, load_cases),
                dir_glue,
            ],
            axis=0,
        )
        displaced = jnp.dot(schur_block, loads, precision=highest)
        left_face = displaced[:face_rows]
        slave_part = displaced[face_rows : face_rows + contact_rows].reshape(
            seg_count, seg_dofs, load_cases
        )
        master_part = displaced[face_rows + contact_rows : face_rows + 2 * contact_rows].reshape(
            seg_count, seg_dofs, load_cases
        )
        right_face = displaced[face_rows + 2 * contact_rows :]
        next_left = passed_along(left_face, "sub", -1)
        image_glue = right_face - next_left
        projected = jnp.einsum("jde,jel->jdl", blocks, master_part, precision=highest)
        reply = jnp.dot(
            recv_hot, projected.reshape(seg_count, seg_dofs * load_cases), precision=highest
        )
        back = route_back(reply, window)
        fetched = jnp.dot(send_hot.T, back, precision=highest).reshape(
            seg_count, seg_dofs, load_cases
        )
        image_contact = (slave_part - fetched) * mask
        image_glue, image_contact = (image_glue, image_contact)
        curvature = lax.psum(
            column_sum(dir_glue * image_glue, dir_contact * image_contact), ("sub", "body")
        )
        alpha = norm_now / curvature
        mult_glue = mult_glue + alpha * dir_glue
        mult_contact = mult_contact + alpha * dir_contact
        res_glue = res_glue - alpha * image_glue
        res_contact = res_contact - alpha * image_contact
        if iteration + 1 < ITERS:
            norm_next = squares(res_glue, res_contact)
            ratio = norm_next / norm_now
            dir_glue = res_glue + ratio * dir_glue
            dir_contact = res_contact + ratio * dir_contact
            norm_now = norm_next
    return (
        mult_glue[None, None],
        mult_contact[None, None],
        res_glue[None, None],
        res_contact[None, None],
    )


def solution(mesh):
    in_specs = (
        P("body", "sub", None, None),
        P("body", "sub", None, None, None),
        P("body", "sub", None, None),
        P("body", "sub", None, None, None),
        P("body", "sub", None, None),
        P("body", "sub", None),
        P("body", "sub", None, None),
    )
    out_specs = (
        P("body", "sub", None, None),
        P("body", "sub", None, None, None),
        P("body", "sub", None, None),
        P("body", "sub", None, None, None),
    )
    return jax.shard_map(
        per_device, mesh=mesh, in_specs=in_specs, out_specs=out_specs, check_vma=False
    )
```

profile of v0, /device:TPU:1, one launch (start us, length us, event | category | flops | bytes accessed | tf_op | source)
XLA Modules:
  0.0 458.7 jit_solution(9640825414118254585)
XLA Ops:
  0.6 0.9 convert_reduce_fusion
  3.2 2.4 fusion.62
  5.6 2.2 collective-permute-start.5
  7.9 1.4 collective-permute-start.1
  9.3 4.7 %collective-permute-start = (f32[176,128]{1,0:T(8,128)S(1)}, f32[176,128]{1,0:T(8,128)S(1)}, u32[]{:S(2)}, u32[]{:S(2)}) collective-permute-start(f32[176,128]{1,0:T(8,128)S(1)} %bitcast.155), channel_id=1, source_target_pairs={{0,4},{4,8},{8,12},{12,16},{16,20},{20,24},{24,28},{28,32},{32,36}... | collective-permute-start | bytes 270344 | tf_op jit(solution)/shard_map/ppermute | solution.py:22
  14.2 17.9 %collective-permute-done.5 = f32[32,8192]{1,0:T(8,128)} collective-permute-done((f32[32,8192]{1,0:T(8,128)S(1)}, f32[32,8192]{1,0:T(8,128)}, u32[]{:S(2)}, u32[]{:S(2)}) %collective-permute-start.5) | collective-permute-done | bytes 1048608 | tf_op jit(solution)/shard_map/ppermute | solution.py:16
  32.1 1.3 fusion.85
  33.4 3.0 collective-permute-start.6
  36.3 1.6 collective-permute-start.7
  38.0 2.0 collective-permute-start.8
  40.1 10.9 %collective-permute-done.2 = s32[8]{0:T(128)S(1)} collective-permute-done((s32[8]{0:T(128)S(1)}, s32[8]{0:T(128)S(1)}, u32[]{:S(2)}, u32[]{:S(2)}) %collective-permute-start.2) | collective-permute-done | bytes 64 | tf_op jit(solution)/shard_map/ppermute | solution.py:16
  51.0 6.8 %collective-permute-done.3 = s32[8]{0:T(128)S(1)} collective-permute-done((s32[8]{0:T(128)S(1)}, s32[8]{0:T(128)S(1)}, u32[]{:S(2)}, u32[]{:S(2)}) %collective-permute-start.3) | collective-permute-done | bytes 64 | tf_op jit(solution)/shard_map/ppermute | solution.py:16
  57.8 7.6 %collective-permute-done.4 = s32[8]{0:T(128)S(1)} collective-permute-done((s32[8]{0:T(128)S(1)}, s32[8]{0:T(128)S(1)}, u32[]{:S(2)}, u32[]{:S(2)}) %collective-permute-start.4) | collective-permute-done | bytes 64 | tf_op jit(solution)/shard_map/ppermute | solution.py:16
  66.2 1.0 convolution_negate_fusion.1
  67.2 22.9 %fusion.4 = f32[2400,128]{1,0:T(8,128)S(1)} fusion(f32[1,1,2400,2400]{3,2,1,0:T(8,128)} %param.7, f32[176,128]{1,0:T(8,128)S(1)} %bitcast.156, f32[1024,128]{1,0:T(8,128)S(1)} %bitcast.158, f32[1024,128]{1,0:T(8,128)S(1)} %bitcast_multiply_fusion.2, f32[176,128]{1,0:T(8,128)S(1)} %neg.18), kind=kOutput, calls=%fused_computation.4 | convolution fusion | flops 8848281600 | bytes 25497600 | tf_op jit(solution)/shard_map/dot_general | solution.py:120
  91.7 6.0 %collective-permute-start.10 = (f32[8,8192]{1,0:T(8,128)S(1)}, f32[8,8192]{1,0:T(8,128)S(1)}, u32[]{:S(2)}, u32[]{:S(2)}) collective-permute-start(f32[8,8192]{1,0:T(8,128)S(1)} %get-tuple-element.29), channel_id=1, source_target_pairs={{0,124},{4,0},{8,4},{12,8},{16,12},{20,16},{24,20},{28,24},{32,28}... | collective-permute-start | bytes 786440 | tf_op jit(solution)/shard_map/ppermute | solution.py:16
  97.8 1.2 collective-permute-done.10
  98.9 8.2 %collective-permute-done.11 = f32[8,8192]{1,0:T(8,128)S(1)} collective-permute-done((f32[8,8192]{1,0:T(8,128)S(1)}, f32[8,8192]{1,0:T(8,128)S(1)}, u32[]{:S(2)}, u32[]{:S(2)}) %collective-permute-start.11) | collective-permute-done | bytes 262176 | tf_op jit(solution)/shard_map/ppermute | solution.py:16
  107.1 5.0 %collective-permute-done.12 = f32[8,8192]{1,0:T(8,128)S(1)} collective-permute-done((f32[8,8192]{1,0:T(8,128)S(1)}, f32[8,8192]{1,0:T(8,128)S(1)}, u32[]{:S(2)}, u32[]{:S(2)}) %collective-permute-start.12) | collective-permute-done | bytes 262176 | tf_op jit(solution)/shard_map/ppermute | solution.py:16
  112.1 1.7 collective-permute-start.13
  113.8 5.6 %collective-permute-start.9 = (f32[176,128]{1,0:T(8,128)S(1)}, f32[176,128]{1,0:T(8,128)S(1)}, u32[]{:S(2)}, u32[]{:S(2)}) collective-permute-start(f32[176,128]{1,0:T(8,128)S(1)} %slice.117), channel_id=1, source_target_pairs={{4,0},{8,4},{12,8},{16,12},{20,16},{24,20},{28,24},{32,28},{36,32}... | collective-permute-start | bytes 270344 | tf_op jit(solution)/shard_map/ppermute | solution.py:22
  119.4 0.9 collective-permute-done.9
  120.4 13.3 %collective-permute-done.13 = f32[32,8192]{1,0:T(8,128)S(1)} collective-permute-done((f32[32,8192]{1,0:T(8,128)S(1)}, f32[32,8192]{1,0:T(8,128)S(1)}, u32[]{:S(2)}, u32[]{:S(2)}) %collective-permute-start.13) | collective-permute-done | bytes 1048608 | tf_op jit(solution)/shard_map/ppermute | solution.py:16
  135.4 65.9 %all-reduce = (f32[128]{0:T(128)S(1)}, f32[128]{0:T(128)S(1)}) all-reduce(f32[128]{0:T(128)S(1)} %add.71, f32[128]{0:T(128)S(1)} %add.76), channel_id=1, replica_groups=mesh['sub'=32,'body'=4] {'sub','body'}, use_global_device_ids=true, to_apply=%region_2.3 | all-reduce | flops 256 | bytes 2048 | tf_op jit(solution)/shard_map/psum | solution.py:69
  202.7 64.4 %psum.30 = f32[128]{0:T(128)S(1)} all-reduce(f32[128]{0:T(128)S(1)} %add.77), channel_id=1, replica_groups=mesh['sub'=32,'body'=4] {'sub','body'}, use_global_device_ids=true, to_apply=%region_10.11 | all-reduce | flops 128 | bytes 1024 | tf_op jit(solution)/shard_map/psum | solution.py:69
  268.3 2.2 multiply_add_fusion.1
  270.5 1.9 reshape.178
  272.4 2.5 fusion.51
  275.0 24.8 %collective-permute-done.15 = f32[32,8192]{1,0:T(8,128)S(1)} collective-permute-done((f32[32,8192]{1,0:T(8,128)S(1)}, f32[32,8192]{1,0:T(8,128)S(1)}, u32[]{:S(2)}, u32[]{:S(2)}) %collective-permute-start.15) | collective-permute-done | bytes 1048608 | tf_op jit(solution)/shard_map/ppermute | solution.py:16
  299.8 1.3 collective-permute-start.16
  301.1 1.8 collective-permute-start.17
  302.9 0.9 collective-permute-start.18
  303.9 2.9 collective-permute-start.14
  306.8 9.9 %collective-permute-done.14 = f32[176,128]{1,0:T(8,128)S(1)} collective-permute-done((f32[176,128]{1,0:T(8,128)S(1)}, f32[176,128]{1,0:T(8,128)S(1)}, u32[]{:S(2)}, u32[]{:S(2)}) %collective-permute-start.14) | collective-permute-done | bytes 90144 | tf_op jit(solution)/shard_map/ppermute | solution.py:22
  316.7 4.3 collective-permute-done.17
  321.0 1.2 collective-permute-done.18
  322.8 1.0 convolution_negate_fusion
  323.9 22.9 %fusion.7 = f32[2400,128]{1,0:T(8,128)S(1)} fusion(f32[1,1,2400,2400]{3,2,1,0:T(8,128)} %param.7, f32[176,128]{1,0:T(8,128)S(1)} %multiply_add_fusion.2, f32[1024,128]{1,0:T(8,128)S(1)} %bitcast.157, f32[1024,128]{1,0:T(8,128)S(1)} %copy-done.7, f32[176,128]{1,0:T(8,128)S(1)} %neg.21), kind=kOutput, calls=%fused_computation.5 | convolution fusion | flops 8848281600 | bytes 25497600 | tf_op jit(solution)/shard_map/dot_general | solution.py:120
  348.4 1.8 collective-permute-start.21
  350.3 11.5 %collective-permute-done.20 = f32[8,8192]{1,0:T(8,128)S(1)} collective-permute-done((f32[8,8192]{1,0:T(8,128)S(1)}, f32[8,8192]{1,0:T(8,128)S(1)}, u32[]{:S(2)}, u32[]{:S(2)}) %collective-permute-start.20) | collective-permute-done | bytes 262176 | tf_op jit(solution)/shard_map/ppermute | solution.py:16
  361.8 2.6 collective-permute-done.22
  364.5 5.5 %collective-permute-start.19 = (f32[176,128]{1,0:T(8,128)S(1)}, f32[176,128]{1,0:T(8,128)S(1)}, u32[]{:S(2)}, u32[]{:S(2)}) collective-permute-start(f32[176,128]{1,0:T(8,128)S(1)} %slice.129), channel_id=1, source_target_pairs={{4,0},{8,4},{12,8},{16,12},{20,16},{24,20},{28,24},{32,28},{36,32}... | collective-permute-start | bytes 270344 | tf_op jit(solution)/shard_map/ppermute | solution.py:22
  370.0 1.0 collective-permute-done.19
  371.7 13.8 %collective-permute-done.23 = f32[32,8192]{1,0:T(8,128)S(1)} collective-permute-done((f32[32,8192]{1,0:T(8,128)S(1)}, f32[32,8192]{1,0:T(8,128)S(1)}, u32[]{:S(2)}, u32[]{:S(2)}) %collective-permute-start.23) | collective-permute-done | bytes 1048608 | tf_op jit(solution)/shard_map/ppermute | solution.py:16
  386.2 1.1 fusion.40
  387.2 67.3 %psum.31 = f32[128]{0:T(128)S(1)} all-reduce(f32[128]{0:T(128)S(1)} %add.82), channel_id=1, replica_groups=mesh['sub'=32,'body'=4] {'sub','body'}, use_global_device_ids=true, to_apply=%region_13.14 | all-reduce | flops 128 | bytes 1024 | tf_op jit(solution)/shard_map/psum | solution.py:141
  454.5 2.6 multiply_subtract_fusion
  457.1 1.6 subtract_bitcast_fusion
  (111 shorter events, 12.6 us)
Async XLA Ops:
  0.6 65.6 %copy-start = (f32[1,1,16,64,64]{4,3,2,1,0:T(8,128)S(1)}, f32[1,1,16,64,64]{4,3,2,1,0:T(8,128)}, u32[]{:S(2)}) copy-start(f32[1,1,16,64,64]{4,3,2,1,0:T(8,128)} %param.8) | copy-start | bytes 786436
  2.9 130.7 %copy-start.14 = (s32[16]{0:T(128)}, s32[16]{0:T(128)S(1)}, u32[]{:S(2)}) copy-start(s32[16]{0:T(128)S(1)} %fusion.76) | copy-start | bytes 196
  2.9 4.9 %copy-start.19 = (s32[1,1,16]{2,1,0:T(1,128)S(1)}, s32[1,1,16]{2,1,0:T(1,128)}, u32[]{:S(2)}) copy-start(s32[1,1,16]{2,1,0:T(1,128)} %param.12) | copy-start | bytes 196
  2.9 6.3 %copy-start.6 = (f32[1,1,176,128]{3,2,1,0:T(8,128)S(1)}, f32[1,1,176,128]{3,2,1,0:T(8,128)}, u32[]{:S(2)}) copy-start(f32[1,1,176,128]{3,2,1,0:T(8,128)} %param.9) | copy-start | bytes 270340
  3.0 11.1 %copy-start.1 = (f32[1,1,16,64,128]{4,3,2,1,0:T(8,128)S(1)}, f32[1,1,16,64,128]{4,3,2,1,0:T(8,128)}, u32[]{:S(2)}) copy-start(f32[1,1,16,64,128]{4,3,2,1,0:T(8,128)} %param.10) | copy-start | bytes 1572868
  3.2 63.0 %copy-start.3 = (f32[16,64,128]{2,1,0:T(8,128)}, f32[16,64,128]{2,1,0:T(8,128)S(1)}, u32[]{:S(2)}) copy-start(f32[16,64,128]{2,1,0:T(8,128)S(1)} %mul.221) | copy-start | bytes 1572868
  5.6 26.5 %collective-permute-start.5 = (f32[32,8192]{1,0:T(8,128)S(1)}, f32[32,8192]{1,0:T(8,128)}, u32[]{:S(2)}, u32[]{:S(2)}) collective-permute-start(f32[32,8192]{1,0:T(8,128)S(1)} %fusion.62), channel_id=1, source_target_pairs={{0,1},{1,2},{2,3},{3,0},{4,5},{5,6},{6,7},{7,4},{8,9},{9,10},{10,1... | collective-permute-start | bytes 3145736 | tf_op jit(solution)/shard_map/ppermute | solution.py:16
  7.9 32.1 %collective-permute-start.1 = (s32[32]{0:T(128)S(1)}, s32[32]{0:T(128)S(1)}, u32[]{:S(2)}, u32[]{:S(2)}) collective-permute-start(s32[32]{0:T(128)S(1)} %broadcast_add_fusion), channel_id=1, source_target_pairs={{0,1},{1,2},{2,3},{3,0},{4,5},{5,6},{6,7},{7,4},{8,9},{9,10},{10,1... | collective-permute-start | bytes 392 | tf_op jit(solution)/shard_map/ppermute | solution.py:16
  9.3 56.2 %collective-permute-start = (f32[176,128]{1,0:T(8,128)S(1)}, f32[176,128]{1,0:T(8,128)S(1)}, u32[]{:S(2)}, u32[]{:S(2)}) collective-permute-start(f32[176,128]{1,0:T(8,128)S(1)} %bitcast.155), channel_id=1, source_target_pairs={{0,4},{4,8},{8,12},{12,16},{16,20},{20,24},{24,28},{28,32},{32,36}... | collective-permute-start | bytes 270344 | tf_op jit(solution)/shard_map/ppermute | solution.py:22
  33.4 32.1 %collective-permute-start.6 = (f32[8,8192]{1,0:T(8,128)S(1)}, f32[8,8192]{1,0:T(8,128)S(1)}, u32[]{:S(2)}, u32[]{:S(2)}) collective-permute-start(f32[8,8192]{1,0:T(8,128)S(1)} %get-tuple-element.33), channel_id=1, source_target_pairs={{0,4},{4,8},{8,12},{12,16},{16,20},{20,24},{24,28},{28,32},{32,36}... | collective-permute-start | bytes 786440 | tf_op jit(solution)/shard_map/ppermute | solution.py:16
  36.3 29.2 %collective-permute-start.7 = (f32[8,8192]{1,0:T(8,128)S(1)}, f32[8,8192]{1,0:T(8,128)S(1)}, u32[]{:S(2)}, u32[]{:S(2)}) collective-permute-start(f32[8,8192]{1,0:T(8,128)S(1)} %get-tuple-element.32), channel_id=1, source_target_pairs={{0,8},{4,12},{8,16},{12,20},{16,24},{20,28},{24,32},{28,36},{32,40... | collective-permute-start | bytes 786440 | tf_op jit(solution)/shard_map/ppermute | solution.py:16
  38.0 27.5 %collective-permute-start.8 = (f32[8,8192]{1,0:T(8,128)S(1)}, f32[8,8192]{1,0:T(8,128)S(1)}, u32[]{:S(2)}, u32[]{:S(2)}) collective-permute-start(f32[8,8192]{1,0:T(8,128)S(1)} %get-tuple-element.31), channel_id=1, source_target_pairs={{0,12},{4,16},{8,20},{12,24},{16,28},{20,32},{24,36},{28,40},{32,4... | collective-permute-start | bytes 786440 | tf_op jit(solution)/shard_map/ppermute | solution.py:16
  40.1 10.9 %collective-permute-start.2 = (s32[8]{0:T(128)S(1)}, s32[8]{0:T(128)S(1)}, u32[]{:S(2)}, u32[]{:S(2)}) collective-permute-start(s32[8]{0:T(128)S(1)} %get-tuple-element.41), channel_id=1, source_target_pairs={{0,4},{4,8},{8,12},{12,16},{16,20},{20,24},{24,28},{28,32},{32,36}... | collective-permute-start | bytes 104 | tf_op jit(solution)/shard_map/ppermute | solution.py:16
  51.0 6.8 %collective-permute-start.3 = (s32[8]{0:T(128)S(1)}, s32[8]{0:T(128)S(1)}, u32[]{:S(2)}, u32[]{:S(2)}) collective-permute-start(s32[8]{0:T(128)S(1)} %get-tuple-element.40), channel_id=1, source_target_pairs={{0,8},{4,12},{8,16},{12,20},{16,24},{20,28},{24,32},{28,36},{32,40... | collective-permute-start | bytes 104 | tf_op jit(solution)/shard_map/ppermute | solution.py:16
  57.8 7.6 %collective-permute-start.4 = (s32[8]{0:T(128)S(1)}, s32[8]{0:T(128)S(1)}, u32[]{:S(2)}, u32[]{:S(2)}) collective-permute-start(s32[8]{0:T(128)S(1)} %get-tuple-element.39), channel_id=1, source_target_pairs={{0,12},{4,16},{8,20},{12,24},{16,28},{20,32},{24,36},{28,40},{32,4... | collective-permute-start | bytes 104 | tf_op jit(solution)/shard_map/ppermute | solution.py:16
  65.5 25.3 %copy-start.17 = (s32[32]{0:T(128)}, s32[32]{0:T(128)S(1)}, u32[]{:S(2)}) copy-start(s32[32]{0:T(128)S(1)} %pad_add_fusion) | copy-start | bytes 388
  91.7 7.2 %collective-permute-start.10 = (f32[8,8192]{1,0:T(8,128)S(1)}, f32[8,8192]{1,0:T(8,128)S(1)}, u32[]{:S(2)}, u32[]{:S(2)}) collective-permute-start(f32[8,8192]{1,0:T(8,128)S(1)} %get-tuple-element.29), channel_id=1, source_target_pairs={{0,124},{4,0},{8,4},{12,8},{16,12},{20,16},{24,20},{28,24},{32,28}... | collective-permute-start | bytes 786440 | tf_op jit(solution)/shard_map/ppermute | solution.py:16
  97.7 9.3 %collective-permute-start.11 = (f32[8,8192]{1,0:T(8,128)S(1)}, f32[8,8192]{1,0:T(8,128)S(1)}, u32[]{:S(2)}, u32[]{:S(2)}) collective-permute-start(f32[8,8192]{1,0:T(8,128)S(1)} %get-tuple-element.28), channel_id=1, source_target_pairs={{0,120},{4,124},{8,0},{12,4},{16,8},{20,12},{24,16},{28,20},{32,24... | collective-permute-start | bytes 786440 | tf_op jit(solution)/shard_map/ppermute | solution.py:16
  97.8 14.3 %collective-permute-start.12 = (f32[8,8192]{1,0:T(8,128)S(1)}, f32[8,8192]{1,0:T(8,128)S(1)}, u32[]{:S(2)}, u32[]{:S(2)}) collective-permute-start(f32[8,8192]{1,0:T(8,128)S(1)} %get-tuple-element.27), channel_id=1, source_target_pairs={{0,116},{4,120},{8,124},{12,0},{16,4},{20,8},{24,12},{28,16},{32,2... | collective-permute-start | bytes 786440 | tf_op jit(solution)/shard_map/ppermute | solution.py:16
  112.1 21.5 %collective-permute-start.13 = (f32[32,8192]{1,0:T(8,128)S(1)}, f32[32,8192]{1,0:T(8,128)S(1)}, u32[]{:S(2)}, u32[]{:S(2)}) collective-permute-start(f32[32,8192]{1,0:T(8,128)S(1)} %pad_maximum_fusion), channel_id=1, source_target_pairs={{0,3},{1,0},{2,1},{3,2},{4,7},{5,4},{6,5},{7,6},{8,11},{9,8},{10,9... | collective-permute-start | bytes 3145736 | tf_op jit(solution)/shard_map/ppermute | solution.py:16
  113.8 6.5 %collective-permute-start.9 = (f32[176,128]{1,0:T(8,128)S(1)}, f32[176,128]{1,0:T(8,128)S(1)}, u32[]{:S(2)}, u32[]{:S(2)}) collective-permute-start(f32[176,128]{1,0:T(8,128)S(1)} %slice.117), channel_id=1, source_target_pairs={{4,0},{8,4},{12,8},{16,12},{20,16},{24,20},{28,24},{32,28},{36,32}... | collective-permute-start | bytes 270344 | tf_op jit(solution)/shard_map/ppermute | solution.py:22
  201.3 0.5 copy-start.22
  267.1 0.5 copy-start.20
  268.3 2.2 copy-start.12
  268.3 4.1 copy-start.15
  274.9 29.0 %copy-start.8 = (f32[176,128]{1,0:T(8,128)S(1)}, f32[176,128]{1,0:T(8,128)}, u32[]{:S(2)}) copy-start(f32[176,128]{1,0:T(8,128)} %get-tuple-element.13) | copy-start | bytes 270340
  274.9 29.0 %copy-start.13 = (f32[128]{0:T(128)S(1)}, f32[128]{0:T(128)}, u32[]{:S(2)}) copy-start(f32[128]{0:T(128)} %copy-done.12) | copy-start | bytes 1540
  274.9 47.2 %copy-start.18 = (s32[32]{0:T(128)S(1)}, s32[32]{0:T(128)}, u32[]{:S(2)}) copy-start(s32[32]{0:T(128)} %copy-done.17) | copy-start | bytes 388
  274.9 24.8 %collective-permute-start.15 = (f32[32,8192]{1,0:T(8,128)S(1)}, f32[32,8192]{1,0:T(8,128)S(1)}, u32[]{:S(2)}, u32[]{:S(2)}) collective-permute-start(f32[32,8192]{1,0:T(8,128)S(1)} %fusion.51), channel_id=1, source_target_pairs={{0,1},{1,2},{2,3},{3,0},{4,5},{5,6},{6,7},{7,4},{8,9},{9,10},{10,1... | collective-permute-start | bytes 3145736 | tf_op jit(solution)/shard_map/ppermute | solution.py:16
  299.8 16.9 %collective-permute-start.16 = (f32[8,8192]{1,0:T(8,128)S(1)}, f32[8,8192]{1,0:T(8,128)S(1)}, u32[]{:S(2)}, u32[]{:S(2)}) collective-permute-start(f32[8,8192]{1,0:T(8,128)S(1)} %get-tuple-element.25), channel_id=1, source_target_pairs={{0,4},{4,8},{8,12},{12,16},{16,20},{20,24},{24,28},{28,32},{32,36}... | collective-permute-start | bytes 786440 | tf_op jit(solution)/shard_map/ppermute | solution.py:16
  301.1 19.9 %collective-permute-start.17 = (f32[8,8192]{1,0:T(8,128)S(1)}, f32[8,8192]{1,0:T(8,128)S(1)}, u32[]{:S(2)}, u32[]{:S(2)}) collective-permute-start(f32[8,8192]{1,0:T(8,128)S(1)} %get-tuple-element.24), channel_id=1, source_target_pairs={{0,8},{4,12},{8,16},{12,20},{16,24},{20,28},{24,32},{28,36},{32,40... | collective-permute-start | bytes 786440 | tf_op jit(solution)/shard_map/ppermute | solution.py:16
  302.9 19.2 %collective-permute-start.18 = (f32[8,8192]{1,0:T(8,128)S(1)}, f32[8,8192]{1,0:T(8,128)S(1)}, u32[]{:S(2)}, u32[]{:S(2)}) collective-permute-start(f32[8,8192]{1,0:T(8,128)S(1)} %get-tuple-element.23), channel_id=1, source_target_pairs={{0,12},{4,16},{8,20},{12,24},{16,28},{20,32},{24,36},{28,40},{32,4... | collective-permute-start | bytes 786440 | tf_op jit(solution)/shard_map/ppermute | solution.py:16
  303.9 12.8 %collective-permute-start.14 = (f32[176,128]{1,0:T(8,128)S(1)}, f32[176,128]{1,0:T(8,128)S(1)}, u32[]{:S(2)}, u32[]{:S(2)}) collective-permute-start(f32[176,128]{1,0:T(8,128)S(1)} %multiply_add_fusion.2), channel_id=1, source_target_pairs={{0,4},{4,8},{8,12},{12,16},{16,20},{20,24},{24,28},{28,32},{32,36}... | collective-permute-start | bytes 270344 | tf_op jit(solution)/shard_map/ppermute | solution.py:22
  322.7 1.1 copy-start.7
  346.8 39.3 %copy-start.2 = (f32[2400,128]{1,0:T(8,128)}, f32[2400,128]{1,0:T(8,128)S(1)}, u32[]{:S(2)}) copy-start(f32[2400,128]{1,0:T(8,128)S(1)} %fusion.7) | copy-start | bytes 3686404
  348.3 13.4 %collective-permute-start.20 = (f32[8,8192]{1,0:T(8,128)S(1)}, f32[8,8192]{1,0:T(8,128)S(1)}, u32[]{:S(2)}, u32[]{:S(2)}) collective-permute-start(f32[8,8192]{1,0:T(8,128)S(1)} %get-tuple-element.21), channel_id=1, source_target_pairs={{0,124},{4,0},{8,4},{12,8},{16,12},{20,16},{24,20},{28,24},{32,28}... | collective-permute-start | bytes 786440 | tf_op jit(solution)/shard_map/ppermute | solution.py:16
  348.4 13.3 %collective-permute-start.21 = (f32[8,8192]{1,0:T(8,128)S(1)}, f32[8,8192]{1,0:T(8,128)S(1)}, u32[]{:S(2)}, u32[]{:S(2)}) collective-permute-start(f32[8,8192]{1,0:T(8,128)S(1)} %get-tuple-element.20), channel_id=1, source_target_pairs={{0,120},{4,124},{8,0},{12,4},{16,8},{20,12},{24,16},{28,20},{32,24... | collective-permute-start | bytes 786440 | tf_op jit(solution)/shard_map/ppermute | solution.py:16
  350.3 14.1 %collective-permute-start.22 = (f32[8,8192]{1,0:T(8,128)S(1)}, f32[8,8192]{1,0:T(8,128)S(1)}, u32[]{:S(2)}, u32[]{:S(2)}) collective-permute-start(f32[8,8192]{1,0:T(8,128)S(1)} %get-tuple-element.19), channel_id=1, source_target_pairs={{0,116},{4,120},{8,124},{12,0},{16,4},{20,8},{24,12},{28,16},{32,2... | collective-permute-start | bytes 786440 | tf_op jit(solution)/shard_map/ppermute | solution.py:16
  364.3 21.2 %copy-start.16 = (s32[16]{0:T(128)S(1)}, s32[16]{0:T(128)}, u32[]{:S(2)}) copy-start(s32[16]{0:T(128)} %copy-done.14) | copy-start | bytes 196
  364.4 21.1 %collective-permute-start.23 = (f32[32,8192]{1,0:T(8,128)S(1)}, f32[32,8192]{1,0:T(8,128)S(1)}, u32[]{:S(2)}, u32[]{:S(2)}) collective-permute-start(f32[32,8192]{1,0:T(8,128)S(1)} %pad_maximum_fusion.1), channel_id=1, source_target_pairs={{0,3},{1,0},{2,1},{3,2},{4,7},{5,4},{6,5},{7,6},{8,11},{9,8},{10,9... | collective-permute-start | bytes 3145736 | tf_op jit(solution)/shard_map/ppermute | solution.py:16
  364.5 6.5 %collective-permute-start.19 = (f32[176,128]{1,0:T(8,128)S(1)}, f32[176,128]{1,0:T(8,128)S(1)}, u32[]{:S(2)}, u32[]{:S(2)}) collective-permute-start(f32[176,128]{1,0:T(8,128)S(1)} %slice.129), channel_id=1, source_target_pairs={{4,0},{8,4},{12,8},{16,12},{20,16},{24,20},{28,24},{32,28},{36,32}... | collective-permute-start | bytes 270344 | tf_op jit(solution)/shard_map/ppermute | solution.py:22
  371.0 0.6 copy-start.10
  386.1 1.1 copy-start.5
  386.1 68.4 %copy-start.21 = (f32[128]{0:T(128)S(1)}, f32[128]{0:T(128)}, u32[]{:S(2)}) copy-start(f32[128]{0:T(128)} %copy-done.20) | copy-start | bytes 1540
  386.1 68.4 %copy-start.4 = (f32[1024,128]{1,0:T(8,128)S(1)}, f32[1024,128]{1,0:T(8,128)}, u32[]{:S(2)}) copy-start(f32[1024,128]{1,0:T(8,128)} %get-tuple-element.17) | copy-start | bytes 1572868
  454.5 2.6 copy-start.9
  454.5 2.6 copy-start.11
where the time goes:
time: 459 us
  blocking collectives  198 us (43%)
  waiting for transfers between devices  141 us (31%)
  matrix products  57.7 us (13%)
  starting transfers between devices  42.7 us (9%)
  other arithmetic  12.1 us (3%)
  local copies, waits for them, and re-layouts  6.85 us (1%)
    psum x2, blocking collectives, squares(): lax.psum(column_sum(res_glue * res_glue, res_contact * res_contact), ('su...  130 us
    ppermute x20, waiting for transfers between devices, shifted(): lax.ppermute(value, axis, [(i, (i + by) % peers) for i in range(peers)])  129 us
    psum x1, blocking collectives, per_device(): lax.psum(column_sum(dir_glue * image_glue, dir_contact * image_contact),...  67.3 us
    dot_general x2, matrix products, per_device(): displaced = jnp.dot(schur_block, loads, precision=highest)  45.8 us
    ppermute x20, starting transfers between devices, shifted(): lax.ppermute(value, axis, [(i, (i + by) % peers) for i in range(peers)])  24 us
    ppermute x4, starting transfers between devices, passed_along(): lax.ppermute(value, axis, [(source, source + steps) for source in range(f...  18.7 us
    ppermute x4, waiting for transfers between devices, passed_along(): lax.ppermute(value, axis, [(source, source + steps) for source in range(f...  11.8 us
  transfers between devices with their start and end apart: 24, of which 17 were waited for; matrix products, arithmetic and copies ran while one was open for 0% of the time, Pallas kernels for 0%

commit v1 on v0

v1 whole, which is shorter than its diff:
```python
import jax
import jax.numpy as jnp
from jax import lax
from jax.experimental import pallas as pl
from jax.experimental.pallas import tpu as pltpu
from jax.sharding import PartitionSpec as P

W = 4
CAP = 8
SLOTS = W * CAP
SEG = 16
SD = 64
LC = 128
G = 176
NS = 2400
CR = SEG * SD
MASTER = G + CR
RIGHT = G + 2 * CR
KP = 2560
K_LOW, K_WIDE = 1152, 1152
TILE = 480
TILES = NS // TILE
INFO = CAP * SD
MIB = 1 << 20

f32 = jnp.float32
bf16 = jnp.bfloat16
highest = lax.Precision.HIGHEST
VM = pl.BlockSpec(memory_space=pltpu.VMEM)
SM = pl.BlockSpec(memory_space=pltpu.SMEM)
ANY = pl.BlockSpec(memory_space=pl.ANY)


def rows(start, size):
    return pl.ds(pl.multiple_of(start, 8), size)


def halves(value):
    high = value.astype(bf16)
    low = (value - high.astype(f32)).astype(bf16)
    return high, low


def product(high, low, both):
    first = jnp.dot(high, both, preferred_element_type=f32)
    second = jnp.dot(low, both, preferred_element_type=f32)
    return (first[:, LC:] + second[:, LC:]) + second[:, :LC] + first[:, :LC]


def pack_kernel(me, owner, slot, act, rhs, out0, out1, out2, out3, pc, mask, source, place, act_wide, count):
    outs = (out0, out1, out2, out3)
    for i in range(SLOTS):
        source[i] = -1
    for o in range(W):
        count[o] = 0
    for k in range(SEG):
        o = lax.rem(owner[k] - me[0] + 32, 32)
        n = count[o]
        source[o * CAP + n] = k
        place[k] = o * CAP + n
        count[o] = n + 1
    active = act[...].astype(f32)
    act_wide[...] = jnp.concatenate([active, jnp.zeros((SEG, 128 - SD), f32)], axis=1)
    columns = jnp.transpose(jnp.concatenate([act_wide[...], jnp.zeros((128 - SEG, 128), f32)], axis=0))
    for k in range(SEG):
        wide = jnp.broadcast_to(columns[:SD, k : k + 1], (SD, LC))
        mask[k * SD : (k + 1) * SD, :] = wide
        pc[k * SD : (k + 1) * SD, :] = rhs[k * SD : (k + 1) * SD, :] * wide
    lane = lax.broadcasted_iota(jnp.int32, (1, 128), 1)
    for o in range(W):
        for n in range(CAP):
            k = source[o * CAP + n]
            at = jnp.maximum(k, 0)
            used = jnp.where(k >= 0, 1.0, 0.0).astype(f32)
            outs[o][n * SD : (n + 1) * SD, :] = pc[rows(at * SD, SD), :] * used
            tag = (slot[at] + 1).astype(f32)
            outs[o][INFO + n : INFO + n + 1, :] = used * jnp.where(lane == SD, tag, act_wide[pl.ds(at, 1), :])


def split_kernel(c_ref, left, pc, pg, high, low, partial, both):
    @pl.when(pl.program_id(0) == 0)
    def _():
        both[...] = jnp.zeros_like(both)
        for start, size, ref, sign in ((0, G, left, -1.0), (G, CR, pc, 1.0), (RIGHT, G, pg, 1.0)):
            part_high, part_low = halves(ref[...] * sign)
            both[start : start + size, :LC] = part_high
            both[start : start + size, LC:] = part_low

    part_high, part_low = halves(c_ref[...])
    pad = jnp.zeros((part_high.shape[0], KP - NS), bf16)
    high[:, :NS] = part_high
    high[:, NS:] = pad
    low[:, :NS] = part_low
    low[:, NS:] = pad
    partial[...] = product(high[...], low[...], both[...])


def start_tiles(high_any, low_any, high, low, sems, first, width):
    copies = []
    for i in range(TILES):
        at = pl.ds(i * TILE, TILE)
        pair = []
        for half, (src, dst) in enumerate(((high_any, high), (low_any, low))):
            copy = pltpu.make_async_copy(src.at[at, pl.ds(first, width)], dst.at[at, :], sems.at[half, i])
            copy.start()
            pair.append(copy)
        copies.append(pair)
    return copies


def mortar_apply(mortar, source, j, transposed):
    block = mortar[j * SD : (j + 1) * SD, :]
    dims = (((0,), (0,)), ((), ())) if transposed else (((1,), (0,)), ((), ()))
    return lax.dot_general(block, source, dims, precision=highest, preferred_element_type=f32)


def column_sum(value):
    return jnp.sum(value, axis=0, keepdims=True)


def first_kernel(
    in0, in1, in2, in3, mortar, left, pc, pg, partial, mask, source, high_any, low_any,
    f0, f1, f2, f3, p0, p1, p2, p3, u, term, projected, actives, slots, sums, left_face, right_face,
    gathered, both, high, low, info, sems, info_sems,
):
    copies = start_tiles(high_any, low_any, high, low, sems, K_LOW, K_WIDE)
    ins = (in0, in1, in2, in3)
    infos = []
    for o in range(W):
        copy = pltpu.make_async_copy(ins[o].at[pl.ds(INFO, 8), :], info.at[pl.ds(o * 8, 8), :], info_sems.at[o])
        copy.start()
        infos.append(copy)
    gathered[...] = jnp.zeros_like(gathered)
    actives[...] = jnp.zeros_like(actives)
    both[...] = jnp.zeros_like(both)
    for copy in infos:
        copy.wait()
    for o in range(W):
        tile = jnp.concatenate([ins[o][INFO : INFO + 8, :], jnp.zeros((120, 128), f32)], axis=0)
        columns = jnp.transpose(tile)
        for n in range(CAP):
            j = info[o * 8 + n, SD].astype(jnp.int32) - 1
            slots[o * CAP + n] = j
            at = rows(jnp.maximum(j, 0) * SD, SD)
            gathered[at, :] += ins[o][n * SD : (n + 1) * SD, :]
            actives[at, :] += jnp.broadcast_to(columns[:SD, n : n + 1], (SD, LC))
    for j in range(SEG):
        value = -mortar_apply(mortar, gathered[j * SD : (j + 1) * SD, :], j, True)
        term[j * SD : (j + 1) * SD, :] = value
        part_high, part_low = halves(value)
        start = MASTER - K_LOW + j * SD
        both[start : start + SD, :LC] = part_high
        both[start : start + SD, LC:] = part_low
    for i in range(TILES):
        at = slice(i * TILE, (i + 1) * TILE)
        for copy in copies[i]:
            copy.wait()
        u[at, :] = partial[at, :] + product(high[at, :], low[at, :], both[...])
    left_face[...] = u[:G, :]
    right_face[...] = u[RIGHT:, :]
    for j in range(SEG):
        start = MASTER + j * SD
        projected[j * SD : (j + 1) * SD, :] = mortar_apply(mortar, u[start : start + SD, :], j, False)
    forward, reply = (f0, f1, f2, f3), (p0, p1, p2, p3)
    for o in range(W):
        for n in range(CAP):
            to = slice(n * SD, (n + 1) * SD)
            k = source[o * CAP + n]
            at = jnp.maximum(k, 0)
            used = jnp.where(k >= 0, 1.0, 0.0).astype(f32)
            forward[o][to, :] = u[rows(G + at * SD, SD), :] * mask[rows(at * SD, SD), :] * used
            j = jnp.maximum(slots[o * CAP + n], 0)
            reply[o][to, :] = projected[rows(j * SD, SD), :]
    norm = column_sum(pg[...] * pg[...]) + column_sum(pc[...] * pc[...])
    curvature = (
        column_sum(pg[...] * u[RIGHT:, :])
        - column_sum(left[...] * u[:G, :])
        + column_sum(pc[...] * u[G:MASTER, :])
        + column_sum(term[...] * u[MASTER:RIGHT, :])
    )
    sums[...] = jnp.concatenate([norm, curvature, jnp.zeros((6, LC), f32)], axis=0)


def second_kernel(
    me, slots, place, f0, f1, f2, f3, b0, b1, b2, b3, next_left, prev_right, u0, projected0, actives, mask,
    mortar, left0, pc, pg, term0, sums0, high_any, low_any,
    p0, p1, p2, p3, u, q_glue, q_contact, sums, left_face,
    gathered, loads, both, high, low, projected, sems,
):
    copies = start_tiles(high_any, low_any, high, low, sems, 0, KP)
    forward, back, reply = (f0, f1, f2, f3), (b0, b1, b2, b3), (p0, p1, p2, p3)
    inner = jnp.where(me[0] > 0, 1.0, 0.0).astype(f32)
    loads[:G, :] = (u0[:G, :] - prev_right[...]) * inner
    glue = u0[RIGHT:, :] - next_left[...]
    q_glue[...] = glue
    loads[RIGHT:, :] = glue
    gathered[...] = -(actives[...] * projected0[...])
    for o in range(W):
        for n in range(CAP):
            at = rows(jnp.maximum(slots[o * CAP + n], 0) * SD, SD)
            gathered[at, :] += forward[o][n * SD : (n + 1) * SD, :]
    for k in range(SEG):
        seat = place[k]
        o, n = lax.div(seat, CAP), lax.rem(seat, CAP)
        here = slice(k * SD, (k + 1) * SD)
        fetched = jnp.zeros((SD, LC), f32)
        for w in range(W):
            fetched = jnp.where(o == w, back[w][rows(n * SD, SD), :], fetched)
        value = mask[here, :] * (u0[G + k * SD : G + (k + 1) * SD, :] - fetched)
        q_contact[here, :] = value
        loads[G + k * SD : G + (k + 1) * SD, :] = value
    for j in range(SEG):
        value = -mortar_apply(mortar, gathered[j * SD : (j + 1) * SD, :], j, True)
        loads[MASTER + j * SD : MASTER + (j + 1) * SD, :] = value
    part_high, part_low = halves(loads[...])
    both[:NS, :LC] = part_high
    both[:NS, LC:] = part_low
    both[NS:, :] = jnp.zeros((KP - NS, 2 * LC), bf16)
    for i in range(TILES):
        at = slice(i * TILE, (i + 1) * TILE)
        for copy in copies[i]:
            copy.wait()
        u[at, :] = product(high[at, :], low[at, :], both[...])
    left_face[...] = u[:G, :]
    for j in range(SEG):
        start = MASTER + j * SD
        projected[j * SD : (j + 1) * SD, :] = mortar_apply(mortar, u[start : start + SD, :], j, False)
    for o in range(W):
        for n in range(CAP):
            j = jnp.maximum(slots[o * CAP + n], 0)
            reply[o][n * SD : (n + 1) * SD, :] = projected[rows(j * SD, SD), :]
    alpha = sums0[0:1, :] / sums0[1:2, :]
    res_glue = pg[...] - alpha * q_glue[...]
    res_contact = pc[...] - alpha * q_contact[...]
    norm = column_sum(res_glue * res_glue) + column_sum(res_contact * res_contact)
    own = jnp.zeros((1, LC), f32)
    cross = jnp.zeros((1, LC), f32)
    for start, size, first, sign in ((0, G, left0, -1.0), (G, CR, pc, 1.0), (MASTER, CR, term0, 1.0), (RIGHT, G, pg, 1.0)):
        at = slice(start, start + size)
        load = first[...] * sign - alpha * loads[at, :]
        own = own + column_sum(load * (u0[at, :] - alpha * u[at, :]))
        cross = cross + column_sum(load * u0[at, :])
    sums[...] = jnp.concatenate([norm, own, cross, jnp.zeros((5, LC), f32)], axis=0)


def last_kernel(
    place, b0, b1, b2, b3, next_left, u, q_glue, q_contact, pc, pg, mask, sums0, sums1,
    mult_glue, mult_contact, res_glue, res_contact,
):
    back = (b0, b1, b2, b3)
    norm0, curvature0 = sums0[0:1, :], sums0[1:2, :]
    norm1, own, cross = sums1[0:1, :], sums1[1:2, :], sums1[2:3, :]
    alpha0 = norm0 / curvature0
    ratio = norm1 / norm0
    curvature1 = own + ratio * (2.0 * cross + ratio * curvature0)
    alpha1 = norm1 / curvature1

    def finish(r0, q, w):
        r1 = r0 - alpha0 * q
        direction = r1 + ratio * r0
        image = (q - alpha0 * w) + ratio * q
        return alpha0 * r0 + alpha1 * direction, r1 - alpha1 * image

    mult, res = finish(pg[...], q_glue[...], u[RIGHT:, :] - next_left[...])
    mult_glue[...] = mult
    res_glue[...] = res
    for k in range(SEG):
        seat = place[k]
        o, n = lax.div(seat, CAP), lax.rem(seat, CAP)
        here = slice(k * SD, (k + 1) * SD)
        fetched = jnp.zeros((SD, LC), f32)
        for w in range(W):
            fetched = jnp.where(o == w, back[w][rows(n * SD, SD), :], fetched)
        value = mask[here, :] * (u[G + k * SD : G + (k + 1) * SD, :] - fetched)
        mult, res = finish(pc[here, :], q_contact[here, :], value)
        mult_contact[here, :] = mult
        res_contact[here, :] = res


def shape(*dims, dtype=f32):
    return jax.ShapeDtypeStruct(dims, dtype)


def params(mib):
    return pltpu.CompilerParams(vmem_limit_bytes=mib * MIB)


def sent(value, body_step, sub_step):
    subs, bodies = lax.axis_size("sub"), lax.axis_size("body")
    pairs = [
        (s * bodies + b, ((s + sub_step) % subs) * bodies + (b + body_step) % bodies)
        for s in range(subs)
        for b in range(bodies)
    ]
    return lax.ppermute(value, ("sub", "body"), pairs)


def passed_along(value, steps):
    count = lax.axis_size("sub")
    first, last = (max(0, -steps), min(count, count - steps))
    return lax.ppermute(value, "sub", [(source, source + steps) for source in range(first, last)])


def rotated(value, block, stride, steps):
    count = lax.axis_size("sub")
    pairs = []
    for s in range(count):
        place = s // stride % block
        pairs.append((s, s + ((place + steps) % block - place) * stride))
    return lax.ppermute(value, "sub", pairs)


def total(value):
    value = value + sent(value, 1, 0) + sent(value, 2, 0) + sent(value, 3, 0)
    for stride in (8, 2):
        value = value + sum(rotated(value, 4, stride, k) for k in (1, 2, 3))
    return value + rotated(value, 2, 1, 1)


def per_device(compliance, mortar, rhs_glue, rhs_contact, owner_sub, master_slot, active_set):
    schur_block = compliance[0, 0]
    blocks = mortar.reshape(CR, SD)
    pg = rhs_glue[0, 0]
    rhs = rhs_contact.reshape(CR, LC)
    me = lax.axis_index("sub").astype(jnp.int32).reshape(1)
    seg_block = shape(INFO, LC)

    *outgoing, pc, mask, source, place = pl.pallas_call(
        pack_kernel,
        out_shape=[shape(INFO + 8, LC)] * 4
        + [shape(CR, LC)] * 2
        + [shape(SLOTS, dtype=jnp.int32), shape(SEG, dtype=jnp.int32)],
        in_specs=[SM, SM, SM, VM, VM],
        out_specs=[VM] * 6 + [SM] * 2,
        scratch_shapes=[pltpu.VMEM((SEG, 128), f32), pltpu.SMEM((W,), jnp.int32)],
        compiler_params=params(16),
        name="pack",
    )(me, owner_sub.reshape(SEG), master_slot.reshape(SEG), active_set.reshape(SEG, SD), rhs)

    incoming = [sent(outgoing[o], 1, o) for o in range(W)]
    left = passed_along(pg, 1)

    block_rows = 240
    steps = NS // block_rows
    high, low, partial = pl.pallas_call(
        split_kernel,
        grid=(steps,),
        out_shape=[shape(NS, KP, dtype=bf16)] * 2 + [shape(NS, LC)],
        in_specs=[
            pl.BlockSpec((block_rows, NS), lambda i: (i, 0)),
            pl.BlockSpec((G, LC), lambda i: (0, 0)),
            pl.BlockSpec((CR, LC), lambda i: (0, 0)),
            pl.BlockSpec((G, LC), lambda i: (0, 0)),
        ],
        out_specs=[
            pl.BlockSpec((block_rows, KP), lambda i: (i, 0)),
            pl.BlockSpec((block_rows, KP), lambda i: (i, 0)),
            pl.BlockSpec((block_rows, LC), lambda i: (i, 0)),
        ],
        scratch_shapes=[pltpu.VMEM((KP, 2 * LC), bf16)],
        compiler_params=params(32),
        cost_estimate=pl.CostEstimate(
            flops=8 * NS * KP * LC, bytes_accessed=4 * NS * NS + 4 * NS * KP, transcendentals=0
        ),
        name="split",
    )(schur_block, left, pc, pg)

    outs = pl.pallas_call(
        first_kernel,
        out_shape=[seg_block] * 8
        + [shape(NS, LC), shape(CR, LC), shape(CR, LC), shape(CR, LC), shape(SLOTS, dtype=jnp.int32)]
        + [shape(8, LC), shape(G, LC), shape(G, LC)],
        in_specs=[VM] * 10 + [SM, ANY, ANY],
        out_specs=[VM] * 12 + [SM] + [VM] * 3,
        scratch_shapes=[
            pltpu.VMEM((CR, LC), f32),
            pltpu.VMEM((K_WIDE, 2 * LC), bf16),
            pltpu.VMEM((NS, K_WIDE), bf16),
            pltpu.VMEM((NS, K_WIDE), bf16),
            pltpu.SMEM((W * 8, 128), f32),
            pltpu.SemaphoreType.DMA((2, TILES)),
            pltpu.SemaphoreType.DMA((W,)),
        ],
        compiler_params=params(40),
        name="first",
    )(*incoming, blocks, left, pc, pg, partial, mask, source, high, low)
    forward, reply = outs[:4], outs[4:8]
    u0, term0, projected0, actives, slots, sums0, left_face, right_face = outs[8:]

    forward = [sent(forward[o], 1, o) for o in range(W)]
    back = [sent(reply[o], -1, -o) for o in range(W)]
    next_left = passed_along(left_face, -1)
    prev_right = passed_along(right_face, 1)
    sums0 = total(sums0)

    outs = pl.pallas_call(
        second_kernel,
        out_shape=[seg_block] * 4
        + [shape(NS, LC), shape(G, LC), shape(CR, LC), shape(8, LC), shape(G, LC)],
        in_specs=[SM] * 3 + [VM] * 20 + [ANY, ANY],
        out_specs=[VM] * 9,
        scratch_shapes=[
            pltpu.VMEM((CR, LC), f32),
            pltpu.VMEM((NS, LC), f32),
            pltpu.VMEM((KP, 2 * LC), bf16),
            pltpu.VMEM((NS, KP), bf16),
            pltpu.VMEM((NS, KP), bf16),
            pltpu.VMEM((CR, LC), f32),
            pltpu.SemaphoreType.DMA((2, TILES)),
        ],
        compiler_params=params(56),
        name="second",
    )(me, slots, place, *forward, *back, next_left, prev_right, u0, projected0, actives, mask,
      blocks, left, pc, pg, term0, sums0, high, low)
    reply, (u1, q_glue, q_contact, sums1, left_face) = outs[:4], outs[4:]

    back = [sent(reply[o], -1, -o) for o in range(W)]
    next_left = passed_along(left_face, -1)
    sums1 = total(sums1)

    mult_glue, mult_contact, res_glue, res_contact = pl.pallas_call(
        last_kernel,
        out_shape=[shape(G, LC), shape(CR, LC)] * 2,
        in_specs=[SM] + [VM] * 13,
        out_specs=[VM] * 4,
        compiler_params=params(24),
        name="last",
    )(place, *back, next_left, u1, q_glue, q_contact, pc, pg, mask, sums0, sums1)
    contact = (1, 1, SEG, SD, LC)
    return (
        mult_glue[None, None],
        mult_contact.reshape(contact),
        res_glue[None, None],
        res_contact.reshape(contact),
    )


def solution(mesh):
    in_specs = (
        P("body", "sub", None, None),
        P("body", "sub", None, None, None),
        P("body", "sub", None, None),
        P("body", "sub", None, None, None),
        P("body", "sub", None, None),
        P("body", "sub", None),
        P("body", "sub", None, None),
    )
    out_specs = (
        P("body", "sub", None, None),
        P("body", "sub", None, None, None),
        P("body", "sub", None, None),
        P("body", "sub", None, None, None),
    )
    return jax.shard_map(
        per_device, mesh=mesh, in_specs=in_specs, out_specs=out_specs, check_vma=False
    )
```

time: 459 us -> 185 us (0.40)
  blocking collectives: 198 us -> 0 us
  waiting for transfers between devices: 141 us -> 43.7 us
  matrix products: 57.7 us -> 0 us
  Pallas kernels: 0 us -> 43.4 us
  starting transfers between devices: 42.7 us -> 78.5 us
  other arithmetic: 12.1 us -> 1.31 us
  local copies, waits for them, and re-layouts: 6.85 us -> 16.4 us
    psum x3 -> x0, blocking collectives: 198 us -> none  [the longest x2 130 us: squares(): lax.psum(column_sum(res_glue * res_glue, res_contact * res_contact), ('su...]
    ppermute x24 -> x40, waiting for transfers between devices: 141 us -> 43.7 us  [the longest x22 20 us: sent(): return lax.ppermute(value, ('sub', 'body'), pairs)]
    dot_general x14 -> x0, matrix products: 57.7 us -> none  [the longest x2 45.8 us: per_device(): displaced = jnp.dot(schur_block, loads, precision=highest)]
    pallas_call x0 -> x5, Pallas kernels: none -> 43.4 us  [the longest x1 17.2 us: per_device(): pl.pallas_call(split_kernel, grid=(steps,), out_shape=[shape(NS, KP, dtyp...]
    ppermute x24 -> x40, starting transfers between devices: 42.7 us -> 78.5 us  [the longest x22 47.4 us: sent(): return lax.ppermute(value, ('sub', 'body'), pairs)]
    unnamed x50 -> x70, local copies, waits for them, and re-layouts: 2.13 us -> 16.4 us
  transfers between devices with their start and end apart: 24 -> 40, of which waited for: 17 -> 13; matrix products, arithmetic and copies ran while one was open for 0% -> 0% of each run, Pallas kernels for 0% -> 10%
where the time goes in v1:
time: 185 us; the launch traced here: 184 us
  starting transfers between devices  78.5 us (42%)
  waiting for transfers between devices  43.7 us (24%)
  Pallas kernels  43.4 us (23%)
  local copies, waits for them, and re-layouts  16.4 us (9%)
    ppermute x22, starting transfers between devices, sent(): return lax.ppermute(value, ('sub', 'body'), pairs)  47.4 us
    ppermute x22, waiting for transfers between devices, sent(): return lax.ppermute(value, ('sub', 'body'), pairs)  20 us
    ppermute x14, starting transfers between devices, rotated(): return lax.ppermute(value, 'sub', pairs)  18.3 us
    pallas_call x1, Pallas kernels, per_device(): pl.pallas_call(split_kernel, grid=(steps,), out_shape=[shape(NS, KP, dtyp...  17.2 us
    unnamed x70, local copies, waits for them, and re-layouts  16.4 us
    ppermute x4, waiting for transfers between devices, passed_along(): lax.ppermute(value, 'sub', [(source, source + steps) for source in range(...  16.1 us
    pallas_call x1, Pallas kernels, per_device(): pl.pallas_call(second_kernel, out_shape=[seg_block] * 4 + [shape(NS, LC),...  15.4 us
    ppermute x4, starting transfers between devices, passed_along(): lax.ppermute(value, 'sub', [(source, source + steps) for source in range(...  12.7 us
  transfers between devices with their start and end apart: 40, of which 13 were waited for; matrix products, arithmetic and copies ran while one was open for 0% of the time, Pallas kernels for 10%

profile of v1, /device:TPU:1, one launch (start us, length us, event | category | flops | bytes accessed | tf_op | source)
XLA Modules:
  0.0 184.3 jit_solution(4617070315626943890)
XLA Ops:
  0.6 4.9 %collective-permute-start.4 = (f32[176,128]{1,0:T(8,128)}, f32[176,128]{1,0:T(8,128)S(1)}, u32[]{:S(2)}, u32[]{:S(2)}) collective-permute-start(f32[176,128]{1,0:T(8,128)} %bitcast.14), channel_id=1, source_target_pairs={{0,4},{4,8},{8,12},{12,16},{16,20},{20,24},{24,28},{28,32},{32,36}... | collective-permute-start | bytes 270344 | tf_op jit(solution)/shard_map/ppermute | solution.py:301
  5.6 1.0 copy-done.16
  8.6 1.4 pack.1
  10.6 1.3 collective-permute-start
  11.9 1.3 collective-permute-start.1
  13.2 2.4 %collective-permute-start.2 = (f32[520,128]{1,0:T(8,128)S(1)}, f32[520,128]{1,0:T(8,128)S(1)}, u32[]{:S(2)}, u32[]{:S(2)}) collective-permute-start(f32[520,128]{1,0:T(8,128)S(1)} %get-tuple-element.47), channel_id=1, source_target_pairs={{0,9},{1,10},{2,11},{3,8},{4,13},{5,14},{6,15},{7,12},{8,17},{9,18... | collective-permute-start | bytes 798728 | tf_op jit(solution)/shard_map/ppermute | solution.py:295
  15.6 2.0 %collective-permute-start.3 = (f32[520,128]{1,0:T(8,128)S(1)}, f32[520,128]{1,0:T(8,128)S(1)}, u32[]{:S(2)}, u32[]{:S(2)}) collective-permute-start(f32[520,128]{1,0:T(8,128)S(1)} %get-tuple-element.48), channel_id=1, source_target_pairs={{0,13},{1,14},{2,15},{3,12},{4,17},{5,18},{6,19},{7,16},{8,21},{9,... | collective-permute-start | bytes 798728 | tf_op jit(solution)/shard_map/ppermute | solution.py:295
  17.6 0.9 copy-done.6
  18.5 17.2 %split.1 = (bf16[2400,2560]{1,0:T(8,128)(2,1)S(1)}, bf16[2400,2560]{1,0:T(8,128)(2,1)}, f32[2400,128]{1,0:T(8,128)S(1)}) custom-call(f32[2400,2400]{1,0:T(8,128)} %bitcast.23, f32[176,128]{1,0:T(8,128)S(1)} %collective-permute-done.4.left.left0, f32[1024,128]{1,0:T(8,128)S(1)} %get-tuple-element.49.pc, f32[176,128]{1,0:T(8,128)S(1)} %bitcast.16), custom_call_target="tpu_custom_call" | custom-call | flops 6291456000 | bytes 47616000 | tf_op jit(solution)/shard_map/split/pallas_call | solution.py:345
  35.6 4.4 %copy-done = bf16[2400,2560]{1,0:T(8,128)(2,1)} copy-done((bf16[2400,2560]{1,0:T(8,128)(2,1)}, bf16[2400,2560]{1,0:T(8,128)(2,1)S(1)}, u32[]{:S(2)}) %copy-start) | copy-done | bytes 12288024
  40.1 7.4 %first.1 = (f32[512,128]{1,0:T(8,128)S(1)}, f32[512,128]{1,0:T(8,128)S(1)}, f32[512,128]{1,0:T(8,128)S(1)}, f32[512,128]{1,0:T(8,128)S(1)}, f32[512,128]{1,0:T(8...) custom-call(f32[520,128]{1,0:T(8,128)S(1)} %collective-permute-done., ...), custom_call_target="tpu_custom_call" | custom-call | tf_op jit(solution)/shard_map/first/pallas_call | solution.py:368
  47.6 1.0 copy-done.9
  48.7 0.8 copy-done.12
  51.1 2.5 %collective-permute-start.17 = (f32[8,128]{1,0:T(8,128)S(1)}, f32[8,128]{1,0:T(8,128)S(1)}, u32[]{:S(2)}, u32[]{:S(2)}) collective-permute-start(f32[8,128]{1,0:T(8,128)S(1)} %get-tuple-element.70), channel_id=1, source_target_pairs={{0,3},{1,0},{2,1},{3,2},{4,7},{5,4},{6,5},{7,6},{8,11},{9,8},{10,9... | collective-permute-start | bytes 12296 | tf_op jit(solution)/shard_map/ppermute | solution.py:295
  54.6 2.9 %collective-permute-done.16 = f32[8,128]{1,0:T(8,128)S(1)} collective-permute-done((f32[8,128]{1,0:T(8,128)S(1)}, f32[8,128]{1,0:T(8,128)S(1)}, u32[]{:S(2)}, u32[]{:S(2)}) %collective-permute-start.16) | collective-permute-done | bytes 4128 | tf_op jit(solution)/shard_map/ppermute | solution.py:295
  57.9 1.4 collective-permute-start.20
  59.3 1.6 collective-permute-start.19
  60.9 2.3 %collective-permute-done.19 = f32[8,128]{1,0:T(8,128)S(1)} collective-permute-done((f32[8,128]{1,0:T(8,128)S(1)}, f32[8,128]{1,0:T(8,128)S(1)}, u32[]{:S(2)}, u32[]{:S(2)}) %collective-permute-start.19) | collective-permute-done | bytes 4128 | tf_op jit(solution)/shard_map/ppermute | solution.py:310
  63.2 1.3 collective-permute-done.18
  64.6 3.1 %collective-permute-start.23 = (f32[8,128]{1,0:T(8,128)S(1)}, f32[8,128]{1,0:T(8,128)S(1)}, u32[]{:S(2)}, u32[]{:S(2)}) collective-permute-start(f32[8,128]{1,0:T(8,128)S(1)} %add_add_fusion.4), channel_id=1, source_target_pairs={{0,24},{4,28},{8,0},{12,4},{16,8},{20,12},{24,16},{28,20},{32,56},... | collective-permute-start | bytes 12296 | tf_op jit(solution)/shard_map/ppermute | solution.py:310
  68.4 5.7 %collective-permute-start.6 = (f32[512,128]{1,0:T(8,128)S(1)}, f32[512,128]{1,0:T(8,128)S(1)}, u32[]{:S(2)}, u32[]{:S(2)}) collective-permute-start(f32[512,128]{1,0:T(8,128)S(1)} %get-tuple-element.57), channel_id=1, source_target_pairs={{0,5},{1,6},{2,7},{3,4},{4,9},{5,10},{6,11},{7,8},{8,13},{9,14},{1... | collective-permute-start | bytes 786440 | tf_op jit(solution)/shard_map/ppermute | solution.py:295
  74.1 1.0 collective-permute-start.24
  75.1 1.9 %collective-permute-start.13 = (f32[176,128]{1,0:T(8,128)S(1)}, f32[176,128]{1,0:T(8,128)S(1)}, u32[]{:S(2)}, u32[]{:S(2)}) collective-permute-start(f32[176,128]{1,0:T(8,128)S(1)} %get-tuple-element.64), channel_id=1, source_target_pairs={{4,0},{8,4},{12,8},{16,12},{20,16},{24,20},{28,24},{32,28},{36,32}... | collective-permute-start | bytes 270344 | tf_op jit(solution)/shard_map/ppermute | solution.py:301
  77.0 3.6 %collective-permute-start.14 = (f32[176,128]{1,0:T(8,128)S(1)}, f32[176,128]{1,0:T(8,128)S(1)}, u32[]{:S(2)}, u32[]{:S(2)}) collective-permute-start(f32[176,128]{1,0:T(8,128)S(1)} %get-tuple-element.65), channel_id=1, source_target_pairs={{0,4},{4,8},{8,12},{12,16},{16,20},{20,24},{24,28},{28,32},{32,36}... | collective-permute-start | bytes 270344 | tf_op jit(solution)/shard_map/ppermute | solution.py:301
  81.2 1.6 collective-permute-start.8
  83.0 10.9 %collective-permute-start.9 = (f32[512,128]{1,0:T(8,128)S(1)}, f32[512,128]{1,0:T(8,128)S(1)}, u32[]{:S(2)}, u32[]{:S(2)}) collective-permute-start(f32[512,128]{1,0:T(8,128)S(1)} %get-tuple-element.60), channel_id=1, source_target_pairs={{0,3},{1,0},{2,1},{3,2},{4,7},{5,4},{6,5},{7,6},{8,11},{9,8},{10,9... | collective-permute-start | bytes 786440 | tf_op jit(solution)/shard_map/ppermute | solution.py:295
  93.9 1.9 %collective-permute-start.11 = (f32[512,128]{1,0:T(8,128)S(1)}, f32[512,128]{1,0:T(8,128)S(1)}, u32[]{:S(2)}, u32[]{:S(2)}) collective-permute-start(f32[512,128]{1,0:T(8,128)S(1)} %get-tuple-element.62), channel_id=1, source_target_pairs={{0,123},{1,120},{2,121},{3,122},{4,127},{5,124},{6,125},{7,126},{8... | collective-permute-start | bytes 786440 | tf_op jit(solution)/shard_map/ppermute | solution.py:295
  95.8 4.4 %collective-permute-start.12 = (f32[512,128]{1,0:T(8,128)S(1)}, f32[512,128]{1,0:T(8,128)S(1)}, u32[]{:S(2)}, u32[]{:S(2)}) collective-permute-start(f32[512,128]{1,0:T(8,128)S(1)} %get-tuple-element.63), channel_id=1, source_target_pairs={{0,119},{1,116},{2,117},{3,118},{4,123},{5,120},{6,121},{7,122},{8... | collective-permute-start | bytes 786440 | tf_op jit(solution)/shard_map/ppermute | solution.py:295
  100.8 9.1 %collective-permute-done.10.b1 = f32[512,128]{1,0:T(8,128)S(1)} collective-permute-done((f32[512,128]{1,0:T(8,128)S(1)}, f32[512,128]{1,0:T(8,128)S(1)}, u32[]{:S(2)}, u32[]{:S(2)}) %collective-permute-start.10) | collective-permute-done | bytes 262176 | tf_op jit(solution)/shard_map/ppermute | solution.py:295
  109.9 4.0 %collective-permute-done.11.b2 = f32[512,128]{1,0:T(8,128)S(1)} collective-permute-done((f32[512,128]{1,0:T(8,128)S(1)}, f32[512,128]{1,0:T(8,128)S(1)}, u32[]{:S(2)}, u32[]{:S(2)}) %collective-permute-start.11) | collective-permute-done | bytes 262176 | tf_op jit(solution)/shard_map/ppermute | solution.py:295
  114.8 15.4 %second.1 = (f32[512,128]{1,0:T(8,128)}, f32[512,128]{1,0:T(8,128)}, f32[512,128]{1,0:T(8,128)}, f32[512,128]{1,0:T(8,128)}, f32[2400,128]{1,0:T(8,128)}, /*inde...) custom-call(s32[1]{0:T(128)} %bitcast.me, s32[32]{0:T(128)} %copy-done.24, ...), custom_call_target="tpu_custom_call" | custom-call | tf_op jit(solution)/shard_map/second/pallas_call | solution.py:396
  130.2 3.2 %collective-permute-start.32 = (f32[8,128]{1,0:T(8,128)}, f32[8,128]{1,0:T(8,128)S(1)}, u32[]{:S(2)}, u32[]{:S(2)}) collective-permute-start(f32[8,128]{1,0:T(8,128)} %get-tuple-element.79), channel_id=1, source_target_pairs={{0,3},{1,0},{2,1},{3,2},{4,7},{5,4},{6,5},{7,6},{8,11},{9,8},{10,9... | collective-permute-start | bytes 12296 | tf_op jit(solution)/shard_map/ppermute | solution.py:295
  134.4 3.2 %collective-permute-done.31 = f32[8,128]{1,0:T(8,128)S(1)} collective-permute-done((f32[8,128]{1,0:T(8,128)}, f32[8,128]{1,0:T(8,128)S(1)}, u32[]{:S(2)}, u32[]{:S(2)}) %collective-permute-start.31) | collective-permute-done | bytes 4128 | tf_op jit(solution)/shard_map/ppermute | solution.py:295
  138.3 6.9 %collective-permute-start.35 = (f32[8,128]{1,0:T(8,128)S(1)}, f32[8,128]{1,0:T(8,128)S(1)}, u32[]{:S(2)}, u32[]{:S(2)}) collective-permute-start(f32[8,128]{1,0:T(8,128)S(1)} %add_add_fusion.2), channel_id=1, source_target_pairs={{0,96},{4,100},{8,104},{12,108},{16,112},{20,116},{24,120},{28,124... | collective-permute-start | bytes 12296 | tf_op jit(solution)/shard_map/ppermute | solution.py:310
  145.2 0.9 collective-permute-start.33
  146.1 3.0 %collective-permute-done.34 = f32[8,128]{1,0:T(8,128)S(1)} collective-permute-done((f32[8,128]{1,0:T(8,128)S(1)}, f32[8,128]{1,0:T(8,128)S(1)}, u32[]{:S(2)}, u32[]{:S(2)}) %collective-permute-start.34) | collective-permute-done | bytes 4128 | tf_op jit(solution)/shard_map/ppermute | solution.py:310
  149.3 1.4 collective-permute-start.36
  150.6 4.2 %collective-permute-start.26 = (f32[512,128]{1,0:T(8,128)}, f32[512,128]{1,0:T(8,128)S(1)}, u32[]{:S(2)}, u32[]{:S(2)}) collective-permute-start(f32[512,128]{1,0:T(8,128)} %get-tuple-element.72), channel_id=1, source_target_pairs={{0,127},{1,124},{2,125},{3,126},{4,3},{5,0},{6,1},{7,2},{8,7},{9,4... | collective-permute-start | bytes 786440 | tf_op jit(solution)/shard_map/ppermute | solution.py:295
  154.9 2.8 %collective-permute-start.27 = (f32[512,128]{1,0:T(8,128)}, f32[512,128]{1,0:T(8,128)S(1)}, u32[]{:S(2)}, u32[]{:S(2)}) collective-permute-start(f32[512,128]{1,0:T(8,128)} %get-tuple-element.73), channel_id=1, source_target_pairs={{0,123},{1,120},{2,121},{3,122},{4,127},{5,124},{6,125},{7,126},{8... | collective-permute-start | bytes 786440 | tf_op jit(solution)/shard_map/ppermute | solution.py:295
  157.7 1.6 collective-permute-start.28
  159.3 1.2 collective-permute-start.39
  160.5 0.8 collective-permute-done.39
  161.3 2.2 %collective-permute-start.29 = (f32[176,128]{1,0:T(8,128)}, f32[176,128]{1,0:T(8,128)S(1)}, u32[]{:S(2)}, u32[]{:S(2)}) collective-permute-start(f32[176,128]{1,0:T(8,128)} %get-tuple-element.75), channel_id=1, source_target_pairs={{4,0},{8,4},{12,8},{16,12},{20,16},{24,20},{28,24},{32,28},{36,32}... | collective-permute-start | bytes 270344 | tf_op jit(solution)/shard_map/ppermute | solution.py:301
  163.6 15.4 %collective-permute-done.29.next_left = f32[176,128]{1,0:T(8,128)S(1)} collective-permute-done((f32[176,128]{1,0:T(8,128)}, f32[176,128]{1,0:T(8,128)S(1)}, u32[]{:S(2)}, u32[]{:S(2)}) %collective-permute-start.29) | collective-permute-done | bytes 90144 | tf_op jit(solution)/shard_map/ppermute | solution.py:301
  179.1 1.3 copy-done.10
  180.4 1.0 copy-done.15
  181.4 0.9 copy-done.17
  182.3 2.0 %last.1 = (f32[176,128]{1,0:T(8,128)}, f32[1024,128]{1,0:T(8,128)}, f32[176,128]{1,0:T(8,128)}, f32[1024,128]{1,0:T(8,128)}) custom-call(s32[16]{0:T(128)S(1)} %copy-done.21, f32[512,128]{1,0:T(8,128)S(1)} %collective-permute-done.25.b0, f32[512,128]{1,0:T(8,128)S(1)} %collective-permute-done.26.b1, f32[512,128]{1,0:T(8,128)S(1)} %collective-permute-done.27.b2, ...), custom_call_target="tpu_custom_call" | custom-call | tf_op jit(solution)/shard_map/last/pallas_call | solution.py:421
  (115 shorter events, 10.3 us)
Async XLA Ops:
  0.6 16.9 %collective-permute-start.4 = (f32[176,128]{1,0:T(8,128)}, f32[176,128]{1,0:T(8,128)S(1)}, u32[]{:S(2)}, u32[]{:S(2)}) collective-permute-start(f32[176,128]{1,0:T(8,128)} %bitcast.14), channel_id=1, source_target_pairs={{0,4},{4,8},{8,12},{12,16},{16,20},{20,24},{24,28},{28,32},{32,36}... | collective-permute-start | bytes 270344 | tf_op jit(solution)/shard_map/ppermute | solution.py:301
  10.6 37.0 %copy-start.1 = (f32[1024,128]{1,0:T(8,128)}, f32[1024,128]{1,0:T(8,128)S(1)}, u32[]{:S(2)}) copy-start(f32[1024,128]{1,0:T(8,128)S(1)} %get-tuple-element.49.pc) | copy-start | bytes 1572868
  10.6 37.0 %copy-start.3 = (f32[1024,128]{1,0:T(8,128)}, f32[1024,128]{1,0:T(8,128)S(1)}, u32[]{:S(2)}) copy-start(f32[1024,128]{1,0:T(8,128)S(1)} %get-tuple-element.51.mask) | copy-start | bytes 1572868
  10.6 29.5 %collective-permute-start = (f32[520,128]{1,0:T(8,128)S(1)}, f32[520,128]{1,0:T(8,128)S(1)}, u32[]{:S(2)}, u32[]{:S(2)}) collective-permute-start(f32[520,128]{1,0:T(8,128)S(1)} %get-tuple-element.45), channel_id=1, source_target_pairs={{0,1},{1,2},{2,3},{3,0},{4,5},{5,6},{6,7},{7,4},{8,9},{9,10},{10,1... | collective-permute-start | bytes 798728 | tf_op jit(solution)/shard_map/ppermute | solution.py:295
  11.9 28.2 %collective-permute-start.1 = (f32[520,128]{1,0:T(8,128)S(1)}, f32[520,128]{1,0:T(8,128)S(1)}, u32[]{:S(2)}, u32[]{:S(2)}) collective-permute-start(f32[520,128]{1,0:T(8,128)S(1)} %get-tuple-element.46), channel_id=1, source_target_pairs={{0,5},{1,6},{2,7},{3,4},{4,9},{5,10},{6,11},{7,8},{8,13},{9,14},{1... | collective-permute-start | bytes 798728 | tf_op jit(solution)/shard_map/ppermute | solution.py:295
  13.2 26.9 %collective-permute-start.2 = (f32[520,128]{1,0:T(8,128)S(1)}, f32[520,128]{1,0:T(8,128)S(1)}, u32[]{:S(2)}, u32[]{:S(2)}) collective-permute-start(f32[520,128]{1,0:T(8,128)S(1)} %get-tuple-element.47), channel_id=1, source_target_pairs={{0,9},{1,10},{2,11},{3,8},{4,13},{5,14},{6,15},{7,12},{8,17},{9,18... | collective-permute-start | bytes 798728 | tf_op jit(solution)/shard_map/ppermute | solution.py:295
  15.6 24.5 %collective-permute-start.3 = (f32[520,128]{1,0:T(8,128)S(1)}, f32[520,128]{1,0:T(8,128)S(1)}, u32[]{:S(2)}, u32[]{:S(2)}) collective-permute-start(f32[520,128]{1,0:T(8,128)S(1)} %get-tuple-element.48), channel_id=1, source_target_pairs={{0,13},{1,14},{2,15},{3,12},{4,17},{5,18},{6,19},{7,16},{8,21},{9,... | collective-permute-start | bytes 798728 | tf_op jit(solution)/shard_map/ppermute | solution.py:295
  51.1 62.9 %copy-start.24 = (s32[32]{0:T(128)}, s32[32]{0:T(128)S(1)}, u32[]{:S(2)}) copy-start(s32[32]{0:T(128)S(1)} %get-tuple-element.55.slots) | copy-start | bytes 388
  51.1 3.5 %collective-permute-start.17 = (f32[8,128]{1,0:T(8,128)S(1)}, f32[8,128]{1,0:T(8,128)S(1)}, u32[]{:S(2)}, u32[]{:S(2)}) collective-permute-start(f32[8,128]{1,0:T(8,128)S(1)} %get-tuple-element.70), channel_id=1, source_target_pairs={{0,3},{1,0},{2,1},{3,2},{4,7},{5,4},{6,5},{7,6},{8,11},{9,8},{10,9... | collective-permute-start | bytes 12296 | tf_op jit(solution)/shard_map/ppermute | solution.py:295
  53.5 4.0 %collective-permute-start.16 = (f32[8,128]{1,0:T(8,128)S(1)}, f32[8,128]{1,0:T(8,128)S(1)}, u32[]{:S(2)}, u32[]{:S(2)}) collective-permute-start(f32[8,128]{1,0:T(8,128)S(1)} %get-tuple-element.70), channel_id=1, source_target_pairs={{0,2},{1,3},{2,0},{3,1},{4,6},{5,7},{6,4},{7,5},{8,10},{9,11},{10,... | collective-permute-start | bytes 12296 | tf_op jit(solution)/shard_map/ppermute | solution.py:295
  53.9 4.0 %collective-permute-start.15 = (f32[8,128]{1,0:T(8,128)S(1)}, f32[8,128]{1,0:T(8,128)S(1)}, u32[]{:S(2)}, u32[]{:S(2)}) collective-permute-start(f32[8,128]{1,0:T(8,128)S(1)} %get-tuple-element.70), channel_id=1, source_target_pairs={{0,1},{1,2},{2,3},{3,0},{4,5},{5,6},{6,7},{7,4},{8,9},{9,10},{10,1... | collective-permute-start | bytes 12296 | tf_op jit(solution)/shard_map/ppermute | solution.py:295
  57.9 3.0 %collective-permute-start.20 = (f32[8,128]{1,0:T(8,128)S(1)}, f32[8,128]{1,0:T(8,128)S(1)}, u32[]{:S(2)}, u32[]{:S(2)}) collective-permute-start(f32[8,128]{1,0:T(8,128)S(1)} %add_add_fusion.5), channel_id=1, source_target_pairs={{0,96},{4,100},{8,104},{12,108},{16,112},{20,116},{24,120},{28,124... | collective-permute-start | bytes 12296 | tf_op jit(solution)/shard_map/ppermute | solution.py:310
  59.3 4.0 %collective-permute-start.19 = (f32[8,128]{1,0:T(8,128)S(1)}, f32[8,128]{1,0:T(8,128)S(1)}, u32[]{:S(2)}, u32[]{:S(2)}) collective-permute-start(f32[8,128]{1,0:T(8,128)S(1)} %add_add_fusion.5), channel_id=1, source_target_pairs={{0,64},{4,68},{8,72},{12,76},{16,80},{20,84},{24,88},{28,92},{32,9... | collective-permute-start | bytes 12296 | tf_op jit(solution)/shard_map/ppermute | solution.py:310
  60.9 3.7 %collective-permute-start.18 = (f32[8,128]{1,0:T(8,128)S(1)}, f32[8,128]{1,0:T(8,128)S(1)}, u32[]{:S(2)}, u32[]{:S(2)}) collective-permute-start(f32[8,128]{1,0:T(8,128)S(1)} %add_add_fusion.5), channel_id=1, source_target_pairs={{0,32},{4,36},{8,40},{12,44},{16,48},{20,52},{24,56},{28,60},{32,6... | collective-permute-start | bytes 12296 | tf_op jit(solution)/shard_map/ppermute | solution.py:310
  64.6 9.5 %collective-permute-start.23 = (f32[8,128]{1,0:T(8,128)S(1)}, f32[8,128]{1,0:T(8,128)S(1)}, u32[]{:S(2)}, u32[]{:S(2)}) collective-permute-start(f32[8,128]{1,0:T(8,128)S(1)} %add_add_fusion.4), channel_id=1, source_target_pairs={{0,24},{4,28},{8,0},{12,4},{16,8},{20,12},{24,16},{28,20},{32,56},... | collective-permute-start | bytes 12296 | tf_op jit(solution)/shard_map/ppermute | solution.py:310
  67.7 6.4 %collective-permute-start.22 = (f32[8,128]{1,0:T(8,128)S(1)}, f32[8,128]{1,0:T(8,128)S(1)}, u32[]{:S(2)}, u32[]{:S(2)}) collective-permute-start(f32[8,128]{1,0:T(8,128)S(1)} %add_add_fusion.4), channel_id=1, source_target_pairs={{0,16},{4,20},{8,24},{12,28},{16,0},{20,4},{24,8},{28,12},{32,48},... | collective-permute-start | bytes 12296 | tf_op jit(solution)/shard_map/ppermute | solution.py:310
  67.7 6.4 %collective-permute-start.21 = (f32[8,128]{1,0:T(8,128)S(1)}, f32[8,128]{1,0:T(8,128)S(1)}, u32[]{:S(2)}, u32[]{:S(2)}) collective-permute-start(f32[8,128]{1,0:T(8,128)S(1)} %add_add_fusion.4), channel_id=1, source_target_pairs={{0,8},{4,12},{8,16},{12,20},{16,24},{20,28},{24,0},{28,4},{32,40},... | collective-permute-start | bytes 12296 | tf_op jit(solution)/shard_map/ppermute | solution.py:310
  68.4 25.5 %collective-permute-start.5 = (f32[512,128]{1,0:T(8,128)S(1)}, f32[512,128]{1,0:T(8,128)S(1)}, u32[]{:S(2)}, u32[]{:S(2)}) collective-permute-start(f32[512,128]{1,0:T(8,128)S(1)} %get-tuple-element.56), channel_id=1, source_target_pairs={{0,1},{1,2},{2,3},{3,0},{4,5},{5,6},{6,7},{7,4},{8,9},{9,10},{10,1... | collective-permute-start | bytes 786440 | tf_op jit(solution)/shard_map/ppermute | solution.py:295
  68.4 25.5 %collective-permute-start.6 = (f32[512,128]{1,0:T(8,128)S(1)}, f32[512,128]{1,0:T(8,128)S(1)}, u32[]{:S(2)}, u32[]{:S(2)}) collective-permute-start(f32[512,128]{1,0:T(8,128)S(1)} %get-tuple-element.57), channel_id=1, source_target_pairs={{0,5},{1,6},{2,7},{3,4},{4,9},{5,10},{6,11},{7,8},{8,13},{9,14},{1... | collective-permute-start | bytes 786440 | tf_op jit(solution)/shard_map/ppermute | solution.py:295
  74.1 21.7 %collective-permute-start.7 = (f32[512,128]{1,0:T(8,128)S(1)}, f32[512,128]{1,0:T(8,128)S(1)}, u32[]{:S(2)}, u32[]{:S(2)}) collective-permute-start(f32[512,128]{1,0:T(8,128)S(1)} %get-tuple-element.58), channel_id=1, source_target_pairs={{0,9},{1,10},{2,11},{3,8},{4,13},{5,14},{6,15},{7,12},{8,17},{9,18... | collective-permute-start | bytes 786440 | tf_op jit(solution)/shard_map/ppermute | solution.py:295
  74.1 2.9 %collective-permute-start.24 = (f32[8,128]{1,0:T(8,128)S(1)}, f32[8,128]{1,0:T(8,128)S(1)}, u32[]{:S(2)}, u32[]{:S(2)}) collective-permute-start(f32[8,128]{1,0:T(8,128)S(1)} %add_add_fusion.3), channel_id=1, source_target_pairs={{0,4},{4,0},{8,12},{12,8},{16,20},{20,16},{24,28},{28,24},{32,36},... | collective-permute-start | bytes 12296 | tf_op jit(solution)/shard_map/ppermute | solution.py:310
  75.1 6.1 %collective-permute-start.13 = (f32[176,128]{1,0:T(8,128)S(1)}, f32[176,128]{1,0:T(8,128)S(1)}, u32[]{:S(2)}, u32[]{:S(2)}) collective-permute-start(f32[176,128]{1,0:T(8,128)S(1)} %get-tuple-element.64), channel_id=1, source_target_pairs={{4,0},{8,4},{12,8},{16,12},{20,16},{24,20},{28,24},{32,28},{36,32}... | collective-permute-start | bytes 270344 | tf_op jit(solution)/shard_map/ppermute | solution.py:301
  77.0 5.9 %collective-permute-start.14 = (f32[176,128]{1,0:T(8,128)S(1)}, f32[176,128]{1,0:T(8,128)S(1)}, u32[]{:S(2)}, u32[]{:S(2)}) collective-permute-start(f32[176,128]{1,0:T(8,128)S(1)} %get-tuple-element.65), channel_id=1, source_target_pairs={{0,4},{4,8},{8,12},{12,16},{16,20},{20,24},{24,28},{28,32},{32,36}... | collective-permute-start | bytes 270344 | tf_op jit(solution)/shard_map/ppermute | solution.py:301
  81.2 19.5 %collective-permute-start.8 = (f32[512,128]{1,0:T(8,128)S(1)}, f32[512,128]{1,0:T(8,128)S(1)}, u32[]{:S(2)}, u32[]{:S(2)}) collective-permute-start(f32[512,128]{1,0:T(8,128)S(1)} %get-tuple-element.59), channel_id=1, source_target_pairs={{0,13},{1,14},{2,15},{3,12},{4,17},{5,18},{6,19},{7,16},{8,21},{9,... | collective-permute-start | bytes 786440 | tf_op jit(solution)/shard_map/ppermute | solution.py:295
  83.0 17.8 %collective-permute-start.9 = (f32[512,128]{1,0:T(8,128)S(1)}, f32[512,128]{1,0:T(8,128)S(1)}, u32[]{:S(2)}, u32[]{:S(2)}) collective-permute-start(f32[512,128]{1,0:T(8,128)S(1)} %get-tuple-element.60), channel_id=1, source_target_pairs={{0,3},{1,0},{2,1},{3,2},{4,7},{5,4},{6,5},{7,6},{8,11},{9,8},{10,9... | collective-permute-start | bytes 786440 | tf_op jit(solution)/shard_map/ppermute | solution.py:295
  93.8 16.1 %collective-permute-start.10 = (f32[512,128]{1,0:T(8,128)S(1)}, f32[512,128]{1,0:T(8,128)S(1)}, u32[]{:S(2)}, u32[]{:S(2)}) collective-permute-start(f32[512,128]{1,0:T(8,128)S(1)} %get-tuple-element.61), channel_id=1, source_target_pairs={{0,127},{1,124},{2,125},{3,126},{4,3},{5,0},{6,1},{7,2},{8,7},{9,4... | collective-permute-start | bytes 786440 | tf_op jit(solution)/shard_map/ppermute | solution.py:295
  93.9 20.1 %collective-permute-start.11 = (f32[512,128]{1,0:T(8,128)S(1)}, f32[512,128]{1,0:T(8,128)S(1)}, u32[]{:S(2)}, u32[]{:S(2)}) collective-permute-start(f32[512,128]{1,0:T(8,128)S(1)} %get-tuple-element.62), channel_id=1, source_target_pairs={{0,123},{1,120},{2,121},{3,122},{4,127},{5,124},{6,125},{7,126},{8... | collective-permute-start | bytes 786440 | tf_op jit(solution)/shard_map/ppermute | solution.py:295
  95.8 18.1 %collective-permute-start.12 = (f32[512,128]{1,0:T(8,128)S(1)}, f32[512,128]{1,0:T(8,128)S(1)}, u32[]{:S(2)}, u32[]{:S(2)}) collective-permute-start(f32[512,128]{1,0:T(8,128)S(1)} %get-tuple-element.63), channel_id=1, source_target_pairs={{0,119},{1,116},{2,117},{3,118},{4,123},{5,120},{6,121},{7,122},{8... | collective-permute-start | bytes 786440 | tf_op jit(solution)/shard_map/ppermute | solution.py:295
  114.7 64.3 %copy-start.2 = (f32[1024,128]{1,0:T(8,128)S(1)}, f32[1024,128]{1,0:T(8,128)}, u32[]{:S(2)}) copy-start(f32[1024,128]{1,0:T(8,128)} %copy-done.1) | copy-start | bytes 1572868
  114.7 64.3 %copy-start.4 = (f32[1024,128]{1,0:T(8,128)S(1)}, f32[1024,128]{1,0:T(8,128)}, u32[]{:S(2)}) copy-start(f32[1024,128]{1,0:T(8,128)} %copy-done.3) | copy-start | bytes 1572868
  114.7 64.3 %copy-start.8 = (f32[1,1,176,128]{3,2,1,0:T(8,128)S(1)}, f32[1,1,176,128]{3,2,1,0:T(8,128)}, u32[]{:S(2)}) copy-start(f32[1,1,176,128]{3,2,1,0:T(8,128)} %param.9) | copy-start | bytes 270340
  114.7 64.3 %copy-start.18 = (f32[8,128]{1,0:T(8,128)S(1)}, f32[8,128]{1,0:T(8,128)}, u32[]{:S(2)}) copy-start(f32[8,128]{1,0:T(8,128)} %add.69.sums0) | copy-start | bytes 12292
  114.7 64.3 %copy-start.21 = (s32[16]{0:T(128)S(1)}, s32[16]{0:T(128)}, u32[]{:S(2)}) copy-start(s32[16]{0:T(128)} %copy-done.20) | copy-start | bytes 196
  130.2 4.2 %collective-permute-start.32 = (f32[8,128]{1,0:T(8,128)}, f32[8,128]{1,0:T(8,128)S(1)}, u32[]{:S(2)}, u32[]{:S(2)}) collective-permute-start(f32[8,128]{1,0:T(8,128)} %get-tuple-element.79), channel_id=1, source_target_pairs={{0,3},{1,0},{2,1},{3,2},{4,7},{5,4},{6,5},{7,6},{8,11},{9,8},{10,9... | collective-permute-start | bytes 12296 | tf_op jit(solution)/shard_map/ppermute | solution.py:295
  133.4 4.2 %collective-permute-start.31 = (f32[8,128]{1,0:T(8,128)}, f32[8,128]{1,0:T(8,128)S(1)}, u32[]{:S(2)}, u32[]{:S(2)}) collective-permute-start(f32[8,128]{1,0:T(8,128)} %get-tuple-element.79), channel_id=1, source_target_pairs={{0,2},{1,3},{2,0},{3,1},{4,6},{5,7},{6,4},{7,5},{8,10},{9,11},{10,... | collective-permute-start | bytes 12296 | tf_op jit(solution)/shard_map/ppermute | solution.py:295
  133.4 4.2 %collective-permute-start.30 = (f32[8,128]{1,0:T(8,128)}, f32[8,128]{1,0:T(8,128)S(1)}, u32[]{:S(2)}, u32[]{:S(2)}) collective-permute-start(f32[8,128]{1,0:T(8,128)} %get-tuple-element.79), channel_id=1, source_target_pairs={{0,1},{1,2},{2,3},{3,0},{4,5},{5,6},{6,7},{7,4},{8,9},{9,10},{10,1... | collective-permute-start | bytes 12296 | tf_op jit(solution)/shard_map/ppermute | solution.py:295
  138.3 7.8 %collective-permute-start.35 = (f32[8,128]{1,0:T(8,128)S(1)}, f32[8,128]{1,0:T(8,128)S(1)}, u32[]{:S(2)}, u32[]{:S(2)}) collective-permute-start(f32[8,128]{1,0:T(8,128)S(1)} %add_add_fusion.2), channel_id=1, source_target_pairs={{0,96},{4,100},{8,104},{12,108},{16,112},{20,116},{24,120},{28,124... | collective-permute-start | bytes 12296 | tf_op jit(solution)/shard_map/ppermute | solution.py:310
  145.1 4.0 %collective-permute-start.34 = (f32[8,128]{1,0:T(8,128)S(1)}, f32[8,128]{1,0:T(8,128)S(1)}, u32[]{:S(2)}, u32[]{:S(2)}) collective-permute-start(f32[8,128]{1,0:T(8,128)S(1)} %add_add_fusion.2), channel_id=1, source_target_pairs={{0,64},{4,68},{8,72},{12,76},{16,80},{20,84},{24,88},{28,92},{32,9... | collective-permute-start | bytes 12296 | tf_op jit(solution)/shard_map/ppermute | solution.py:310
  145.2 3.9 %collective-permute-start.33 = (f32[8,128]{1,0:T(8,128)S(1)}, f32[8,128]{1,0:T(8,128)S(1)}, u32[]{:S(2)}, u32[]{:S(2)}) collective-permute-start(f32[8,128]{1,0:T(8,128)S(1)} %add_add_fusion.2), channel_id=1, source_target_pairs={{0,32},{4,36},{8,40},{12,44},{16,48},{20,52},{24,56},{28,60},{32,6... | collective-permute-start | bytes 12296 | tf_op jit(solution)/shard_map/ppermute | solution.py:310
  149.1 5.8 %collective-permute-start.38 = (f32[8,128]{1,0:T(8,128)S(1)}, f32[8,128]{1,0:T(8,128)S(1)}, u32[]{:S(2)}, u32[]{:S(2)}) collective-permute-start(f32[8,128]{1,0:T(8,128)S(1)} %add_add_fusion.1), channel_id=1, source_target_pairs={{0,24},{4,28},{8,0},{12,4},{16,8},{20,12},{24,16},{28,20},{32,56},... | collective-permute-start | bytes 12296 | tf_op jit(solution)/shard_map/ppermute | solution.py:310
  149.2 8.5 %collective-permute-start.37 = (f32[8,128]{1,0:T(8,128)S(1)}, f32[8,128]{1,0:T(8,128)S(1)}, u32[]{:S(2)}, u32[]{:S(2)}) collective-permute-start(f32[8,128]{1,0:T(8,128)S(1)} %add_add_fusion.1), channel_id=1, source_target_pairs={{0,16},{4,20},{8,24},{12,28},{16,0},{20,4},{24,8},{28,12},{32,48},... | collective-permute-start | bytes 12296 | tf_op jit(solution)/shard_map/ppermute | solution.py:310
  149.3 10.0 %collective-permute-start.36 = (f32[8,128]{1,0:T(8,128)S(1)}, f32[8,128]{1,0:T(8,128)S(1)}, u32[]{:S(2)}, u32[]{:S(2)}) collective-permute-start(f32[8,128]{1,0:T(8,128)S(1)} %add_add_fusion.1), channel_id=1, source_target_pairs={{0,8},{4,12},{8,16},{12,20},{16,24},{20,28},{24,0},{28,4},{32,40},... | collective-permute-start | bytes 12296 | tf_op jit(solution)/shard_map/ppermute | solution.py:310
  150.6 28.4 %collective-permute-start.25 = (f32[512,128]{1,0:T(8,128)}, f32[512,128]{1,0:T(8,128)S(1)}, u32[]{:S(2)}, u32[]{:S(2)}) collective-permute-start(f32[512,128]{1,0:T(8,128)} %get-tuple-element.71), channel_id=1, source_target_pairs={{0,3},{1,0},{2,1},{3,2},{4,7},{5,4},{6,5},{7,6},{8,11},{9,8},{10,9... | collective-permute-start | bytes 786440 | tf_op jit(solution)/shard_map/ppermute | solution.py:295
  150.6 28.4 %collective-permute-start.26 = (f32[512,128]{1,0:T(8,128)}, f32[512,128]{1,0:T(8,128)S(1)}, u32[]{:S(2)}, u32[]{:S(2)}) collective-permute-start(f32[512,128]{1,0:T(8,128)} %get-tuple-element.72), channel_id=1, source_target_pairs={{0,127},{1,124},{2,125},{3,126},{4,3},{5,0},{6,1},{7,2},{8,7},{9,4... | collective-permute-start | bytes 786440 | tf_op jit(solution)/shard_map/ppermute | solution.py:295
  154.9 24.2 %collective-permute-start.27 = (f32[512,128]{1,0:T(8,128)}, f32[512,128]{1,0:T(8,128)S(1)}, u32[]{:S(2)}, u32[]{:S(2)}) collective-permute-start(f32[512,128]{1,0:T(8,128)} %get-tuple-element.73), channel_id=1, source_target_pairs={{0,123},{1,120},{2,121},{3,122},{4,127},{5,124},{6,125},{7,126},{8... | collective-permute-start | bytes 786440 | tf_op jit(solution)/shard_map/ppermute | solution.py:295
  157.7 21.4 %collective-permute-start.28 = (f32[512,128]{1,0:T(8,128)}, f32[512,128]{1,0:T(8,128)S(1)}, u32[]{:S(2)}, u32[]{:S(2)}) collective-permute-start(f32[512,128]{1,0:T(8,128)} %get-tuple-element.74), channel_id=1, source_target_pairs={{0,119},{1,116},{2,117},{3,118},{4,123},{5,120},{6,121},{7,122},{8... | collective-permute-start | bytes 786440 | tf_op jit(solution)/shard_map/ppermute | solution.py:295
  159.3 2.1 %collective-permute-start.39 = (f32[8,128]{1,0:T(8,128)S(1)}, f32[8,128]{1,0:T(8,128)S(1)}, u32[]{:S(2)}, u32[]{:S(2)}) collective-permute-start(f32[8,128]{1,0:T(8,128)S(1)} %add_add_fusion), channel_id=1, source_target_pairs={{0,4},{4,0},{8,12},{12,8},{16,20},{20,16},{24,28},{28,24},{32,36},... | collective-permute-start | bytes 12296 | tf_op jit(solution)/shard_map/ppermute | solution.py:310
  161.3 17.7 %collective-permute-start.29 = (f32[176,128]{1,0:T(8,128)}, f32[176,128]{1,0:T(8,128)S(1)}, u32[]{:S(2)}, u32[]{:S(2)}) collective-permute-start(f32[176,128]{1,0:T(8,128)} %get-tuple-element.75), channel_id=1, source_target_pairs={{4,0},{8,4},{12,8},{16,12},{20,16},{24,20},{28,24},{32,28},{36,32}... | collective-permute-start | bytes 270344 | tf_op jit(solution)/shard_map/ppermute | solution.py:301
  (27 other events, 253.0 us)

commit v2 on v1

v2 whole, which is shorter than its diff:
```python
import jax
import jax.numpy as jnp
from jax import lax
from jax.experimental import pallas as pl
from jax.experimental.pallas import tpu as pltpu
from jax.sharding import PartitionSpec as P

W = 4
CAP = 8
SLOTS = W * CAP
SEG = 16
SD = 64
LC = 128
G = 176
NS = 2400
CR = SEG * SD
MASTER = G + CR
RIGHT = G + 2 * CR
KP = 2560
K_LOW, K_WIDE = 1152, 1152
TILE = 480
TILES = NS // TILE
PIECE = 240
PIECES = NS // PIECE
DEPTH = 4
NEAR = CAP * SD
FAR = SEG * SD
MIB = 1 << 20

f32 = jnp.float32
bf16 = jnp.bfloat16
highest = lax.Precision.HIGHEST
VM = pl.BlockSpec(memory_space=pltpu.VMEM)
SM = pl.BlockSpec(memory_space=pltpu.SMEM)
ANY = pl.BlockSpec(memory_space=pl.ANY)


def rows(start, size):
    return pl.ds(pl.multiple_of(start, 8), size)


def halves(value):
    high = value.astype(bf16)
    low = (value - high.astype(f32)).astype(bf16)
    return high, low


def product(high, low, both):
    first = jnp.dot(high, both, preferred_element_type=f32)
    second = jnp.dot(low, both, preferred_element_type=f32)
    return (first[:, LC:] + second[:, LC:]) + second[:, :LC] + first[:, :LC]


def segment(index):
    return pl.ds(pl.multiple_of(index * SD, SD), SD)


def flag(condition):
    return jnp.where(condition, 1.0, 0.0).astype(f32)


def pack_kernel(
    me, owner, slot, act_any, rhs_any, glue_any,
    near, far, pc, mask, pg, near_source, far_source, place,
    act, rhs, act_wide, count, position, sems,
):
    copies = [
        pltpu.make_async_copy(src, dst, sems.at[i])
        for i, (src, dst) in enumerate(((act_any, act), (rhs_any, rhs), (glue_any, pg)))
    ]
    for copy in copies:
        copy.start()
    for i in range(SEG):
        far_source[i] = -1
    for n in range(CAP):
        near_source[n] = -1
    for o in range(W + 1):
        count[o] = 0
    for k in range(SEG):
        o = lax.rem(owner[k] - me[0] + 32, 32)
        n = count[o]
        q = count[W]
        count[o] = n + 1
        position[k] = o * CAP + n

        @pl.when(o == 0)
        def _():
            near_source[n] = k
            place[k] = n

        @pl.when(o > 0)
        def _():
            far_source[q] = k
            place[k] = CAP + q
            count[W] = q + 1

    for copy in copies:
        copy.wait()
    active = act[...].astype(f32)
    act_wide[...] = jnp.concatenate([active, jnp.zeros((SEG, 128 - SD), f32)], axis=1)
    columns = jnp.transpose(jnp.concatenate([act_wide[...], jnp.zeros((128 - SEG, 128), f32)], axis=0))
    for k in range(SEG):
        wide = jnp.broadcast_to(columns[:SD, k : k + 1], (SD, LC))
        here = slice(k * SD, (k + 1) * SD)
        mask[here, :] = wide
        pc[here, :] = rhs[here, :] * wide
    lane = lax.broadcasted_iota(jnp.int32, (1, 128), 1)
    for ref, source, slots in ((near, near_source, CAP), (far, far_source, SEG)):
        for n in range(slots):
            k = source[n]
            at = jnp.maximum(k, 0)
            used = flag(k >= 0)
            ref[n * SD : (n + 1) * SD, :] = pc[segment(at), :] * used
            tag = (slot[at] + 1).astype(f32)
            seat = position[at].astype(f32)
            row = jnp.where(lane == SD, tag, jnp.where(lane == SD + 1, seat, act_wide[pl.ds(at, 1), :]))
            ref[slots * SD + n : slots * SD + n + 1, :] = used * row


def spread(source, inverse, outs, info):
    for o in range(1, W):
        for n in range(CAP):
            q = inverse[o * CAP + n]
            at = jnp.maximum(q, 0)
            used = flag(q >= 0)
            outs[o - 1][n * SD : (n + 1) * SD, :] = source[segment(at), :] * used
            if info:
                outs[o - 1][NEAR + n : NEAR + n + 1, :] = source[pl.ds(FAR + at, 1), :] * used


def collect(route, replies, out):
    for q in range(SEG):
        o, n = lax.div(route[q], CAP), lax.rem(route[q], CAP)
        value = replies[1][segment(n), :]
        for w in (0, 2):
            value = jnp.where(o == w + 1, replies[w][segment(n), :], value)
        out[q * SD : (q + 1) * SD, :] = value


def fetch(place, near, far, k):
    seat = place[k]
    here = near[segment(jnp.minimum(seat, CAP - 1)), :]
    there = far[segment(jnp.maximum(seat - CAP, 0)), :]
    return jnp.where(seat < CAP, here, there)


def relay_kernel(far, token, out1, out2, out3, route, inverse, info, sem):
    copy = pltpu.make_async_copy(far.at[pl.ds(FAR, SEG), :], info, sem)
    copy.start()
    for i in range(SLOTS):
        inverse[i] = -1
    copy.wait()
    for q in range(SEG):
        seat = info[q, SD + 1].astype(jnp.int32)
        route[q] = seat

        @pl.when(seat > 0)
        def _():
            inverse[seat] = q

    spread(far, inverse, (out1, out2, out3), True)


def exchange_kernel(
    route, inverse, near_source, far, r1, r2, r3, u, mask, right, token0, token1,
    f1, f2, f3, back, near, face,
):
    spread(far, inverse, (f1, f2, f3), False)
    collect(route, (r1, r2, r3), back)
    for n in range(CAP):
        k = near_source[n]
        at = jnp.maximum(k, 0)
        near[n * SD : (n + 1) * SD, :] = u[rows(G + at * SD, SD), :] * mask[segment(at), :] * flag(k >= 0)
    face[...] = right[...]


def collect_kernel(route, r1, r2, r3, back):
    collect(route, (r1, r2, r3), back)


def split_kernel(
    c_any, left, pc, pg, mortar, high, low, partial, forth, back, both, tiles, sems
):
    def fetch(i):
        return pltpu.make_async_copy(
            c_any.at[pl.ds(i * PIECE, PIECE), :], tiles.at[i % DEPTH], sems.at[i % DEPTH]
        )

    for i in range(DEPTH - 1):
        fetch(i).start()
    both[...] = jnp.zeros_like(both)
    for start, size, ref, sign in ((0, G, left, -1.0), (G, CR, pc, 1.0), (RIGHT, G, pg, 1.0)):
        part_high, part_low = halves(ref[...] * sign)
        both[start : start + size, :LC] = part_high
        both[start : start + size, LC:] = part_low
    for j in range(SEG):
        block = mortar[j * SD : (j + 1) * SD, :]
        for ref, value in ((forth, -jnp.transpose(block)), (back, block)):
            part_high, part_low = halves(value)
            ref[2 * j * SD : (2 * j + 1) * SD, :] = part_high
            ref[(2 * j + 1) * SD : (2 * j + 2) * SD, :] = part_low
    for i in range(PIECES):
        if i + DEPTH - 1 < PIECES:
            fetch(i + DEPTH - 1).start()
        fetch(i).wait()
        at = slice(i * PIECE, (i + 1) * PIECE)
        part_high, part_low = halves(tiles[i % DEPTH])
        pad = jnp.zeros((PIECE, KP - NS), bf16)
        high[at, :NS] = part_high
        high[at, NS:] = pad
        low[at, :NS] = part_low
        low[at, NS:] = pad
        partial[at, :] = product(high[at, :], low[at, :], both[...])


def mortar_apply(mortar, j, value):
    part_high, part_low = halves(value)
    wide = jnp.concatenate([part_high, part_low], axis=1)
    parts = jnp.dot(mortar[2 * j * SD : (2 * j + 2) * SD, :], wide, preferred_element_type=f32)
    return (parts[SD:, LC:] + parts[SD:, :LC]) + parts[:SD, LC:] + parts[:SD, :LC]


def column_sum(value):
    return jnp.sum(value, axis=0, keepdims=True)


def first_kernel(
    in0, in1, in2, in3, forth, back, left, pc, pg, partial, mask, source, high, low,
    far, p0, p1, p2, p3, u, projected, actives, slots, sums, left_face, right_face,
    gathered, term, both, info, info_sems,
):
    ins = (in0, in1, in2, in3)
    infos = []
    for o in range(W):
        copy = pltpu.make_async_copy(ins[o].at[pl.ds(NEAR, 8), :], info.at[pl.ds(o * 8, 8), :], info_sems.at[o])
        copy.start()
        infos.append(copy)
    gathered[...] = jnp.zeros_like(gathered)
    actives[...] = jnp.zeros_like(actives)
    both[...] = jnp.zeros_like(both)
    for copy in infos:
        copy.wait()
    for o in range(W):
        tile = jnp.concatenate([ins[o][NEAR : NEAR + 8, :], jnp.zeros((120, 128), f32)], axis=0)
        columns = jnp.transpose(tile)
        for n in range(CAP):
            j = info[o * 8 + n, SD].astype(jnp.int32) - 1
            slots[o * CAP + n] = j
            at = rows(jnp.maximum(j, 0) * SD, SD)
            gathered[at, :] += ins[o][n * SD : (n + 1) * SD, :]
            actives[at, :] += jnp.broadcast_to(columns[:SD, n : n + 1], (SD, LC))
    for j in range(SEG):
        value = mortar_apply(forth, j, gathered[j * SD : (j + 1) * SD, :])
        term[j * SD : (j + 1) * SD, :] = value
        part_high, part_low = halves(value)
        start = MASTER - K_LOW + j * SD
        both[start : start + SD, :LC] = part_high
        both[start : start + SD, LC:] = part_low
    for i in range(TILES):
        at = slice(i * TILE, (i + 1) * TILE)
        u[at, :] = partial[at, :] + product(
            high[at, K_LOW : K_LOW + K_WIDE], low[at, K_LOW : K_LOW + K_WIDE], both[...]
        )
    left_face[...] = u[:G, :]
    right_face[...] = u[RIGHT:, :]
    for j in range(SEG):
        start = MASTER + j * SD
        projected[j * SD : (j + 1) * SD, :] = mortar_apply(back, j, u[start : start + SD, :])
    for q in range(SEG):
        k = source[q]
        at = jnp.maximum(k, 0)
        far[q * SD : (q + 1) * SD, :] = u[rows(G + at * SD, SD), :] * mask[segment(at), :] * flag(k >= 0)
    for o, reply in enumerate((p0, p1, p2, p3)):
        for n in range(CAP):
            j = jnp.maximum(slots[o * CAP + n], 0)
            reply[n * SD : (n + 1) * SD, :] = projected[segment(j), :]
    norm = column_sum(pg[...] * pg[...]) + column_sum(pc[...] * pc[...])
    curvature = (
        column_sum(pg[...] * u[RIGHT:, :])
        - column_sum(left[...] * u[:G, :])
        + column_sum(pc[...] * u[G:MASTER, :])
        + column_sum(term[...] * u[MASTER:RIGHT, :])
    )
    sums[...] = jnp.concatenate([norm, curvature, jnp.zeros((6, LC), f32)], axis=0)


def second_kernel(
    me, slots, place, f0, f1, f2, f3, near, far, next_left, prev_right, u0, projected0, actives, mask,
    forth, project, sums0, high, low,
    p0, p1, p2, p3, u, q_glue, q_contact, sums, left_face,
    gathered, loads, both, projected,
):
    forward, reply = (f0, f1, f2, f3), (p0, p1, p2, p3)
    inner = jnp.where(me[0] > 0, 1.0, 0.0).astype(f32)
    loads[:G, :] = (u0[:G, :] - prev_right[...]) * inner
    glue = u0[RIGHT:, :] - next_left[...]
    q_glue[...] = glue
    loads[RIGHT:, :] = glue
    gathered[...] = -(actives[...] * projected0[...])
    for o in range(W):
        for n in range(CAP):
            at = rows(jnp.maximum(slots[o * CAP + n], 0) * SD, SD)
            gathered[at, :] += forward[o][n * SD : (n + 1) * SD, :]
    for k in range(SEG):
        here = slice(k * SD, (k + 1) * SD)
        fetched = fetch(place, near, far, k)
        value = mask[here, :] * (u0[G + k * SD : G + (k + 1) * SD, :] - fetched)
        q_contact[here, :] = value
        loads[G + k * SD : G + (k + 1) * SD, :] = value
    for j in range(SEG):
        value = mortar_apply(forth, j, gathered[j * SD : (j + 1) * SD, :])
        loads[MASTER + j * SD : MASTER + (j + 1) * SD, :] = value
    part_high, part_low = halves(loads[...])
    both[:NS, :LC] = part_high
    both[:NS, LC:] = part_low
    both[NS:, :] = jnp.zeros((KP - NS, 2 * LC), bf16)
    for i in range(TILES):
        at = slice(i * TILE, (i + 1) * TILE)
        u[at, :] = product(high[at, :], low[at, :], both[...])
    left_face[...] = u[:G, :]
    for j in range(SEG):
        start = MASTER + j * SD
        projected[j * SD : (j + 1) * SD, :] = mortar_apply(project, j, u[start : start + SD, :])
    for o in range(W):
        for n in range(CAP):
            j = jnp.maximum(slots[o * CAP + n], 0)
            reply[o][n * SD : (n + 1) * SD, :] = projected[rows(j * SD, SD), :]
    square = column_sum(q_glue[...] * q_glue[...]) + column_sum(q_contact[...] * q_contact[...])
    energy = column_sum(loads[...] * u[...])
    sums[...] = jnp.concatenate([sums0[0:2, :], square, energy, jnp.zeros((4, LC), f32)], axis=0)


def last_kernel(
    place, near, far, next_left, u, q_glue, q_contact, pc, pg, mask, sums,
    mult_glue, mult_contact, res_glue, res_contact,
):
    norm0, curvature0, square, energy = (sums[i : i + 1, :] for i in range(4))
    alpha0 = norm0 / curvature0
    norm1 = (norm0 - alpha0 * curvature0) + alpha0 * (alpha0 * square - curvature0)
    own = (curvature0 - alpha0 * square) + alpha0 * (alpha0 * energy - square)
    cross = curvature0 - alpha0 * square
    ratio = norm1 / norm0
    curvature1 = own + ratio * (2.0 * cross + ratio * curvature0)
    alpha1 = norm1 / curvature1

    def finish(r0, q, w):
        r1 = r0 - alpha0 * q
        direction = r1 + ratio * r0
        image = (q - alpha0 * w) + ratio * q
        return alpha0 * r0 + alpha1 * direction, r1 - alpha1 * image

    mult, res = finish(pg[...], q_glue[...], u[RIGHT:, :] - next_left[...])
    mult_glue[...] = mult
    res_glue[...] = res
    for k in range(SEG):
        here = slice(k * SD, (k + 1) * SD)
        fetched = fetch(place, near, far, k)
        value = mask[here, :] * (u[G + k * SD : G + (k + 1) * SD, :] - fetched)
        mult, res = finish(pc[here, :], q_contact[here, :], value)
        mult_contact[here, :] = mult
        res_contact[here, :] = res


def shape(*dims, dtype=f32):
    return jax.ShapeDtypeStruct(dims, dtype)


def params(mib):
    return pltpu.CompilerParams(vmem_limit_bytes=mib * MIB)


def sent(value, body_step, sub_step):
    subs, bodies = lax.axis_size("sub"), lax.axis_size("body")
    pairs = [
        (s * bodies + b, ((s + sub_step) % subs) * bodies + (b + body_step) % bodies)
        for s in range(subs)
        for b in range(bodies)
    ]
    return lax.ppermute(value, ("sub", "body"), pairs)


def passed_along(value, steps):
    count = lax.axis_size("sub")
    first, last = (max(0, -steps), min(count, count - steps))
    return lax.ppermute(value, "sub", [(source, source + steps) for source in range(first, last)])


def rotated(value, block, stride, steps):
    count = lax.axis_size("sub")
    pairs = []
    for s in range(count):
        place = s // stride % block
        pairs.append((s, s + ((place + steps) % block - place) * stride))
    return lax.ppermute(value, "sub", pairs)


def total(value):
    value = value + sent(value, 1, 0) + sent(value, 2, 0) + sent(value, 3, 0)
    for stride in (8, 2):
        value = value + sum(rotated(value, 4, stride, k) for k in (1, 2, 3))
    return value + rotated(value, 2, 1, 1)


def kept(value):
    return pltpu.with_memory_space_constraint(value, pltpu.VMEM)


def per_device(compliance, mortar, rhs_glue, rhs_contact, owner_sub, master_slot, active_set):
    schur_block = compliance[0, 0]
    blocks = mortar.reshape(CR, SD)
    rhs = rhs_contact.reshape(CR, LC)
    me = lax.axis_index("sub").astype(jnp.int32).reshape(1)
    seg_block = shape(NEAR, LC)
    far_block = shape(FAR, LC)
    index = [shape(n, dtype=jnp.int32) for n in (CAP, SEG, SEG)]

    near, far, pc, mask, pg, near_source, far_source, place = pl.pallas_call(
        pack_kernel,
        out_shape=[shape(NEAR + CAP, LC), shape(FAR + SEG, LC)]
        + [shape(CR, LC)] * 2
        + [shape(G, LC)]
        + index,
        in_specs=[SM, SM, SM, ANY, ANY, ANY],
        out_specs=[VM] * 5 + [SM] * 3,
        scratch_shapes=[
            pltpu.VMEM((SEG, SD), jnp.int32),
            pltpu.VMEM((CR, LC), f32),
            pltpu.VMEM((SEG, 128), f32),
            pltpu.SMEM((W + 1,), jnp.int32),
            pltpu.SMEM((SEG,), jnp.int32),
            pltpu.SemaphoreType.DMA((3,)),
        ],
        compiler_params=params(8),
        name="pack",
    )(me, owner_sub.reshape(SEG), master_slot.reshape(SEG), active_set.reshape(SEG, SD), rhs, rhs_glue[0, 0])

    far_in = sent(far, 1, 2)
    near_in = sent(near, 1, 0)
    left = passed_along(pg, 1)

    stacked = shape(2 * CR, SD, dtype=bf16)
    high, low, partial, forth, project = pl.pallas_call(
        split_kernel,
        out_shape=[pltpu.VMEM((NS, KP), bf16)] * 2 + [shape(NS, LC), stacked, stacked],
        in_specs=[ANY] + [VM] * 4,
        out_specs=[VM] * 5,
        scratch_shapes=[
            pltpu.VMEM((KP, 2 * LC), bf16),
            pltpu.VMEM((DEPTH, PIECE, NS), f32),
            pltpu.SemaphoreType.DMA((DEPTH,)),
        ],
        compiler_params=params(20),
        cost_estimate=pl.CostEstimate(
            flops=8 * NS * KP * LC, bytes_accessed=4 * NS * NS, transcendentals=0
        ),
        name="split",
    )(schur_block, left, pc, pg, blocks)
    high, low = kept(high), kept(low)

    out1, kept2, out3, route, inverse = pl.pallas_call(
        relay_kernel,
        out_shape=[shape(NEAR + CAP, LC)] * 3 + [shape(SEG, dtype=jnp.int32), shape(SLOTS, dtype=jnp.int32)],
        in_specs=[VM, ANY],
        out_specs=[VM] * 3 + [SM] * 2,
        scratch_shapes=[pltpu.SMEM((SEG, 128), f32), pltpu.SemaphoreType.DMA],
        compiler_params=params(6),
        name="relay",
    )(far_in, partial)
    in1, in3 = sent(out1, 0, -1), sent(out3, 0, 1)

    outs = pl.pallas_call(
        first_kernel,
        out_shape=[far_block] + [seg_block] * 4
        + [shape(NS, LC), shape(CR, LC), shape(CR, LC), shape(SLOTS, dtype=jnp.int32)]
        + [shape(8, LC), shape(G, LC), shape(G, LC)],
        in_specs=[VM] * 11 + [SM, VM, VM],
        out_specs=[VM] * 8 + [SM] + [VM] * 3,
        scratch_shapes=[
            pltpu.VMEM((CR, LC), f32),
            pltpu.VMEM((CR, LC), f32),
            pltpu.VMEM((K_WIDE, 2 * LC), bf16),
            pltpu.SMEM((W * 8, 128), f32),
            pltpu.SemaphoreType.DMA((W,)),
        ],
        compiler_params=params(12),
        name="first",
    )(near_in, in1, kept2, in3, forth, project, left, pc, pg, partial, mask, far_source, high, low)
    far, replies = outs[0], outs[1:5]
    u0, projected0, actives, slots, sums0, left_face, right_face = outs[5:]

    far_in = sent(far, 1, 2)
    reply1, reply3 = sent(replies[1], 0, 1), sent(replies[3], 0, -1)
    near_back = sent(replies[0], -1, 0)
    next_left = passed_along(left_face, -1)

    out1, kept2, out3, far, near, right_face = pl.pallas_call(
        exchange_kernel,
        out_shape=[seg_block] * 3 + [far_block, seg_block, shape(G, LC)],
        in_specs=[SM] * 3 + [VM] * 7 + [ANY] * 2,
        out_specs=[VM] * 6,
        compiler_params=params(12),
        name="exchange",
    )(route, inverse, near_source, far_in, reply1, replies[2], reply3, u0, mask, right_face, near_back, next_left)
    far_back = sent(far, -1, -2)
    in1, in3 = sent(out1, 0, -1), sent(out3, 0, 1)
    near_in = sent(near, 1, 0)
    prev_right = passed_along(right_face, 1)

    outs = pl.pallas_call(
        second_kernel,
        out_shape=[seg_block] * 4
        + [shape(NS, LC), shape(G, LC), shape(CR, LC), shape(8, LC), shape(G, LC)],
        in_specs=[SM] * 3 + [VM] * 17,
        out_specs=[VM] * 9,
        scratch_shapes=[
            pltpu.VMEM((CR, LC), f32),
            pltpu.VMEM((NS, LC), f32),
            pltpu.VMEM((KP, 2 * LC), bf16),
            pltpu.VMEM((CR, LC), f32),
        ],
        compiler_params=params(12),
        name="second",
    )(me, slots, place, near_in, in1, kept2, in3, near_back, far_back, next_left, prev_right,
      u0, projected0, actives, mask, forth, project, sums0, high, low)
    replies, (u1, q_glue, q_contact, sums, left_face) = outs[:4], outs[4:]

    reply1, reply3 = sent(replies[1], 0, 1), sent(replies[3], 0, -1)
    near_back = sent(replies[0], -1, 0)
    next_left = passed_along(left_face, -1)
    sums = total(sums)

    far = pl.pallas_call(
        collect_kernel,
        out_shape=far_block,
        in_specs=[SM] + [VM] * 3,
        out_specs=VM,
        compiler_params=params(6),
        name="collect",
    )(route, reply1, replies[2], reply3)
    far_back = sent(far, -1, -2)

    mult_glue, mult_contact, res_glue, res_contact = pl.pallas_call(
        last_kernel,
        out_shape=[shape(G, LC), shape(CR, LC)] * 2,
        in_specs=[SM] + [VM] * 10,
        out_specs=[VM] * 4,
        compiler_params=params(24),
        name="last",
    )(place, near_back, far_back, next_left, u1, q_glue, q_contact, pc, pg, mask, sums)
    contact = (1, 1, SEG, SD, LC)
    return (
        mult_glue[None, None],
        mult_contact.reshape(contact),
        res_glue[None, None],
        res_contact.reshape(contact),
    )


def solution(mesh):
    in_specs = (
        P("body", "sub", None, None),
        P("body", "sub", None, None, None),
        P("body", "sub", None, None),
        P("body", "sub", None, None, None),
        P("body", "sub", None, None),
        P("body", "sub", None),
        P("body", "sub", None, None),
    )
    out_specs = (
        P("body", "sub", None, None),
        P("body", "sub", None, None, None),
        P("body", "sub", None, None),
        P("body", "sub", None, None, None),
    )
    return jax.shard_map(
        per_device, mesh=mesh, in_specs=in_specs, out_specs=out_specs, check_vma=False
    )
```

time: 185 us -> 130 us (0.70)
  starting transfers between devices: 78.5 us -> 60.2 us
  Pallas kernels: 43.4 us -> 30.3 us
  local copies, waits for them, and re-layouts: 16.4 us -> 4.97 us
  waiting for transfers between devices: 43.7 us -> 32.8 us
    ppermute x14 -> x7, starting transfers between devices: 18.3 us -> 3.05 us  [rotated(): return lax.ppermute(value, 'sub', pairs)]
    unnamed x70 -> x12, local copies, waits for them, and re-layouts: 16.4 us -> 4.97 us
    ppermute x4, waiting for transfers between devices: 16.1 us -> 5.12 us  [passed_along(): lax.ppermute(value, 'sub', [(source, source + steps) for source in range(...]
    pallas_call x1, Pallas kernels: 15.4 us -> 8.01 us  [per_device(): pl.pallas_call(second_kernel, out_shape=[seg_block] * 4 + [shape(NS, LC),...]
    ppermute x22 -> x19, starting transfers between devices: 47.4 us -> 40.5 us  [sent(): return lax.ppermute(value, ('sub', 'body'), pairs)]
    pallas_call x3 -> x6, Pallas kernels: 26.1 us -> 20.5 us  [the longest x1 9.86 us: per_device(): pl.pallas_call(split_kernel, out_shape=[pltpu.VMEM((NS, KP), bf16)] * 2 +...]
    ppermute x4, starting transfers between devices: 12.7 us -> 16.6 us  [passed_along(): lax.ppermute(value, 'sub', [(source, source + steps) for source in range(...]
    ppermute x14 -> x7, waiting for transfers between devices: 7.54 us -> 9.88 us  [rotated(): return lax.ppermute(value, 'sub', pairs)]
  transfers between devices with their start and end apart: 40 -> 30, of which waited for: 13 -> 13; matrix products, arithmetic and copies ran while one was open for 0% -> 0% of each run, Pallas kernels for 10% -> 9%
where the time goes in v2:
time: 130 us; the launch traced here: 129 us
  starting transfers between devices  60.2 us (46%)
  waiting for transfers between devices  32.8 us (25%)
  Pallas kernels  30.3 us (23%)
  local copies, waits for them, and re-layouts  4.97 us (4%)
    ppermute x19, starting transfers between devices, sent(): return lax.ppermute(value, ('sub', 'body'), pairs)  40.5 us
    ppermute x19, waiting for transfers between devices, sent(): return lax.ppermute(value, ('sub', 'body'), pairs)  17.8 us
    ppermute x4, starting transfers between devices, passed_along(): lax.ppermute(value, 'sub', [(source, source + steps) for source in range(...  16.6 us
    ppermute x7, waiting for transfers between devices, rotated(): return lax.ppermute(value, 'sub', pairs)  9.88 us
    pallas_call x1, Pallas kernels, per_device(): pl.pallas_call(split_kernel, out_shape=[pltpu.VMEM((NS, KP), bf16)] * 2 +...  9.86 us
    pallas_call x1, Pallas kernels, per_device(): pl.pallas_call(second_kernel, out_shape=[seg_block] * 4 + [shape(NS, LC),...  8.01 us
    pallas_call x1, Pallas kernels, per_device(): pl.pallas_call(first_kernel, out_shape=[far_block] + [seg_block] * 4 + [s...  6 us
    ppermute x4, waiting for transfers between devices, passed_along(): lax.ppermute(value, 'sub', [(source, source + steps) for source in range(...  5.12 us
  transfers between devices with their start and end apart: 30, of which 13 were waited for; matrix products, arithmetic and copies ran while one was open for 0% of the time, Pallas kernels for 9%

profile of v2, /device:TPU:1, one launch (start us, length us, event | category | flops | bytes accessed | tf_op | source)
XLA Modules:
  0.0 129.2 jit_solution(1490169527316443544)
XLA Ops:
  0.6 1.0 copy-done.1
  1.7 0.9 copy-done.2
  2.6 0.7 copy-done.3
  3.3 0.7 copy-done.4
  3.9 0.7 copy-done.5
  4.6 1.8 %pack.1 = (f32[520,128]{1,0:T(8,128)S(1)}, f32[1040,128]{1,0:T(8,128)S(1)}, f32[1024,128]{1,0:T(8,128)S(1)}, f32[1024,128]{1,0:T(8,128)S(1)}, f32[176,128]{1,0:T...) custom-call(s32[1]{0:T(128)} %bitcast.me, s32[16]{0:T(128)S(1)} %bitcast.16, s32[16]{0:T(128)S(1)} %bitcast.17, ...), custom_call_target="tpu_custom_call" | custom-call | tf_op jit(solution)/shard_map/pack/pallas_call | solution.py:417
  6.4 4.9 %collective-permute-start.2 = (f32[176,128]{1,0:T(8,128)S(1)}, f32[176,128]{1,0:T(8,128)S(1)}, u32[]{:S(2)}, u32[]{:S(2)}) collective-permute-start(f32[176,128]{1,0:T(8,128)S(1)} %get-tuple-element.56.pg), channel_id=1, source_target_pairs={{0,4},{4,8},{8,12},{12,16},{16,20},{20,24},{24,28},{28,32},{32,36}... | collective-permute-start | bytes 270344 | tf_op jit(solution)/shard_map/ppermute | solution.py:385
  11.3 1.4 %collective-permute-start = (f32[520,128]{1,0:T(8,128)S(1)}, f32[520,128]{1,0:T(8,128)S(1)}, u32[]{:S(2)}, u32[]{:S(2)}) collective-permute-start(f32[520,128]{1,0:T(8,128)S(1)} %get-tuple-element.54), channel_id=1, source_target_pairs={{0,1},{1,2},{2,3},{3,0},{4,5},{5,6},{6,7},{7,4},{8,9},{9,10},{10,1... | collective-permute-start | bytes 798728 | tf_op jit(solution)/shard_map/ppermute | solution.py:379
  12.7 2.6 %collective-permute-start.1 = (f32[1040,128]{1,0:T(8,128)S(1)}, f32[1040,128]{1,0:T(8,128)S(1)}, u32[]{:S(2)}, u32[]{:S(2)}) collective-permute-start(f32[1040,128]{1,0:T(8,128)S(1)} %get-tuple-element.55), channel_id=1, source_target_pairs={{0,9},{1,10},{2,11},{3,8},{4,13},{5,14},{6,15},{7,12},{8,17},{9,18... | collective-permute-start | bytes 1597448 | tf_op jit(solution)/shard_map/ppermute | solution.py:379
  15.3 1.0 copy-done
  16.4 9.9 %split.1 = (bf16[2400,2560]{1,0:T(8,128)(2,1)S(1)}, bf16[2400,2560]{1,0:T(8,128)(2,1)S(1)}, f32[2400,128]{1,0:T(8,128)S(1)}, bf16[2048,64]{1,0:T(8,128)(2,1)S(1)}, bf16[2048,64]{1,0:T(8,128)(2,1)S(1)}) custom-call(f32[2400,2400]{1,0:T(8,128)} %bitcast.18, f32[176,128]{1,0:T(8,128)S(1)} %collective-permute-done.2.left, f32[1024,128]{1,0:T(8,128)S(1)} %get-tuple-element.57.pc, ...), custom_call_target="tpu_custom_call" | custom-call | flops 6291456000 | bytes 23040000 | tf_op jit(solution)/shard_map/split/pallas_call | solution.py:442
  26.2 4.9 %collective-permute-done.1.far = f32[1040,128]{1,0:T(8,128)S(1)} collective-permute-done((f32[1040,128]{1,0:T(8,128)S(1)}, f32[1040,128]{1,0:T(8,128)S(1)}, u32[]{:S(2)}, u32[]{:S(2)}) %collective-permute-start.1) | collective-permute-done | bytes 532512 | tf_op jit(solution)/shard_map/ppermute | solution.py:379
  31.1 1.4 %relay.1 = (f32[520,128]{1,0:T(8,128)S(1)}, f32[520,128]{1,0:T(8,128)S(1)}, f32[520,128]{1,0:T(8,128)S(1)}, s32[16]{0:T(128)S(1)}, s32[32]{0:T(128)S(1)}) custom-call(f32[1040,128]{1,0:T(8,128)S(1)} %collective-permute-done.1.far, f32[2400,128]{1,0:T(8,128)S(1)} %get-tuple-element.58.token.partial), custom_call_target="tpu_custom_call" | custom-call | tf_op jit(solution)/shard_map/relay/pallas_call | solution.py:460
  32.6 1.7 %collective-permute-start.4 = (f32[520,128]{1,0:T(8,128)S(1)}, f32[520,128]{1,0:T(8,128)S(1)}, u32[]{:S(2)}, u32[]{:S(2)}) collective-permute-start(f32[520,128]{1,0:T(8,128)S(1)} %get-tuple-element.61), channel_id=1, source_target_pairs={{0,4},{1,5},{2,6},{3,7},{4,8},{5,9},{6,10},{7,11},{8,12},{9,13},{1... | collective-permute-start | bytes 798728 | tf_op jit(solution)/shard_map/ppermute | solution.py:379
  34.4 4.1 %collective-permute-done.3.in1 = f32[520,128]{1,0:T(8,128)S(1)} collective-permute-done((f32[520,128]{1,0:T(8,128)S(1)}, f32[520,128]{1,0:T(8,128)S(1)}, u32[]{:S(2)}, u32[]{:S(2)}) %collective-permute-start.3) | collective-permute-done | bytes 266272 | tf_op jit(solution)/shard_map/ppermute | solution.py:379
  38.5 1.3 %collective-permute-done.4.in3 = f32[520,128]{1,0:T(8,128)S(1)} collective-permute-done((f32[520,128]{1,0:T(8,128)S(1)}, f32[520,128]{1,0:T(8,128)S(1)}, u32[]{:S(2)}, u32[]{:S(2)}) %collective-permute-start.4) | collective-permute-done | bytes 266272 | tf_op jit(solution)/shard_map/ppermute | solution.py:379
  39.8 6.0 %first.1 = (f32[1024,128]{1,0:T(8,128)S(1)}, f32[512,128]{1,0:T(8,128)S(1)}, f32[512,128]{1,0:T(8,128)S(1)}, f32[512,128]{1,0:T(8,128)S(1)}, f32[512,128]{1,0:T(...) custom-call(f32[520,128]{1,0:T(8,128)S(1)} %collective-permute-done., ...), custom_call_target="tpu_custom_call" | custom-call | tf_op jit(solution)/shard_map/first/pallas_call | solution.py:471
  45.8 1.4 %collective-permute-start.6 = (f32[512,128]{1,0:T(8,128)S(1)}, f32[512,128]{1,0:T(8,128)S(1)}, u32[]{:S(2)}, u32[]{:S(2)}) collective-permute-start(f32[512,128]{1,0:T(8,128)S(1)} %get-tuple-element.73), channel_id=1, source_target_pairs={{0,4},{1,5},{2,6},{3,7},{4,8},{5,9},{6,10},{7,11},{8,12},{9,13},{1... | collective-permute-start | bytes 786440 | tf_op jit(solution)/shard_map/ppermute | solution.py:379
  47.3 6.8 %collective-permute-start.7 = (f32[512,128]{1,0:T(8,128)S(1)}, f32[512,128]{1,0:T(8,128)S(1)}, u32[]{:S(2)}, u32[]{:S(2)}) collective-permute-start(f32[512,128]{1,0:T(8,128)S(1)} %get-tuple-element.75), channel_id=1, source_target_pairs={{0,124},{1,125},{2,126},{3,127},{4,0},{5,1},{6,2},{7,3},{8,4},{9,5... | collective-permute-start | bytes 786440 | tf_op jit(solution)/shard_map/ppermute | solution.py:379
  54.1 1.5 %collective-permute-start.8 = (f32[512,128]{1,0:T(8,128)S(1)}, f32[512,128]{1,0:T(8,128)S(1)}, u32[]{:S(2)}, u32[]{:S(2)}) collective-permute-start(f32[512,128]{1,0:T(8,128)S(1)} %get-tuple-element.78), channel_id=1, source_target_pairs={{0,3},{1,0},{2,1},{3,2},{4,7},{5,4},{6,5},{7,6},{8,11},{9,8},{10,9... | collective-permute-start | bytes 786440 | tf_op jit(solution)/shard_map/ppermute | solution.py:379
  55.7 7.2 %collective-permute-start.9 = (f32[176,128]{1,0:T(8,128)S(1)}, f32[176,128]{1,0:T(8,128)S(1)}, u32[]{:S(2)}, u32[]{:S(2)}) collective-permute-start(f32[176,128]{1,0:T(8,128)S(1)} %get-tuple-element.79), channel_id=1, source_target_pairs={{4,0},{8,4},{12,8},{16,12},{20,16},{24,20},{28,24},{32,28},{36,32}... | collective-permute-start | bytes 270344 | tf_op jit(solution)/shard_map/ppermute | solution.py:385
  62.8 0.9 collective-permute-done.9.token1.next_left
  63.8 0.8 exchange.1
  64.5 5.4 %collective-permute-start.13 = (f32[1024,128]{1,0:T(8,128)S(1)}, f32[1024,128]{1,0:T(8,128)S(1)}, u32[]{:S(2)}, u32[]{:S(2)}) collective-permute-start(f32[1024,128]{1,0:T(8,128)S(1)} %get-tuple-element.84), channel_id=1, source_target_pairs={{0,123},{1,120},{2,121},{3,122},{4,127},{5,124},{6,125},{7,126},{8... | collective-permute-start | bytes 1572872 | tf_op jit(solution)/shard_map/ppermute | solution.py:379
  69.9 2.9 %collective-permute-start.11 = (f32[512,128]{1,0:T(8,128)S(1)}, f32[512,128]{1,0:T(8,128)S(1)}, u32[]{:S(2)}, u32[]{:S(2)}) collective-permute-start(f32[512,128]{1,0:T(8,128)S(1)} %get-tuple-element.81), channel_id=1, source_target_pairs={{0,124},{1,125},{2,126},{3,127},{4,0},{5,1},{6,2},{7,3},{8,4},{9,5... | collective-permute-start | bytes 786440 | tf_op jit(solution)/shard_map/ppermute | solution.py:379
  72.8 1.6 %collective-permute-start.12 = (f32[512,128]{1,0:T(8,128)S(1)}, f32[512,128]{1,0:T(8,128)S(1)}, u32[]{:S(2)}, u32[]{:S(2)}) collective-permute-start(f32[512,128]{1,0:T(8,128)S(1)} %get-tuple-element.83), channel_id=1, source_target_pairs={{0,4},{1,5},{2,6},{3,7},{4,8},{5,9},{6,10},{7,11},{8,12},{9,13},{1... | collective-permute-start | bytes 786440 | tf_op jit(solution)/shard_map/ppermute | solution.py:379
  74.4 2.6 %collective-permute-start.14 = (f32[176,128]{1,0:T(8,128)S(1)}, f32[176,128]{1,0:T(8,128)S(1)}, u32[]{:S(2)}, u32[]{:S(2)}) collective-permute-start(f32[176,128]{1,0:T(8,128)S(1)} %get-tuple-element.85), channel_id=1, source_target_pairs={{0,4},{4,8},{8,12},{12,16},{16,20},{20,24},{24,28},{28,32},{32,36}... | collective-permute-start | bytes 270344 | tf_op jit(solution)/shard_map/ppermute | solution.py:385
  77.0 1.7 %collective-permute-done.14.prev_right = f32[176,128]{1,0:T(8,128)S(1)} collective-permute-done((f32[176,128]{1,0:T(8,128)S(1)}, f32[176,128]{1,0:T(8,128)S(1)}, u32[]{:S(2)}, u32[]{:S(2)}) %collective-permute-start.14) | collective-permute-done | bytes 90144 | tf_op jit(solution)/shard_map/ppermute | solution.py:385
  78.7 4.8 %collective-permute-done.11.f1 = f32[512,128]{1,0:T(8,128)S(1)} collective-permute-done((f32[512,128]{1,0:T(8,128)S(1)}, f32[512,128]{1,0:T(8,128)S(1)}, u32[]{:S(2)}, u32[]{:S(2)}) %collective-permute-start.11) | collective-permute-done | bytes 262176 | tf_op jit(solution)/shard_map/ppermute | solution.py:379
  83.5 8.0 %second.1 = (f32[512,128]{1,0:T(8,128)S(1)}, f32[512,128]{1,0:T(8,128)S(1)}, f32[512,128]{1,0:T(8,128)S(1)}, f32[512,128]{1,0:T(8,128)S(1)}, f32[2400,128]{1,0:T...) custom-call(s32[1]{0:T(128)} %bitcast.me, ...), custom_call_target="tpu_custom_call" | custom-call | tf_op jit(solution)/shard_map/second/pallas_call | solution.py:509
  91.6 1.4 %collective-permute-start.17 = (f32[512,128]{1,0:T(8,128)S(1)}, f32[512,128]{1,0:T(8,128)S(1)}, u32[]{:S(2)}, u32[]{:S(2)}) collective-permute-start(f32[512,128]{1,0:T(8,128)S(1)} %get-tuple-element.92), channel_id=1, source_target_pairs={{0,124},{1,125},{2,126},{3,127},{4,0},{5,1},{6,2},{7,3},{8,4},{9,5... | collective-permute-start | bytes 786440 | tf_op jit(solution)/shard_map/ppermute | solution.py:379
  93.0 1.0 collective-permute-start.22
  94.1 0.7 collective-permute-start.21
  94.8 0.1 collective-permute-done.16.r1
  94.9 2.6 %collective-permute-done.17.r3 = f32[512,128]{1,0:T(8,128)S(1)} collective-permute-done((f32[512,128]{1,0:T(8,128)S(1)}, f32[512,128]{1,0:T(8,128)S(1)}, u32[]{:S(2)}, u32[]{:S(2)}) %collective-permute-start.17) | collective-permute-done | bytes 262176 | tf_op jit(solution)/shard_map/ppermute | solution.py:379
  97.5 0.7 collect.1
  98.1 11.7 %collective-permute-start.18 = (f32[1024,128]{1,0:T(8,128)S(1)}, f32[1024,128]{1,0:T(8,128)S(1)}, u32[]{:S(2)}, u32[]{:S(2)}) collective-permute-start(f32[1024,128]{1,0:T(8,128)S(1)} %collect.1), channel_id=1, source_target_pairs={{0,123},{1,120},{2,121},{3,122},{4,127},{5,124},{6,125},{7,126},{8... | collective-permute-start | bytes 1572872 | tf_op jit(solution)/shard_map/ppermute | solution.py:379
  109.9 0.1 collective-permute-start.24
  110.0 1.4 %collective-permute-start.23 = (f32[8,128]{1,0:T(8,128)S(1)}, f32[8,128]{1,0:T(8,128)S(1)}, u32[]{:S(2)}, u32[]{:S(2)}) collective-permute-start(f32[8,128]{1,0:T(8,128)S(1)} %add_add_fusion.2), channel_id=1, source_target_pairs={{0,32},{4,36},{8,40},{12,44},{16,48},{20,52},{24,56},{28,60},{32,6... | collective-permute-start | bytes 12296 | tf_op jit(solution)/shard_map/ppermute | solution.py:394
  111.4 7.3 %collective-permute-done.25 = f32[8,128]{1,0:T(8,128)S(1)} collective-permute-done((f32[8,128]{1,0:T(8,128)S(1)}, f32[8,128]{1,0:T(8,128)S(1)}, u32[]{:S(2)}, u32[]{:S(2)}) %collective-permute-start.25) | collective-permute-done | bytes 4128 | tf_op jit(solution)/shard_map/ppermute | solution.py:394
  118.7 0.1 collective-permute-start.27
  118.8 1.4 %collective-permute-start.26 = (f32[8,128]{1,0:T(8,128)S(1)}, f32[8,128]{1,0:T(8,128)S(1)}, u32[]{:S(2)}, u32[]{:S(2)}) collective-permute-start(f32[8,128]{1,0:T(8,128)S(1)} %add_add_fusion.1), channel_id=1, source_target_pairs={{0,8},{4,12},{8,16},{12,20},{16,24},{20,28},{24,0},{28,4},{32,40},... | collective-permute-start | bytes 12296 | tf_op jit(solution)/shard_map/ppermute | solution.py:394
  120.2 1.3 collective-permute-done.28
  121.5 1.9 %collective-permute-start.19 = (f32[176,128]{1,0:T(8,128)S(1)}, f32[176,128]{1,0:T(8,128)S(1)}, u32[]{:S(2)}, u32[]{:S(2)}) collective-permute-start(f32[176,128]{1,0:T(8,128)S(1)} %get-tuple-element.93), channel_id=1, source_target_pairs={{4,0},{8,4},{12,8},{16,12},{20,16},{24,20},{28,24},{32,28},{36,32}... | collective-permute-start | bytes 270344 | tf_op jit(solution)/shard_map/ppermute | solution.py:385
  123.4 0.2 collective-permute-done.26
  123.6 1.2 collective-permute-done.29
  124.7 2.6 %collective-permute-done.19.next_left = f32[176,128]{1,0:T(8,128)S(1)} collective-permute-done((f32[176,128]{1,0:T(8,128)S(1)}, f32[176,128]{1,0:T(8,128)S(1)}, u32[]{:S(2)}, u32[]{:S(2)}) %collective-permute-start.19) | collective-permute-done | bytes 90144 | tf_op jit(solution)/shard_map/ppermute | solution.py:385
  127.3 1.9 %last.1 = (f32[176,128]{1,0:T(8,128)}, f32[1024,128]{1,0:T(8,128)}, f32[176,128]{1,0:T(8,128)}, f32[1024,128]{1,0:T(8,128)}) custom-call(s32[16]{0:T(128)S(1)} %get-tuple-element.53.place, f32[512,128]{1,0:T(8,128)S(1)} %collective-permute-done.15.near, f32[1024,128]{1,0:T(8,128)S(1)} %collective-permute-done.18.far, ...), custom_call_target="tpu_custom_call" | custom-call | tf_op jit(solution)/shard_map/last/pallas_call | solution.py:542
  (36 shorter events, 0.5 us)
Async XLA Ops:
  0.6 1.0 copy-start.1
  1.7 0.9 copy-start.2
  2.6 0.7 copy-start.3
  3.3 0.7 copy-start.4
  3.9 0.7 copy-start.5
  6.4 9.0 %collective-permute-start.2 = (f32[176,128]{1,0:T(8,128)S(1)}, f32[176,128]{1,0:T(8,128)S(1)}, u32[]{:S(2)}, u32[]{:S(2)}) collective-permute-start(f32[176,128]{1,0:T(8,128)S(1)} %get-tuple-element.56.pg), channel_id=1, source_target_pairs={{0,4},{4,8},{8,12},{12,16},{16,20},{20,24},{24,28},{28,32},{32,36}... | collective-permute-start | bytes 270344 | tf_op jit(solution)/shard_map/ppermute | solution.py:385
  11.3 23.1 %collective-permute-start = (f32[520,128]{1,0:T(8,128)S(1)}, f32[520,128]{1,0:T(8,128)S(1)}, u32[]{:S(2)}, u32[]{:S(2)}) collective-permute-start(f32[520,128]{1,0:T(8,128)S(1)} %get-tuple-element.54), channel_id=1, source_target_pairs={{0,1},{1,2},{2,3},{3,0},{4,5},{5,6},{6,7},{7,4},{8,9},{9,10},{10,1... | collective-permute-start | bytes 798728 | tf_op jit(solution)/shard_map/ppermute | solution.py:379
  12.7 18.5 %collective-permute-start.1 = (f32[1040,128]{1,0:T(8,128)S(1)}, f32[1040,128]{1,0:T(8,128)S(1)}, u32[]{:S(2)}, u32[]{:S(2)}) collective-permute-start(f32[1040,128]{1,0:T(8,128)S(1)} %get-tuple-element.55), channel_id=1, source_target_pairs={{0,9},{1,10},{2,11},{3,8},{4,13},{5,14},{6,15},{7,12},{8,17},{9,18... | collective-permute-start | bytes 1597448 | tf_op jit(solution)/shard_map/ppermute | solution.py:379
  15.3 1.0 copy-start
  32.5 5.9 %collective-permute-start.3 = (f32[520,128]{1,0:T(8,128)S(1)}, f32[520,128]{1,0:T(8,128)S(1)}, u32[]{:S(2)}, u32[]{:S(2)}) collective-permute-start(f32[520,128]{1,0:T(8,128)S(1)} %get-tuple-element.59), channel_id=1, source_target_pairs={{0,124},{1,125},{2,126},{3,127},{4,0},{5,1},{6,2},{7,3},{8,4},{9,5... | collective-permute-start | bytes 798728 | tf_op jit(solution)/shard_map/ppermute | solution.py:379
  32.6 7.1 %collective-permute-start.4 = (f32[520,128]{1,0:T(8,128)S(1)}, f32[520,128]{1,0:T(8,128)S(1)}, u32[]{:S(2)}, u32[]{:S(2)}) collective-permute-start(f32[520,128]{1,0:T(8,128)S(1)} %get-tuple-element.61), channel_id=1, source_target_pairs={{0,4},{1,5},{2,6},{3,7},{4,8},{5,9},{6,10},{7,11},{8,12},{9,13},{1... | collective-permute-start | bytes 798728 | tf_op jit(solution)/shard_map/ppermute | solution.py:379
  45.8 18.0 %collective-permute-start.5 = (f32[1024,128]{1,0:T(8,128)S(1)}, f32[1024,128]{1,0:T(8,128)S(1)}, u32[]{:S(2)}, u32[]{:S(2)}) collective-permute-start(f32[1024,128]{1,0:T(8,128)S(1)} %get-tuple-element.72), channel_id=1, source_target_pairs={{0,9},{1,10},{2,11},{3,8},{4,13},{5,14},{6,15},{7,12},{8,17},{9,18... | collective-permute-start | bytes 1572872 | tf_op jit(solution)/shard_map/ppermute | solution.py:379
  45.8 17.9 %collective-permute-start.6 = (f32[512,128]{1,0:T(8,128)S(1)}, f32[512,128]{1,0:T(8,128)S(1)}, u32[]{:S(2)}, u32[]{:S(2)}) collective-permute-start(f32[512,128]{1,0:T(8,128)S(1)} %get-tuple-element.73), channel_id=1, source_target_pairs={{0,4},{1,5},{2,6},{3,7},{4,8},{5,9},{6,10},{7,11},{8,12},{9,13},{1... | collective-permute-start | bytes 786440 | tf_op jit(solution)/shard_map/ppermute | solution.py:379
  47.3 16.4 %collective-permute-start.7 = (f32[512,128]{1,0:T(8,128)S(1)}, f32[512,128]{1,0:T(8,128)S(1)}, u32[]{:S(2)}, u32[]{:S(2)}) collective-permute-start(f32[512,128]{1,0:T(8,128)S(1)} %get-tuple-element.75), channel_id=1, source_target_pairs={{0,124},{1,125},{2,126},{3,127},{4,0},{5,1},{6,2},{7,3},{8,4},{9,5... | collective-permute-start | bytes 786440 | tf_op jit(solution)/shard_map/ppermute | solution.py:379
  54.1 9.6 %collective-permute-start.8 = (f32[512,128]{1,0:T(8,128)S(1)}, f32[512,128]{1,0:T(8,128)S(1)}, u32[]{:S(2)}, u32[]{:S(2)}) collective-permute-start(f32[512,128]{1,0:T(8,128)S(1)} %get-tuple-element.78), channel_id=1, source_target_pairs={{0,3},{1,0},{2,1},{3,2},{4,7},{5,4},{6,5},{7,6},{8,11},{9,8},{10,9... | collective-permute-start | bytes 786440 | tf_op jit(solution)/shard_map/ppermute | solution.py:379
  55.7 8.1 %collective-permute-start.9 = (f32[176,128]{1,0:T(8,128)S(1)}, f32[176,128]{1,0:T(8,128)S(1)}, u32[]{:S(2)}, u32[]{:S(2)}) collective-permute-start(f32[176,128]{1,0:T(8,128)S(1)} %get-tuple-element.79), channel_id=1, source_target_pairs={{4,0},{8,4},{12,8},{16,12},{20,16},{24,20},{28,24},{32,28},{36,32}... | collective-permute-start | bytes 270344 | tf_op jit(solution)/shard_map/ppermute | solution.py:385
  64.5 19.0 %collective-permute-start.13 = (f32[1024,128]{1,0:T(8,128)S(1)}, f32[1024,128]{1,0:T(8,128)S(1)}, u32[]{:S(2)}, u32[]{:S(2)}) collective-permute-start(f32[1024,128]{1,0:T(8,128)S(1)} %get-tuple-element.84), channel_id=1, source_target_pairs={{0,123},{1,120},{2,121},{3,122},{4,127},{5,124},{6,125},{7,126},{8... | collective-permute-start | bytes 1572872 | tf_op jit(solution)/shard_map/ppermute | solution.py:379
  69.9 8.8 %collective-permute-start.10 = (f32[512,128]{1,0:T(8,128)S(1)}, f32[512,128]{1,0:T(8,128)S(1)}, u32[]{:S(2)}, u32[]{:S(2)}) collective-permute-start(f32[512,128]{1,0:T(8,128)S(1)} %get-tuple-element.80), channel_id=1, source_target_pairs={{0,1},{1,2},{2,3},{3,0},{4,5},{5,6},{6,7},{7,4},{8,9},{9,10},{10,1... | collective-permute-start | bytes 786440 | tf_op jit(solution)/shard_map/ppermute | solution.py:379
  69.9 13.6 %collective-permute-start.11 = (f32[512,128]{1,0:T(8,128)S(1)}, f32[512,128]{1,0:T(8,128)S(1)}, u32[]{:S(2)}, u32[]{:S(2)}) collective-permute-start(f32[512,128]{1,0:T(8,128)S(1)} %get-tuple-element.81), channel_id=1, source_target_pairs={{0,124},{1,125},{2,126},{3,127},{4,0},{5,1},{6,2},{7,3},{8,4},{9,5... | collective-permute-start | bytes 786440 | tf_op jit(solution)/shard_map/ppermute | solution.py:379
  72.8 10.7 %collective-permute-start.12 = (f32[512,128]{1,0:T(8,128)S(1)}, f32[512,128]{1,0:T(8,128)S(1)}, u32[]{:S(2)}, u32[]{:S(2)}) collective-permute-start(f32[512,128]{1,0:T(8,128)S(1)} %get-tuple-element.83), channel_id=1, source_target_pairs={{0,4},{1,5},{2,6},{3,7},{4,8},{5,9},{6,10},{7,11},{8,12},{9,13},{1... | collective-permute-start | bytes 786440 | tf_op jit(solution)/shard_map/ppermute | solution.py:379
  74.4 4.3 %collective-permute-start.14 = (f32[176,128]{1,0:T(8,128)S(1)}, f32[176,128]{1,0:T(8,128)S(1)}, u32[]{:S(2)}, u32[]{:S(2)}) collective-permute-start(f32[176,128]{1,0:T(8,128)S(1)} %get-tuple-element.85), channel_id=1, source_target_pairs={{0,4},{4,8},{8,12},{12,16},{16,20},{20,24},{24,28},{28,32},{32,36}... | collective-permute-start | bytes 270344 | tf_op jit(solution)/shard_map/ppermute | solution.py:385
  91.5 3.4 %collective-permute-start.16 = (f32[512,128]{1,0:T(8,128)S(1)}, f32[512,128]{1,0:T(8,128)S(1)}, u32[]{:S(2)}, u32[]{:S(2)}) collective-permute-start(f32[512,128]{1,0:T(8,128)S(1)} %get-tuple-element.90), channel_id=1, source_target_pairs={{0,4},{1,5},{2,6},{3,7},{4,8},{5,9},{6,10},{7,11},{8,12},{9,13},{1... | collective-permute-start | bytes 786440 | tf_op jit(solution)/shard_map/ppermute | solution.py:379
  91.6 5.9 %collective-permute-start.17 = (f32[512,128]{1,0:T(8,128)S(1)}, f32[512,128]{1,0:T(8,128)S(1)}, u32[]{:S(2)}, u32[]{:S(2)}) collective-permute-start(f32[512,128]{1,0:T(8,128)S(1)} %get-tuple-element.92), channel_id=1, source_target_pairs={{0,124},{1,125},{2,126},{3,127},{4,0},{5,1},{6,2},{7,3},{8,4},{9,5... | collective-permute-start | bytes 786440 | tf_op jit(solution)/shard_map/ppermute | solution.py:379
  93.0 16.8 %collective-permute-start.22 = (f32[8,128]{1,0:T(8,128)S(1)}, f32[8,128]{1,0:T(8,128)S(1)}, u32[]{:S(2)}, u32[]{:S(2)}) collective-permute-start(f32[8,128]{1,0:T(8,128)S(1)} %get-tuple-element.97), channel_id=1, source_target_pairs={{0,3},{1,0},{2,1},{3,2},{4,7},{5,4},{6,5},{7,6},{8,11},{9,8},{10,9... | collective-permute-start | bytes 12296 | tf_op jit(solution)/shard_map/ppermute | solution.py:379
  94.1 15.7 %collective-permute-start.21 = (f32[8,128]{1,0:T(8,128)S(1)}, f32[8,128]{1,0:T(8,128)S(1)}, u32[]{:S(2)}, u32[]{:S(2)}) collective-permute-start(f32[8,128]{1,0:T(8,128)S(1)} %get-tuple-element.97), channel_id=1, source_target_pairs={{0,2},{1,3},{2,0},{3,1},{4,6},{5,7},{6,4},{7,5},{8,10},{9,11},{10,... | collective-permute-start | bytes 12296 | tf_op jit(solution)/shard_map/ppermute | solution.py:379
  94.8 15.1 %collective-permute-start.20 = (f32[8,128]{1,0:T(8,128)S(1)}, f32[8,128]{1,0:T(8,128)S(1)}, u32[]{:S(2)}, u32[]{:S(2)}) collective-permute-start(f32[8,128]{1,0:T(8,128)S(1)} %get-tuple-element.97), channel_id=1, source_target_pairs={{0,1},{1,2},{2,3},{3,0},{4,5},{5,6},{6,7},{7,4},{8,9},{9,10},{10,1... | collective-permute-start | bytes 12296 | tf_op jit(solution)/shard_map/ppermute | solution.py:379
  98.1 29.2 %collective-permute-start.18 = (f32[1024,128]{1,0:T(8,128)S(1)}, f32[1024,128]{1,0:T(8,128)S(1)}, u32[]{:S(2)}, u32[]{:S(2)}) collective-permute-start(f32[1024,128]{1,0:T(8,128)S(1)} %collect.1), channel_id=1, source_target_pairs={{0,123},{1,120},{2,121},{3,122},{4,127},{5,124},{6,125},{7,126},{8... | collective-permute-start | bytes 1572872 | tf_op jit(solution)/shard_map/ppermute | solution.py:379
  109.8 8.8 %collective-permute-start.25 = (f32[8,128]{1,0:T(8,128)S(1)}, f32[8,128]{1,0:T(8,128)S(1)}, u32[]{:S(2)}, u32[]{:S(2)}) collective-permute-start(f32[8,128]{1,0:T(8,128)S(1)} %add_add_fusion.2), channel_id=1, source_target_pairs={{0,96},{4,100},{8,104},{12,108},{16,112},{20,116},{24,120},{28,124... | collective-permute-start | bytes 12296 | tf_op jit(solution)/shard_map/ppermute | solution.py:394
  109.9 8.7 %collective-permute-start.24 = (f32[8,128]{1,0:T(8,128)S(1)}, f32[8,128]{1,0:T(8,128)S(1)}, u32[]{:S(2)}, u32[]{:S(2)}) collective-permute-start(f32[8,128]{1,0:T(8,128)S(1)} %add_add_fusion.2), channel_id=1, source_target_pairs={{0,64},{4,68},{8,72},{12,76},{16,80},{20,84},{24,88},{28,92},{32,9... | collective-permute-start | bytes 12296 | tf_op jit(solution)/shard_map/ppermute | solution.py:394
  110.0 8.6 %collective-permute-start.23 = (f32[8,128]{1,0:T(8,128)S(1)}, f32[8,128]{1,0:T(8,128)S(1)}, u32[]{:S(2)}, u32[]{:S(2)}) collective-permute-start(f32[8,128]{1,0:T(8,128)S(1)} %add_add_fusion.2), channel_id=1, source_target_pairs={{0,32},{4,36},{8,40},{12,44},{16,48},{20,52},{24,56},{28,60},{32,6... | collective-permute-start | bytes 12296 | tf_op jit(solution)/shard_map/ppermute | solution.py:394
  111.4 15.9 %collective-permute-start.15 = (f32[512,128]{1,0:T(8,128)S(1)}, f32[512,128]{1,0:T(8,128)S(1)}, u32[]{:S(2)}, u32[]{:S(2)}) collective-permute-start(f32[512,128]{1,0:T(8,128)S(1)} %get-tuple-element.89), channel_id=1, source_target_pairs={{0,3},{1,0},{2,1},{3,2},{4,7},{5,4},{6,5},{7,6},{8,11},{9,8},{10,9... | collective-permute-start | bytes 786440 | tf_op jit(solution)/shard_map/ppermute | solution.py:379
  118.6 2.8 %collective-permute-start.28 = (f32[8,128]{1,0:T(8,128)S(1)}, f32[8,128]{1,0:T(8,128)S(1)}, u32[]{:S(2)}, u32[]{:S(2)}) collective-permute-start(f32[8,128]{1,0:T(8,128)S(1)} %add_add_fusion.1), channel_id=1, source_target_pairs={{0,24},{4,28},{8,0},{12,4},{16,8},{20,12},{24,16},{28,20},{32,56},... | collective-permute-start | bytes 12296 | tf_op jit(solution)/shard_map/ppermute | solution.py:394
  118.7 4.7 %collective-permute-start.27 = (f32[8,128]{1,0:T(8,128)S(1)}, f32[8,128]{1,0:T(8,128)S(1)}, u32[]{:S(2)}, u32[]{:S(2)}) collective-permute-start(f32[8,128]{1,0:T(8,128)S(1)} %add_add_fusion.1), channel_id=1, source_target_pairs={{0,16},{4,20},{8,24},{12,28},{16,0},{20,4},{24,8},{28,12},{32,48},... | collective-permute-start | bytes 12296 | tf_op jit(solution)/shard_map/ppermute | solution.py:394
  118.8 4.7 %collective-permute-start.26 = (f32[8,128]{1,0:T(8,128)S(1)}, f32[8,128]{1,0:T(8,128)S(1)}, u32[]{:S(2)}, u32[]{:S(2)}) collective-permute-start(f32[8,128]{1,0:T(8,128)S(1)} %add_add_fusion.1), channel_id=1, source_target_pairs={{0,8},{4,12},{8,16},{12,20},{16,24},{20,28},{24,0},{28,4},{32,40},... | collective-permute-start | bytes 12296 | tf_op jit(solution)/shard_map/ppermute | solution.py:394
  121.5 5.8 %collective-permute-start.19 = (f32[176,128]{1,0:T(8,128)S(1)}, f32[176,128]{1,0:T(8,128)S(1)}, u32[]{:S(2)}, u32[]{:S(2)}) collective-permute-start(f32[176,128]{1,0:T(8,128)S(1)} %get-tuple-element.93), channel_id=1, source_target_pairs={{4,0},{8,4},{12,8},{16,12},{20,16},{24,20},{28,24},{32,28},{36,32}... | collective-permute-start | bytes 270344 | tf_op jit(solution)/shard_map/ppermute | solution.py:385
  123.6 1.2 collective-permute-start.29

commit v3 on v2

v3 whole, which is shorter than its diff:
```python
import jax
import jax.numpy as jnp
from jax import lax
from jax.experimental import pallas as pl
from jax.experimental.pallas import tpu as pltpu
from jax.sharding import PartitionSpec as P

W = 4
CAP = 8
SLOTS = W * CAP
SEG = 16
SD = 64
LC = 128
G = 176
NS = 2400
CR = SEG * SD
MASTER = G + CR
RIGHT = G + 2 * CR
KP = 2560
K_LOW, K_WIDE = 1152, 1152
K_LEFT = 256
K_NEAR = 1280
K_RIGHT = 2176
K_PAD = 256
HOP = 1
BACK_HOP = 1
TILE = 480
TILES = NS // TILE
PIECE = 240
PIECES = NS // PIECE
DEPTH = 4
NEAR = CAP * SD
FAR = SEG * SD
NSUB = 32
MIB = 1 << 20

f32 = jnp.float32
bf16 = jnp.bfloat16
highest = lax.Precision.HIGHEST
VM = pl.BlockSpec(memory_space=pltpu.VMEM)
SM = pl.BlockSpec(memory_space=pltpu.SMEM)
ANY = pl.BlockSpec(memory_space=pl.ANY)


def rows(start, size):
    return pl.ds(pl.multiple_of(start, 8), size)


def halves(value):
    high = value.astype(bf16)
    low = (value - high.astype(f32)).astype(bf16)
    return high, low


def product(high, low, both):
    first = jnp.dot(high, both, preferred_element_type=f32)
    second = jnp.dot(low, both, preferred_element_type=f32)
    return (first[:, LC:] + second[:, LC:]) + second[:, :LC] + first[:, :LC]


def segment(index):
    return pl.ds(pl.multiple_of(index * SD, SD), SD)


def flag(condition):
    return jnp.where(condition, 1.0, 0.0).astype(f32)


def put_slots(ref, source, slots, pc, act_wide, slot, position):
    lane = lax.broadcasted_iota(jnp.int32, (1, 128), 1)
    for n in range(slots):
        k = source[n]
        at = jnp.maximum(k, 0)
        used = flag(k >= 0)
        ref[n * SD : (n + 1) * SD, :] = pc[segment(at), :] * used
        tag = (slot[at] + 1).astype(f32)
        seat = position[at].astype(f32)
        row = jnp.where(lane == SD, tag, jnp.where(lane == SD + 1, seat, act_wide[pl.ds(at, 1), :]))
        ref[slots * SD + n : slots * SD + n + 1, :] = used * row


def pack_kernel(
    me, owner_any, slot_any, act_any, rhs_any, glue_any,
    far, pc, mask, pg, act_wide, near_source, far_source, place, position, slot,
    owner, act, rhs, count, sems,
):
    pairs = ((owner_any, owner), (slot_any, slot), (act_any, act), (rhs_any, rhs), (glue_any, pg))
    copies = [pltpu.make_async_copy(src, dst, sems.at[i]) for i, (src, dst) in enumerate(pairs)]
    for copy in copies:
        copy.start()
    for i in range(SEG):
        far_source[i] = -1
    for n in range(CAP):
        near_source[n] = -1
    for o in range(W + 1):
        count[o] = 0
    copies[0].wait()
    for k in range(SEG):
        o = lax.rem(owner[k] - me[0] + NSUB, NSUB)
        n = count[o]
        q = count[W]
        count[o] = n + 1
        position[k] = o * CAP + n

        @pl.when(o == 0)
        def _():
            near_source[n] = k
            place[k] = n

        @pl.when(o > 0)
        def _():
            far_source[q] = k
            place[k] = CAP + q
            count[W] = q + 1

    for copy in copies[1:]:
        copy.wait()
    active = act[...].astype(f32)
    act_wide[...] = jnp.concatenate([active, jnp.zeros((SEG, 128 - SD), f32)], axis=1)
    columns = jnp.transpose(jnp.concatenate([act_wide[...], jnp.zeros((128 - SEG, 128), f32)], axis=0))
    for k in range(SEG):
        wide = jnp.broadcast_to(columns[:SD, k : k + 1], (SD, LC))
        here = slice(k * SD, (k + 1) * SD)
        mask[here, :] = wide
        pc[here, :] = rhs[here, :] * wide
    put_slots(far, far_source, SEG, pc, act_wide, slot, position)


def read_route(info, first, route, inverse):
    for i in range(SLOTS):
        inverse[i] = -1
    for q in range(SEG):
        seat = info[first + q, SD + 1].astype(jnp.int32)
        if route is not None:
            route[q] = seat

        @pl.when(seat > 0)
        def _():
            inverse[seat] = q


def spread(source, inverse, outs, info):
    for o in range(1, W):
        for n in range(CAP):
            q = inverse[o * CAP + n]
            at = jnp.maximum(q, 0)
            used = flag(q >= 0)
            outs[o - 1][n * SD : (n + 1) * SD, :] = source[segment(at), :] * used
            if info:
                outs[o - 1][NEAR + n : NEAR + n + 1, :] = source[pl.ds(FAR + at, 1), :] * used


def collect(route, replies, out):
    for q in range(SEG):
        o, n = lax.div(route[q], CAP), lax.rem(route[q], CAP)
        value = replies[1][segment(n), :]
        for w in (0, 2):
            value = jnp.where(o == w + 1, replies[w][segment(n), :], value)
        out[q * SD : (q + 1) * SD, :] = value


def fetch(place, near, far, k):
    seat = place[k]
    here = near[segment(jnp.minimum(seat, CAP - 1)), :]
    there = far[segment(jnp.maximum(seat - CAP, 0)), :]
    return jnp.where(seat < CAP, here, there)


def relay_kernel(far, pg, token, out1, out2, out3, inverse, info, sem):
    copy = pltpu.make_async_copy(far.at[pl.ds(FAR, SEG), :], info, sem)
    copy.start()
    copy.wait()
    outs = (out1, out2, out3)
    read_route(info, 0, None, inverse)
    spread(far, inverse, outs, True)
    out1[NEAR + CAP : NEAR + CAP + SEG, :] = far[FAR:, :]
    outs[HOP][NEAR + CAP :, :] = pg[...]


def exchange_kernel(
    route, inverse, near_source, far, r1, r2, r3, u, mask, token,
    f1, f2, f3, back, near,
):
    spread(far, inverse, (f1, f2, f3), False)
    f2[NEAR:, :] = u[RIGHT:, :]
    collect(route, (r1, r2, r3), back)
    for n in range(CAP):
        k = near_source[n]
        at = jnp.maximum(k, 0)
        near[n * SD : (n + 1) * SD, :] = u[rows(G + at * SD, SD), :] * mask[segment(at), :] * flag(k >= 0)


def select_kernel(near, u, token, s0, s1, s2, s3, info, sem):
    copy = pltpu.make_async_copy(near.at[pl.ds(CR, 8), :], info, sem)
    copy.start()
    copy.wait()
    for o, out in enumerate((s0, s1, s2, s3)):
        for n in range(CAP):
            j = info[0, o * CAP + n].astype(jnp.int32)
            out[n * SD : (n + 1) * SD, :] = near[segment(j), :]
    s2[NEAR:, :] = u[:G, :]


def split_kernel(
    near_source, position, slot, c_any, pc, pg, mortar, act_wide,
    high, low, partial, forth, back, near, both, tiles, sems,
):
    def fetch(i):
        return pltpu.make_async_copy(
            c_any.at[pl.ds(i * PIECE, PIECE), :], tiles.at[i % DEPTH], sems.at[i % DEPTH]
        )

    for i in range(DEPTH - 1):
        fetch(i).start()
    put_slots(near, near_source, CAP, pc, act_wide, slot, position)
    both[...] = jnp.zeros_like(both)
    for start, size, ref in ((G, CR, pc), (RIGHT, G, pg)):
        part_high, part_low = halves(ref[...])
        both[start : start + size, :LC] = part_high
        both[start : start + size, LC:] = part_low
    for j in range(SEG):
        block = mortar[j * SD : (j + 1) * SD, :]
        for ref, value in ((forth, -jnp.transpose(block)), (back, block)):
            part_high, part_low = halves(value)
            ref[2 * j * SD : (2 * j + 1) * SD, :] = part_high
            ref[(2 * j + 1) * SD : (2 * j + 2) * SD, :] = part_low
    for i in range(PIECES):
        if i + DEPTH - 1 < PIECES:
            fetch(i + DEPTH - 1).start()
        fetch(i).wait()
        at = slice(i * PIECE, (i + 1) * PIECE)
        part_high, part_low = halves(tiles[i % DEPTH])
        pad = jnp.zeros((PIECE, KP - NS), bf16)
        high[at, :NS] = part_high
        high[at, NS:] = pad
        low[at, :NS] = part_low
        low[at, NS:] = pad
        partial[at, :] = product(high[at, :], low[at, :], both[...])


def mortar_apply(mortar, j, value):
    part_high, part_low = halves(value)
    wide = jnp.concatenate([part_high, part_low], axis=1)
    parts = jnp.dot(mortar[2 * j * SD : (2 * j + 2) * SD, :], wide, preferred_element_type=f32)
    return (parts[SD:, LC:] + parts[SD:, :LC]) + parts[:SD, LC:] + parts[:SD, :LC]


def column_sum(value):
    return jnp.sum(value, axis=0, keepdims=True)


def first_kernel(
    me, in0, in1, in2, in3, forth, back, pc, pg, partial, mask, source, high, low,
    far, p0, p1, p2, p3, u, projected, actives, slots, route, inverse, sums,
    gathered, term, both, info, info_sems,
):
    ins = (in0, in1, in2, in3)
    infos = []
    for o in range(W):
        copy = pltpu.make_async_copy(ins[o].at[pl.ds(NEAR, 8), :], info.at[pl.ds(o * 8, 8), :], info_sems.at[o])
        copy.start()
        infos.append(copy)
    gathered[...] = jnp.zeros_like(gathered)
    actives[...] = jnp.zeros_like(actives)
    both[...] = jnp.zeros_like(both)
    left = -ins[HOP + 1][NEAR + CAP :, :] * flag(me[0] > 0)
    part_high, part_low = halves(left)
    both[:G, :LC] = part_high
    both[:G, LC:] = part_low
    copy = pltpu.make_async_copy(
        in1.at[pl.ds(NEAR + CAP, SEG), :], info.at[pl.ds(W * 8, SEG), :], info_sems.at[W]
    )
    copy.start()
    infos.append(copy)
    for copy in infos:
        copy.wait()
    read_route(info, W * 8, route, inverse)
    for o in range(W):
        tile = jnp.concatenate([ins[o][NEAR : NEAR + 8, :], jnp.zeros((120, 128), f32)], axis=0)
        columns = jnp.transpose(tile)
        for n in range(CAP):
            j = info[o * 8 + n, SD].astype(jnp.int32) - 1
            slots[o * CAP + n] = j
            at = rows(jnp.maximum(j, 0) * SD, SD)
            gathered[at, :] += ins[o][n * SD : (n + 1) * SD, :]
            actives[at, :] += jnp.broadcast_to(columns[:SD, n : n + 1], (SD, LC))
    for j in range(SEG):
        value = mortar_apply(forth, j, gathered[j * SD : (j + 1) * SD, :])
        term[j * SD : (j + 1) * SD, :] = value
        part_high, part_low = halves(value)
        start = K_LEFT + MASTER - K_LOW + j * SD
        both[start : start + SD, :LC] = part_high
        both[start : start + SD, LC:] = part_low
    for i in range(TILES):
        at = slice(i * TILE, (i + 1) * TILE)
        wide = slice(K_LOW, K_LOW + K_WIDE)
        u[at, :] = (
            partial[at, :]
            + product(high[at, :K_LEFT], low[at, :K_LEFT], both[:K_LEFT, :])
            + product(high[at, wide], low[at, wide], both[K_LEFT:, :])
        )
    p2[NEAR:, :] = u[:G, :]
    for j in range(SEG):
        start = MASTER + j * SD
        projected[j * SD : (j + 1) * SD, :] = mortar_apply(back, j, u[start : start + SD, :])
    for q in range(SEG):
        k = source[q]
        at = jnp.maximum(k, 0)
        far[q * SD : (q + 1) * SD, :] = u[rows(G + at * SD, SD), :] * mask[segment(at), :] * flag(k >= 0)
    for o, reply in enumerate((p0, p1, p2, p3)):
        for n in range(CAP):
            j = jnp.maximum(slots[o * CAP + n], 0)
            reply[n * SD : (n + 1) * SD, :] = projected[segment(j), :]
    norm = column_sum(pg[...] * pg[...]) + column_sum(pc[...] * pc[...])
    curvature = (
        column_sum(pg[...] * u[RIGHT:, :])
        + column_sum(left * u[:G, :])
        + column_sum(pc[...] * u[G:MASTER, :])
        + column_sum(term[...] * u[MASTER:RIGHT, :])
    )
    sums[...] = jnp.concatenate([norm, curvature, jnp.zeros((6, LC), f32)], axis=0)


def master_kernel(
    slots, f0, f1, f2, f3, projected0, actives, forth, high, low, partial, term, gathered, both
):
    gathered[...] = -(actives[...] * projected0[...])
    for o, source in enumerate((f0, f1, f2, f3)):
        for n in range(CAP):
            at = segment(jnp.maximum(slots[o * CAP + n], 0))
            gathered[at, :] += source[n * SD : (n + 1) * SD, :]
    both[...] = jnp.zeros_like(both)
    for j in range(SEG):
        value = mortar_apply(forth, j, gathered[j * SD : (j + 1) * SD, :])
        term[j * SD : (j + 1) * SD, :] = value
        part_high, part_low = halves(value)
        start = MASTER - K_LOW + j * SD
        both[start : start + SD, :LC] = part_high
        both[start : start + SD, LC:] = part_low
    wide = slice(K_LOW, K_LOW + K_WIDE)
    for i in range(TILES):
        at = slice(i * TILE, (i + 1) * TILE)
        partial[at, :] = product(high[at, wide], low[at, wide], both[...])


def second_kernel(
    me, place, near, far, r2, f2, u0, mask, partial, term, sums0, high, low,
    u, q_glue, q_contact, sums,
    loads, both,
):
    loads[:G, :] = (u0[:G, :] - f2[NEAR:, :]) * flag(me[0] > 0)
    glue = u0[RIGHT:, :] - r2[NEAR:, :] * flag(me[0] < NSUB - 1)
    q_glue[...] = glue
    for k in range(SEG):
        here = slice(k * SD, (k + 1) * SD)
        fetched = fetch(place, near, far, k)
        value = mask[here, :] * (u0[G + k * SD : G + (k + 1) * SD, :] - fetched)
        q_contact[here, :] = value
        loads[G + k * SD : G + (k + 1) * SD, :] = value
    loads[MASTER:K_NEAR, :] = jnp.zeros((K_NEAR - MASTER, LC), f32)
    both[K_NEAR:, :] = jnp.zeros((K_PAD, 2 * LC), bf16)
    start = K_NEAR + RIGHT - K_RIGHT
    for at, value in ((slice(0, K_NEAR), loads[...]), (slice(start, start + G), glue)):
        part_high, part_low = halves(value)
        both[at, :LC] = part_high
        both[at, LC:] = part_low
    tail = slice(K_RIGHT, K_RIGHT + K_PAD)
    for i in range(TILES):
        at = slice(i * TILE, (i + 1) * TILE)
        u[at, :] = (
            partial[at, :]
            + product(high[at, :K_NEAR], low[at, :K_NEAR], both[:K_NEAR, :])
            + product(high[at, tail], low[at, tail], both[K_NEAR:, :])
        )
    square = column_sum(glue * glue) + column_sum(q_contact[...] * q_contact[...])
    energy = (
        column_sum(loads[:MASTER, :] * u[:MASTER, :])
        + column_sum(term[...] * u[MASTER:RIGHT, :])
        + column_sum(glue * u[RIGHT:, :])
    )
    sums[...] = jnp.concatenate([sums0[0:2, :], square, energy, jnp.zeros((4, LC), f32)], axis=0)


def reply_kernel(slots, project, u, sums, out, kept):
    kept[...] = sums[...]
    for j in range(SEG):
        start = MASTER + j * SD
        out[j * SD : (j + 1) * SD, :] = mortar_apply(project, j, u[start : start + SD, :])
    lane = lax.broadcasted_iota(jnp.int32, (8, 128), 1)
    row = jnp.zeros((8, 128), f32)
    for i in range(SLOTS):
        row = jnp.where(lane == i, jnp.maximum(slots[i], 0).astype(f32), row)
    out[CR:, :] = row


def last_kernel(
    me, position, s0, s1, s2, s3, u, q_glue, q_contact, pc, pg, mask, sums,
    mult_glue, mult_contact, res_glue, res_contact,
):
    norm0, curvature0, square, energy = (sums[i : i + 1, :] for i in range(4))
    alpha0 = norm0 / curvature0
    norm1 = (norm0 - alpha0 * curvature0) + alpha0 * (alpha0 * square - curvature0)
    own = (curvature0 - alpha0 * square) + alpha0 * (alpha0 * energy - square)
    cross = curvature0 - alpha0 * square
    ratio = norm1 / norm0
    curvature1 = own + ratio * (2.0 * cross + ratio * curvature0)
    alpha1 = norm1 / curvature1

    def finish(r0, q, w):
        r1 = r0 - alpha0 * q
        direction = r1 + ratio * r0
        image = (q - alpha0 * w) + ratio * q
        return alpha0 * r0 + alpha1 * direction, r1 - alpha1 * image

    mult, res = finish(pg[...], q_glue[...], u[RIGHT:, :] - s2[NEAR:, :] * flag(me[0] < NSUB - 1))
    mult_glue[...] = mult
    res_glue[...] = res
    for k in range(SEG):
        here = slice(k * SD, (k + 1) * SD)
        o, n = lax.div(position[k], CAP), lax.rem(position[k], CAP)
        fetched = s0[segment(n), :]
        for w, ref in ((1, s1), (2, s2), (3, s3)):
            fetched = jnp.where(o == w, ref[segment(n), :], fetched)
        value = mask[here, :] * (u[G + k * SD : G + (k + 1) * SD, :] - fetched)
        mult, res = finish(pc[here, :], q_contact[here, :], value)
        mult_contact[here, :] = mult
        res_contact[here, :] = res


def shape(*dims, dtype=f32):
    return jax.ShapeDtypeStruct(dims, dtype)


def params(mib):
    return pltpu.CompilerParams(vmem_limit_bytes=mib * MIB)


def sent(value, body_step, sub_step):
    subs, bodies = lax.axis_size("sub"), lax.axis_size("body")
    pairs = [
        (s * bodies + b, ((s + sub_step) % subs) * bodies + (b + body_step) % bodies)
        for s in range(subs)
        for b in range(bodies)
    ]
    return lax.ppermute(value, ("sub", "body"), pairs)


def moved(value, body_step, sub_step):
    return sent(value, body_step, sub_step) if body_step or sub_step else value


def rotated(value, block, stride, steps):
    count = lax.axis_size("sub")
    pairs = []
    for s in range(count):
        place = s // stride % block
        pairs.append((s, s + ((place + steps) % block - place) * stride))
    return lax.ppermute(value, "sub", pairs)


def total(value):
    value = value + sum(rotated(value, 4, 2, k) for k in (1, 2, 3))
    value = value + rotated(value, 2, 1, 1)
    value = value + sum(rotated(value, 4, 8, k) for k in (1, 2, 3))
    token = value
    value = value + sent(value, 1, 0) + sent(value, 2, 0) + sent(value, 3, 0)
    return value, token


def in_hbm(value):
    return pltpu.with_memory_space_constraint(value, pltpu.HBM)


def kept(value):
    return pltpu.with_memory_space_constraint(value, pltpu.VMEM)


def per_device(compliance, mortar, rhs_glue, rhs_contact, owner_sub, master_slot, active_set):
    schur_block = compliance[0, 0]
    blocks = mortar.reshape(CR, SD)
    rhs = rhs_contact.reshape(CR, LC)
    me = lax.axis_index("sub").astype(jnp.int32).reshape(1)
    seg_block = shape(NEAR, LC)
    far_block = shape(FAR, LC)
    info_block = shape(NEAR + CAP, LC)
    face_block = shape(NEAR + G, LC)

    def index(n):
        return shape(n, dtype=jnp.int32)

    far, pc, mask, pg, act_wide, near_source, far_source, place, position, slot = pl.pallas_call(
        pack_kernel,
        out_shape=[shape(FAR + SEG, LC), shape(CR, LC), shape(CR, LC), shape(G, LC), shape(SEG, 128)]
        + [index(n) for n in (CAP, SEG, SEG, SEG, SEG)],
        in_specs=[SM] + [ANY] * 5,
        out_specs=[VM] * 5 + [SM] * 5,
        scratch_shapes=[
            pltpu.SMEM((SEG,), jnp.int32),
            pltpu.VMEM((SEG, SD), jnp.int32),
            pltpu.VMEM((CR, LC), f32),
            pltpu.SMEM((W + 1,), jnp.int32),
            pltpu.SemaphoreType.DMA((5,)),
        ],
        compiler_params=params(8),
        name="pack",
    )(me, *(in_hbm(v) for v in (
        owner_sub.reshape(SEG), master_slot.reshape(SEG), active_set.reshape(SEG, SD), rhs, rhs_glue[0, 0],
    )))

    far_in = sent(far, 1, HOP)

    stacked = shape(2 * CR, SD, dtype=bf16)
    high, low, partial, forth, project, near = pl.pallas_call(
        split_kernel,
        out_shape=[pltpu.VMEM((NS, KP), bf16)] * 2 + [shape(NS, LC), stacked, stacked, info_block],
        in_specs=[SM] * 3 + [ANY] + [VM] * 4,
        out_specs=[VM] * 6,
        scratch_shapes=[
            pltpu.VMEM((KP, 2 * LC), bf16),
            pltpu.VMEM((DEPTH, PIECE, NS), f32),
            pltpu.SemaphoreType.DMA((DEPTH,)),
        ],
        compiler_params=params(20),
        cost_estimate=pl.CostEstimate(
            flops=8 * NS * KP * LC, bytes_accessed=4 * NS * NS, transcendentals=0
        ),
        name="split",
    )(near_source, position, slot, in_hbm(schur_block), pc, pg, blocks, act_wide)
    high, low = kept(high), kept(low)
    near_in = sent(near, 1, 0)

    relayed = [shape(NEAR + CAP + extra, LC) for extra in ((SEG, 0, G) if HOP == 2 else (SEG, G, 0))]
    outgoing = pl.pallas_call(
        relay_kernel,
        out_shape=relayed + [index(SLOTS)],
        in_specs=[VM, VM, ANY],
        out_specs=[VM] * 3 + [SM],
        scratch_shapes=[pltpu.SMEM((SEG, 128), f32), pltpu.SemaphoreType.DMA],
        compiler_params=params(6),
        name="relay",
    )(far_in, pg, partial)
    incoming = [near_in] + [moved(outgoing[o - 1], 0, o - HOP) for o in range(1, W)]

    outs = pl.pallas_call(
        first_kernel,
        out_shape=[far_block, seg_block, seg_block, face_block, seg_block]
        + [shape(NS, LC), shape(CR, LC), shape(CR, LC)]
        + [index(SLOTS), index(SEG), index(SLOTS), shape(8, LC)],
        in_specs=[SM] + [VM] * 10 + [SM, VM, VM],
        out_specs=[VM] * 8 + [SM] * 3 + [VM],
        scratch_shapes=[
            pltpu.VMEM((CR, LC), f32),
            pltpu.VMEM((CR, LC), f32),
            pltpu.VMEM((K_LEFT + K_WIDE, 2 * LC), bf16),
            pltpu.SMEM((W * 8 + SEG, 128), f32),
            pltpu.SemaphoreType.DMA((W + 1,)),
        ],
        compiler_params=params(12),
        name="first",
    )(me, *incoming, forth, project, pc, pg, partial, mask, far_source, high, low)
    far, replies = outs[0], outs[1:5]
    u0, projected0, actives, slots, route, inverse, sums0 = outs[5:]

    far_in = sent(far, 1, BACK_HOP)
    replies = [sent(replies[0], -1, 0)] + [moved(replies[o], 0, BACK_HOP - o) for o in range(1, W)]
    near_back, next_left = replies[0], replies[2]

    *outgoing, far, near = pl.pallas_call(
        exchange_kernel,
        out_shape=[seg_block, face_block, seg_block, far_block, seg_block],
        in_specs=[SM] * 3 + [VM] * 6 + [ANY],
        out_specs=[VM] * 5,
        compiler_params=params(12),
        name="exchange",
    )(route, inverse, near_source, far_in, *replies[1:], u0, mask, near_back)
    far_back = sent(far, -1, -BACK_HOP)
    incoming = [sent(near, 1, 0)] + [moved(outgoing[o - 1], 0, o - BACK_HOP) for o in range(1, W)]

    partial, term = pl.pallas_call(
        master_kernel,
        out_shape=[shape(NS, LC), shape(CR, LC)],
        in_specs=[SM] + [VM] * 9,
        out_specs=[VM] * 2,
        scratch_shapes=[pltpu.VMEM((CR, LC), f32), pltpu.VMEM((K_WIDE, 2 * LC), bf16)],
        compiler_params=params(12),
        cost_estimate=pl.CostEstimate(flops=8 * NS * K_WIDE * LC, bytes_accessed=MIB, transcendentals=0),
        name="master",
    )(slots, *incoming, projected0, actives, forth, high, low)

    u1, q_glue, q_contact, sums = pl.pallas_call(
        second_kernel,
        out_shape=[shape(NS, LC), shape(G, LC), shape(CR, LC), shape(8, LC)],
        in_specs=[SM] * 2 + [VM] * 11,
        out_specs=[VM] * 4,
        scratch_shapes=[pltpu.VMEM((K_NEAR, LC), f32), pltpu.VMEM((K_NEAR + K_PAD, 2 * LC), bf16)],
        compiler_params=params(12),
        name="second",
    )(me, place, near_back, far_back, next_left, incoming[2], u0, mask, partial, term, sums0, high, low)

    replied, sums = pl.pallas_call(
        reply_kernel,
        out_shape=[shape(CR + 8, LC), shape(8, LC)],
        in_specs=[SM] + [VM] * 3,
        out_specs=[VM] * 2,
        compiler_params=params(8),
        cost_estimate=pl.CostEstimate(flops=0, bytes_accessed=8 * MIB, transcendentals=0),
        name="reply",
    )(slots, project, u1, sums)
    replied = sent(replied, -1, -1)
    sums, token = total(sums)

    *outgoing, = pl.pallas_call(
        select_kernel,
        out_shape=[seg_block, seg_block, face_block, seg_block],
        in_specs=[VM] * 2 + [ANY],
        out_specs=[VM] * 4,
        scratch_shapes=[pltpu.SMEM((8, 128), f32), pltpu.SemaphoreType.DMA],
        compiler_params=params(6),
        name="select",
    )(replied, u1, token)
    fetched = [moved(outgoing[o], 0, 1 - o) for o in range(W)]

    mult_glue, mult_contact, res_glue, res_contact = pl.pallas_call(
        last_kernel,
        out_shape=[shape(G, LC), shape(CR, LC)] * 2,
        in_specs=[SM] * 2 + [VM] * 11,
        out_specs=[VM] * 4,
        compiler_params=params(24),
        name="last",
    )(me, position, *fetched, u1, q_glue, q_contact, pc, pg, mask, sums)
    contact = (1, 1, SEG, SD, LC)
    return (
        mult_glue[None, None],
        mult_contact.reshape(contact),
        res_glue[None, None],
        res_contact.reshape(contact),
    )


def solution(mesh):
    in_specs = (
        P("body", "sub", None, None),
        P("body", "sub", None, None, None),
        P("body", "sub", None, None),
        P("body", "sub", None, None, None),
        P("body", "sub", None, None),
        P("body", "sub", None),
        P("body", "sub", None, None),
    )
    out_specs = (
        P("body", "sub", None, None),
        P("body", "sub", None, None, None),
        P("body", "sub", None, None),
        P("body", "sub", None, None, None),
    )
    return jax.shard_map(
        per_device, mesh=mesh, in_specs=in_specs, out_specs=out_specs, check_vma=False
    )
```

time: 130 us -> 118 us (0.908)
  starting transfers between devices: 60.2 us -> 36.1 us
  waiting for transfers between devices: 32.8 us -> 46 us
  Pallas kernels: 30.3 us -> 34.3 us
  local copies, waits for them, and re-layouts: 4.97 us -> 1.04 us
    ppermute x19, waiting for transfers between devices: 17.8 us -> 38.4 us  [sent(): return lax.ppermute(value, ('sub', 'body'), pairs)]
    ppermute x4 -> x0, starting transfers between devices: 16.6 us -> none  [passed_along(): lax.ppermute(value, 'sub', [(source, source + steps) for source in range(...]
    ppermute x19, starting transfers between devices: 40.5 us -> 27.9 us  [sent(): return lax.ppermute(value, ('sub', 'body'), pairs)]
    ppermute x7, starting transfers between devices: 3.05 us -> 8.25 us  [rotated(): return lax.ppermute(value, 'sub', pairs)]
    ppermute x4 -> x0, waiting for transfers between devices: 5.12 us -> none  [passed_along(): lax.ppermute(value, 'sub', [(source, source + steps) for source in range(...]
    unnamed x12 -> x2, local copies, waits for them, and re-layouts: 4.97 us -> 1.04 us
    pallas_call x6 -> x8, Pallas kernels: 18.6 us -> 22 us  [the longest x1 7.13 us: per_device(): pl.pallas_call(first_kernel, out_shape=[far_block, seg_block, seg_block,...]
    ppermute x7, waiting for transfers between devices: 9.88 us -> 7.59 us  [rotated(): return lax.ppermute(value, 'sub', pairs)]
  transfers between devices with their start and end apart: 30 -> 26, of which waited for: 13 -> 17; matrix products, arithmetic and copies ran while one was open for 0% -> 0% of each run, Pallas kernels for 9% -> 13%
where the time goes in v3:
time: 118 us
  waiting for transfers between devices  46 us (39%)
  starting transfers between devices  36.1 us (31%)
  Pallas kernels  34.3 us (29%)
    ppermute x19, waiting for transfers between devices, sent(): return lax.ppermute(value, ('sub', 'body'), pairs)  38.4 us
    ppermute x19, starting transfers between devices, sent(): return lax.ppermute(value, ('sub', 'body'), pairs)  27.9 us
    pallas_call x1, Pallas kernels, per_device(): pl.pallas_call(split_kernel, out_shape=[pltpu.VMEM((NS, KP), bf16)] * 2 +...  10.4 us
    ppermute x7, starting transfers between devices, rotated(): return lax.ppermute(value, 'sub', pairs)  8.25 us
    ppermute x7, waiting for transfers between devices, rotated(): return lax.ppermute(value, 'sub', pairs)  7.59 us
    pallas_call x1, Pallas kernels, per_device(): pl.pallas_call(first_kernel, out_shape=[far_block, seg_block, seg_block,...  7.13 us
    pallas_call x1, Pallas kernels, per_device(): pl.pallas_call(second_kernel, out_shape=[shape(NS, LC), shape(G, LC), sha...  4.72 us
    pallas_call x1, Pallas kernels, per_device(): pl.pallas_call(master_kernel, out_shape=[shape(NS, LC), shape(CR, LC)], i...  4.42 us
  transfers between devices with their start and end apart: 26, of which 17 were waited for; matrix products, arithmetic and copies ran while one was open for 0% of the time, Pallas kernels for 13%

profile of v3, /device:TPU:1, one launch (start us, length us, event | category | flops | bytes accessed | tf_op | source)
XLA Modules:
  0.0 118.3 jit_solution(18023268115661970635)
XLA Ops:
  0.6 2.0 %pack.1 = (f32[1040,128]{1,0:T(8,128)S(1)}, f32[1024,128]{1,0:T(8,128)S(1)}, f32[1024,128]{1,0:T(8,128)S(1)}, f32[176,128]{1,0:T(8,128)S(1)}, f32[16,128]{1,0:T(...) custom-call(s32[1]{0:T(128)} %bitcast.me, s32[16]{0:T(128)} %bitcast.17, ...), custom_call_target="tpu_custom_call" | custom-call | tf_op jit(solution)/shard_map/pack/pallas_call | solution.py:491
  2.7 4.1 %collective-permute-start.1 = (f32[1040,128]{1,0:T(8,128)S(1)}, f32[1040,128]{1,0:T(8,128)S(1)}, u32[]{:S(2)}, u32[]{:S(2)}) collective-permute-start(f32[1040,128]{1,0:T(8,128)S(1)} %get-tuple-element.63), channel_id=1, source_target_pairs={{0,5},{1,6},{2,7},{3,4},{4,9},{5,10},{6,11},{7,8},{8,13},{9,14},{1... | collective-permute-start | bytes 1597448 | tf_op jit(solution)/shard_map/ppermute | solution.py:445
  6.8 1.0 copy-done
  7.8 10.4 %split.1 = (bf16[2400,2560]{1,0:T(8,128)(2,1)S(1)}, bf16[2400,2560]{1,0:T(8,128)(2,1)S(1)}, f32[2400,128]{1,0:T(8,128)S(1)}, bf16[2048,64]{1,0:T(8,128)(2,1)S(1)...) custom-call(s32[8]{0:T(128)S(1)} %get-tuple-element.57.near_source, s32[16]{0:T(128)S(1)} %get-tuple-element.56.position, ...), custom_call_target="tpu_custom_call" | custom-call | flops 6291456000 | bytes 23040000 | tf_op jit(solution)/shard_map/split/pallas_call | solution.py:513
  18.2 0.6 collective-permute-done.1.far
  18.8 1.3 %relay.1 = (f32[536,128]{1,0:T(8,128)S(1)}, f32[696,128]{1,0:T(8,128)S(1)}, f32[520,128]{1,0:T(8,128)S(1)}, s32[32]{0:T(128)}) custom-call(f32[1040,128]{1,0:T(8,128)S(1)} %collective-permute-done.1.far, f32[176,128]{1,0:T(8,128)S(1)} %get-tuple-element.60.pg, f32[2400,128]{1,0:T(8,128)S(1)} %get-tuple-element.64.token.partial), custom_call_target="tpu_custom_call" | custom-call | tf_op jit(solution)/shard_map/relay/pallas_call | solution.py:533
  20.1 2.5 %collective-permute-start.2 = (f32[696,128]{1,0:T(8,128)S(1)}, f32[696,128]{1,0:T(8,128)S(1)}, u32[]{:S(2)}, u32[]{:S(2)}) collective-permute-start(f32[696,128]{1,0:T(8,128)S(1)} %get-tuple-element.66), channel_id=1, source_target_pairs={{0,4},{1,5},{2,6},{3,7},{4,8},{5,9},{6,10},{7,11},{8,12},{9,13},{1... | collective-permute-start | bytes 1069064 | tf_op jit(solution)/shard_map/ppermute | solution.py:445
  22.6 1.6 %collective-permute-start.3 = (f32[520,128]{1,0:T(8,128)S(1)}, f32[520,128]{1,0:T(8,128)S(1)}, u32[]{:S(2)}, u32[]{:S(2)}) collective-permute-start(f32[520,128]{1,0:T(8,128)S(1)} %get-tuple-element.67), channel_id=1, source_target_pairs={{0,8},{1,9},{2,10},{3,11},{4,12},{5,13},{6,14},{7,15},{8,16},{9,17... | collective-permute-start | bytes 798728 | tf_op jit(solution)/shard_map/ppermute | solution.py:445
  24.3 6.7 %collective-permute-done.in0 = f32[520,128]{1,0:T(8,128)S(1)} collective-permute-done((f32[520,128]{1,0:T(8,128)S(1)}, f32[520,128]{1,0:T(8,128)S(1)}, u32[]{:S(2)}, u32[]{:S(2)}) %collective-permute-start) | collective-permute-done | bytes 266272 | tf_op jit(solution)/shard_map/ppermute | solution.py:445
  31.0 6.1 %collective-permute-done.3.in3 = f32[520,128]{1,0:T(8,128)S(1)} collective-permute-done((f32[520,128]{1,0:T(8,128)S(1)}, f32[520,128]{1,0:T(8,128)S(1)}, u32[]{:S(2)}, u32[]{:S(2)}) %collective-permute-start.3) | collective-permute-done | bytes 266272 | tf_op jit(solution)/shard_map/ppermute | solution.py:445
  37.0 7.1 %first.1 = (f32[1024,128]{1,0:T(8,128)S(1)}, f32[512,128]{1,0:T(8,128)S(1)}, f32[512,128]{1,0:T(8,128)S(1)}, f32[688,128]{1,0:T(8,128)S(1)}, f32[512,128]{1,0:T(...) custom-call(s32[1]{0:T(128)} %bitcast.me, ...), custom_call_target="tpu_custom_call" | custom-call | tf_op jit(solution)/shard_map/first/pallas_call | solution.py:544
  44.2 0.1 collective-permute-start.5
  44.2 0.3 collective-permute-start.6
  44.5 2.8 %collective-permute-start.4 = (f32[512,128]{1,0:T(8,128)S(1)}, f32[512,128]{1,0:T(8,128)S(1)}, u32[]{:S(2)}, u32[]{:S(2)}) collective-permute-start(f32[512,128]{1,0:T(8,128)S(1)} %get-tuple-element.76), channel_id=1, source_target_pairs={{0,3},{1,0},{2,1},{3,2},{4,7},{5,4},{6,5},{7,6},{8,11},{9,8},{10,9... | collective-permute-start | bytes 786440 | tf_op jit(solution)/shard_map/ppermute | solution.py:445
  47.3 2.3 %collective-permute-start.7 = (f32[512,128]{1,0:T(8,128)S(1)}, f32[512,128]{1,0:T(8,128)S(1)}, u32[]{:S(2)}, u32[]{:S(2)}) collective-permute-start(f32[512,128]{1,0:T(8,128)S(1)} %get-tuple-element.82), channel_id=1, source_target_pairs={{0,120},{1,121},{2,122},{3,123},{4,124},{5,125},{6,126},{7,127},{8... | collective-permute-start | bytes 786440 | tf_op jit(solution)/shard_map/ppermute | solution.py:445
  49.6 1.0 collective-permute-done.4.token.near
  50.6 5.1 %collective-permute-done.7.r3 = f32[512,128]{1,0:T(8,128)S(1)} collective-permute-done((f32[512,128]{1,0:T(8,128)S(1)}, f32[512,128]{1,0:T(8,128)S(1)}, u32[]{:S(2)}, u32[]{:S(2)}) %collective-permute-start.7) | collective-permute-done | bytes 262176 | tf_op jit(solution)/shard_map/ppermute | solution.py:445
  55.7 2.0 %collective-permute-done.5.far = f32[1024,128]{1,0:T(8,128)S(1)} collective-permute-done((f32[1024,128]{1,0:T(8,128)S(1)}, f32[1024,128]{1,0:T(8,128)S(1)}, u32[]{:S(2)}, u32[]{:S(2)}) %collective-permute-start.5) | collective-permute-done | bytes 524320 | tf_op jit(solution)/shard_map/ppermute | solution.py:445
  57.7 0.8 exchange.1
  58.5 0.1 collective-permute-start.9
  58.6 1.5 %collective-permute-start.10 = (f32[512,128]{1,0:T(8,128)S(1)}, f32[512,128]{1,0:T(8,128)S(1)}, u32[]{:S(2)}, u32[]{:S(2)}) collective-permute-start(f32[512,128]{1,0:T(8,128)S(1)} %get-tuple-element.86), channel_id=1, source_target_pairs={{0,1},{1,2},{2,3},{3,0},{4,5},{5,6},{6,7},{7,4},{8,9},{9,10},{10,1... | collective-permute-start | bytes 786440 | tf_op jit(solution)/shard_map/ppermute | solution.py:445
  60.1 2.5 %collective-permute-start.8 = (f32[1024,128]{1,0:T(8,128)S(1)}, f32[1024,128]{1,0:T(8,128)S(1)}, u32[]{:S(2)}, u32[]{:S(2)}) collective-permute-start(f32[1024,128]{1,0:T(8,128)S(1)} %get-tuple-element.84), channel_id=1, source_target_pairs={{0,127},{1,124},{2,125},{3,126},{4,3},{5,0},{6,1},{7,2},{8,7},{9,4... | collective-permute-start | bytes 1572872 | tf_op jit(solution)/shard_map/ppermute | solution.py:445
  62.6 4.0 %collective-permute-done.10.f0 = f32[512,128]{1,0:T(8,128)S(1)} collective-permute-done((f32[512,128]{1,0:T(8,128)S(1)}, f32[512,128]{1,0:T(8,128)S(1)}, u32[]{:S(2)}, u32[]{:S(2)}) %collective-permute-start.10) | collective-permute-done | bytes 262176 | tf_op jit(solution)/shard_map/ppermute | solution.py:445
  66.5 8.1 %collective-permute-done.11.f3 = f32[512,128]{1,0:T(8,128)S(1)} collective-permute-done((f32[512,128]{1,0:T(8,128)S(1)}, f32[512,128]{1,0:T(8,128)S(1)}, u32[]{:S(2)}, u32[]{:S(2)}) %collective-permute-start.11) | collective-permute-done | bytes 262176 | tf_op jit(solution)/shard_map/ppermute | solution.py:445
  74.7 4.4 %master.1 = (f32[2400,128]{1,0:T(8,128)S(1)}, f32[1024,128]{1,0:T(8,128)S(1)}) custom-call(s32[32]{0:T(128)S(1)} %get-tuple-element.74.slots, f32[512,128]{1,0:T(8,128)S(1)} %collective-permute-done.10.f0, f32[512,128]{1,0:T(8,128)S(1)} %get-tuple-element.87.f1, f32[688,128]{1,0:T(8,128)S(1)} %collective-permute-done.9.f2, ...), custom_call_target="tpu_custom_call" | custom-call | flops 2831155200 | bytes 1048576 | tf_op jit(solution)/shard_map/master/pallas_call | solution.py:579
  79.1 4.7 %second.1 = (f32[2400,128]{1,0:T(8,128)S(1)}, f32[176,128]{1,0:T(8,128)S(1)}, f32[1024,128]{1,0:T(8,128)S(1)}, f32[8,128]{1,0:T(8,128)S(1)}) custom-call(s32[1]{0:T(128)} %bitcast.me, s32[16]{0:T(128)S(1)} %get-tuple-element.75.place, f32[512,128]{1,0:T(8,128)S(1)} %collective-permute-done.4.token.near, f32[1024,128]{1,0:T(8,128)S(1)} %collective-permute-done.8.far, ...), custom_call_target="tpu_custom_call" | custom-call | tf_op jit(solution)/shard_map/second/pallas_call | solution.py:590
  83.8 1.0 reply.1
  84.8 1.0 collective-permute-start.12
  85.8 1.5 %collective-permute-start.13 = (f32[8,128]{1,0:T(8,128)S(1)}, f32[8,128]{1,0:T(8,128)S(1)}, u32[]{:S(2)}, u32[]{:S(2)}) collective-permute-start(f32[8,128]{1,0:T(8,128)S(1)} %get-tuple-element.97), channel_id=1, source_target_pairs={{0,8},{4,12},{8,16},{12,20},{16,24},{20,28},{24,0},{28,4},{32,40},... | collective-permute-start | bytes 12296 | tf_op jit(solution)/shard_map/ppermute | solution.py:458
  87.3 1.3 %collective-permute-done.15 = f32[8,128]{1,0:T(8,128)S(1)} collective-permute-done((f32[8,128]{1,0:T(8,128)S(1)}, f32[8,128]{1,0:T(8,128)S(1)}, u32[]{:S(2)}, u32[]{:S(2)}) %collective-permute-start.15) | collective-permute-done | bytes 4128 | tf_op jit(solution)/shard_map/ppermute | solution.py:458
  88.6 1.2 %collective-permute-done.14 = f32[8,128]{1,0:T(8,128)S(1)} collective-permute-done((f32[8,128]{1,0:T(8,128)S(1)}, f32[8,128]{1,0:T(8,128)S(1)}, u32[]{:S(2)}, u32[]{:S(2)}) %collective-permute-start.14) | collective-permute-done | bytes 4128 | tf_op jit(solution)/shard_map/ppermute | solution.py:458
  89.8 0.9 collective-permute-done.13
  90.7 4.7 %collective-permute-start.16 = (f32[8,128]{1,0:T(8,128)S(1)}, f32[8,128]{1,0:T(8,128)S(1)}, u32[]{:S(2)}, u32[]{:S(2)}) collective-permute-start(f32[8,128]{1,0:T(8,128)S(1)} %add_add_fusion.2), channel_id=1, source_target_pairs={{0,4},{4,0},{8,12},{12,8},{16,20},{20,16},{24,28},{28,24},{32,36},... | collective-permute-start | bytes 12296 | tf_op jit(solution)/shard_map/ppermute | solution.py:458
  95.4 0.8 collective-permute-done.16
  96.2 1.5 %collective-permute-start.19 = (f32[8,128]{1,0:T(8,128)S(1)}, f32[8,128]{1,0:T(8,128)S(1)}, u32[]{:S(2)}, u32[]{:S(2)}) collective-permute-start(f32[8,128]{1,0:T(8,128)S(1)} %add.33), channel_id=1, source_target_pairs={{0,96},{4,100},{8,104},{12,108},{16,112},{20,116},{24,120},{28,124... | collective-permute-start | bytes 12296 | tf_op jit(solution)/shard_map/ppermute | solution.py:458
  97.7 0.6 collective-permute-start.17
  98.3 0.4 collective-permute-done.19
  98.7 3.0 %collective-permute-done.18 = f32[8,128]{1,0:T(8,128)S(1)} collective-permute-done((f32[8,128]{1,0:T(8,128)S(1)}, f32[8,128]{1,0:T(8,128)S(1)}, u32[]{:S(2)}, u32[]{:S(2)}) %collective-permute-start.18) | collective-permute-done | bytes 4128 | tf_op jit(solution)/shard_map/ppermute | solution.py:458
  101.7 0.7 select.1
  102.4 1.8 %collective-permute-start.21 = (f32[688,128]{1,0:T(8,128)S(1)}, f32[688,128]{1,0:T(8,128)S(1)}, u32[]{:S(2)}, u32[]{:S(2)}) collective-permute-start(f32[688,128]{1,0:T(8,128)S(1)} %get-tuple-element.100), channel_id=1, source_target_pairs={{0,124},{1,125},{2,126},{3,127},{4,0},{5,1},{6,2},{7,3},{8,4},{9,5... | collective-permute-start | bytes 1056776 | tf_op jit(solution)/shard_map/ppermute | solution.py:445
  104.2 0.1 collective-permute-start.20
  104.3 5.5 %collective-permute-start.22 = (f32[512,128]{1,0:T(8,128)S(1)}, f32[512,128]{1,0:T(8,128)S(1)}, u32[]{:S(2)}, u32[]{:S(2)}) collective-permute-start(f32[512,128]{1,0:T(8,128)S(1)} %get-tuple-element.101), channel_id=1, source_target_pairs={{0,120},{1,121},{2,122},{3,123},{4,124},{5,125},{6,126},{7,127},{8... | collective-permute-start | bytes 786440 | tf_op jit(solution)/shard_map/ppermute | solution.py:445
  109.9 1.0 collective-permute-start.25
  110.8 0.6 collective-permute-start.24
  111.4 1.2 collective-permute-done.25
  112.6 2.2 %collective-permute-done.24 = f32[8,128]{1,0:T(8,128)S(1)} collective-permute-done((f32[8,128]{1,0:T(8,128)S(1)}, f32[8,128]{1,0:T(8,128)S(1)}, u32[]{:S(2)}, u32[]{:S(2)}) %collective-permute-start.24) | collective-permute-done | bytes 4128 | tf_op jit(solution)/shard_map/ppermute | solution.py:445
  114.8 1.5 %collective-permute-done.23 = f32[8,128]{1,0:T(8,128)S(1)} collective-permute-done((f32[8,128]{1,0:T(8,128)S(1)}, f32[8,128]{1,0:T(8,128)S(1)}, u32[]{:S(2)}, u32[]{:S(2)}) %collective-permute-start.23) | collective-permute-done | bytes 4128 | tf_op jit(solution)/shard_map/ppermute | solution.py:445
  116.3 2.0 %last.1 = (f32[176,128]{1,0:T(8,128)}, f32[1024,128]{1,0:T(8,128)}, f32[176,128]{1,0:T(8,128)}, f32[1024,128]{1,0:T(8,128)}) custom-call(s32[1]{0:T(128)} %bitcast.me, s32[16]{0:T(128)S(1)} %get-tuple-element.56.position, f32[512,128]{1,0:T(8,128)S(1)} %collective-permute-done.20.s0, f32[512,128]{1,0:T(8,128)S(1)} %get-tuple-element.99.s1, ...), custom_call_target="tpu_custom_call" | custom-call | tf_op jit(solution)/shard_map/last/pallas_call | solution.py:623
  (20 shorter events, 0.1 us)
Async XLA Ops:
  2.7 16.2 %collective-permute-start.1 = (f32[1040,128]{1,0:T(8,128)S(1)}, f32[1040,128]{1,0:T(8,128)S(1)}, u32[]{:S(2)}, u32[]{:S(2)}) collective-permute-start(f32[1040,128]{1,0:T(8,128)S(1)} %get-tuple-element.63), channel_id=1, source_target_pairs={{0,5},{1,6},{2,7},{3,4},{4,9},{5,10},{6,11},{7,8},{8,13},{9,14},{1... | collective-permute-start | bytes 1597448 | tf_op jit(solution)/shard_map/ppermute | solution.py:445
  6.8 1.0 copy-start
  20.1 16.9 %collective-permute-start.2 = (f32[696,128]{1,0:T(8,128)S(1)}, f32[696,128]{1,0:T(8,128)S(1)}, u32[]{:S(2)}, u32[]{:S(2)}) collective-permute-start(f32[696,128]{1,0:T(8,128)S(1)} %get-tuple-element.66), channel_id=1, source_target_pairs={{0,4},{1,5},{2,6},{3,7},{4,8},{5,9},{6,10},{7,11},{8,12},{9,13},{1... | collective-permute-start | bytes 1069064 | tf_op jit(solution)/shard_map/ppermute | solution.py:445
  22.6 8.3 %collective-permute-start = (f32[520,128]{1,0:T(8,128)S(1)}, f32[520,128]{1,0:T(8,128)S(1)}, u32[]{:S(2)}, u32[]{:S(2)}) collective-permute-start(f32[520,128]{1,0:T(8,128)S(1)} %get-tuple-element.62), channel_id=1, source_target_pairs={{0,1},{1,2},{2,3},{3,0},{4,5},{5,6},{6,7},{7,4},{8,9},{9,10},{10,1... | collective-permute-start | bytes 798728 | tf_op jit(solution)/shard_map/ppermute | solution.py:445
  22.6 14.4 %collective-permute-start.3 = (f32[520,128]{1,0:T(8,128)S(1)}, f32[520,128]{1,0:T(8,128)S(1)}, u32[]{:S(2)}, u32[]{:S(2)}) collective-permute-start(f32[520,128]{1,0:T(8,128)S(1)} %get-tuple-element.67), channel_id=1, source_target_pairs={{0,8},{1,9},{2,10},{3,11},{4,12},{5,13},{6,14},{7,15},{8,16},{9,17... | collective-permute-start | bytes 798728 | tf_op jit(solution)/shard_map/ppermute | solution.py:445
  44.2 13.6 %collective-permute-start.5 = (f32[1024,128]{1,0:T(8,128)S(1)}, f32[1024,128]{1,0:T(8,128)S(1)}, u32[]{:S(2)}, u32[]{:S(2)}) collective-permute-start(f32[1024,128]{1,0:T(8,128)S(1)} %get-tuple-element.79), channel_id=1, source_target_pairs={{0,5},{1,6},{2,7},{3,4},{4,9},{5,10},{6,11},{7,8},{8,13},{9,14},{1... | collective-permute-start | bytes 1572872 | tf_op jit(solution)/shard_map/ppermute | solution.py:445
  44.2 11.5 %collective-permute-start.6 = (f32[688,128]{1,0:T(8,128)S(1)}, f32[688,128]{1,0:T(8,128)S(1)}, u32[]{:S(2)}, u32[]{:S(2)}) collective-permute-start(f32[688,128]{1,0:T(8,128)S(1)} %get-tuple-element.81), channel_id=1, source_target_pairs={{0,124},{1,125},{2,126},{3,127},{4,0},{5,1},{6,2},{7,3},{8,4},{9,5... | collective-permute-start | bytes 1056776 | tf_op jit(solution)/shard_map/ppermute | solution.py:445
  44.5 6.1 %collective-permute-start.4 = (f32[512,128]{1,0:T(8,128)S(1)}, f32[512,128]{1,0:T(8,128)S(1)}, u32[]{:S(2)}, u32[]{:S(2)}) collective-permute-start(f32[512,128]{1,0:T(8,128)S(1)} %get-tuple-element.76), channel_id=1, source_target_pairs={{0,3},{1,0},{2,1},{3,2},{4,7},{5,4},{6,5},{7,6},{8,11},{9,8},{10,9... | collective-permute-start | bytes 786440 | tf_op jit(solution)/shard_map/ppermute | solution.py:445
  47.3 8.4 %collective-permute-start.7 = (f32[512,128]{1,0:T(8,128)S(1)}, f32[512,128]{1,0:T(8,128)S(1)}, u32[]{:S(2)}, u32[]{:S(2)}) collective-permute-start(f32[512,128]{1,0:T(8,128)S(1)} %get-tuple-element.82), channel_id=1, source_target_pairs={{0,120},{1,121},{2,122},{3,123},{4,124},{5,125},{6,126},{7,127},{8... | collective-permute-start | bytes 786440 | tf_op jit(solution)/shard_map/ppermute | solution.py:445
  58.5 16.2 %collective-permute-start.9 = (f32[688,128]{1,0:T(8,128)S(1)}, f32[688,128]{1,0:T(8,128)S(1)}, u32[]{:S(2)}, u32[]{:S(2)}) collective-permute-start(f32[688,128]{1,0:T(8,128)S(1)} %get-tuple-element.85), channel_id=1, source_target_pairs={{0,4},{1,5},{2,6},{3,7},{4,8},{5,9},{6,10},{7,11},{8,12},{9,13},{1... | collective-permute-start | bytes 1056776 | tf_op jit(solution)/shard_map/ppermute | solution.py:445
  58.6 8.0 %collective-permute-start.10 = (f32[512,128]{1,0:T(8,128)S(1)}, f32[512,128]{1,0:T(8,128)S(1)}, u32[]{:S(2)}, u32[]{:S(2)}) collective-permute-start(f32[512,128]{1,0:T(8,128)S(1)} %get-tuple-element.86), channel_id=1, source_target_pairs={{0,1},{1,2},{2,3},{3,0},{4,5},{5,6},{6,7},{7,4},{8,9},{9,10},{10,1... | collective-permute-start | bytes 786440 | tf_op jit(solution)/shard_map/ppermute | solution.py:445
  60.1 14.5 %collective-permute-start.11 = (f32[512,128]{1,0:T(8,128)S(1)}, f32[512,128]{1,0:T(8,128)S(1)}, u32[]{:S(2)}, u32[]{:S(2)}) collective-permute-start(f32[512,128]{1,0:T(8,128)S(1)} %get-tuple-element.88), channel_id=1, source_target_pairs={{0,8},{1,9},{2,10},{3,11},{4,12},{5,13},{6,14},{7,15},{8,16},{9,17... | collective-permute-start | bytes 786440 | tf_op jit(solution)/shard_map/ppermute | solution.py:445
  60.1 19.0 %collective-permute-start.8 = (f32[1024,128]{1,0:T(8,128)S(1)}, f32[1024,128]{1,0:T(8,128)S(1)}, u32[]{:S(2)}, u32[]{:S(2)}) collective-permute-start(f32[1024,128]{1,0:T(8,128)S(1)} %get-tuple-element.84), channel_id=1, source_target_pairs={{0,127},{1,124},{2,125},{3,126},{4,3},{5,0},{6,1},{7,2},{8,7},{9,4... | collective-permute-start | bytes 1572872 | tf_op jit(solution)/shard_map/ppermute | solution.py:445
  84.8 16.9 %collective-permute-start.12 = (f32[1032,128]{1,0:T(8,128)S(1)}, f32[1032,128]{1,0:T(8,128)S(1)}, u32[]{:S(2)}, u32[]{:S(2)}) collective-permute-start(f32[1032,128]{1,0:T(8,128)S(1)} %get-tuple-element.96), channel_id=1, source_target_pairs={{0,127},{1,124},{2,125},{3,126},{4,3},{5,0},{6,1},{7,2},{8,7},{9,4... | collective-permute-start | bytes 1585160 | tf_op jit(solution)/shard_map/ppermute | solution.py:445
  85.8 2.8 %collective-permute-start.15 = (f32[8,128]{1,0:T(8,128)S(1)}, f32[8,128]{1,0:T(8,128)S(1)}, u32[]{:S(2)}, u32[]{:S(2)}) collective-permute-start(f32[8,128]{1,0:T(8,128)S(1)} %get-tuple-element.97), channel_id=1, source_target_pairs={{0,24},{4,28},{8,0},{12,4},{16,8},{20,12},{24,16},{28,20},{32,56},... | collective-permute-start | bytes 12296 | tf_op jit(solution)/shard_map/ppermute | solution.py:458
  85.8 4.0 %collective-permute-start.14 = (f32[8,128]{1,0:T(8,128)S(1)}, f32[8,128]{1,0:T(8,128)S(1)}, u32[]{:S(2)}, u32[]{:S(2)}) collective-permute-start(f32[8,128]{1,0:T(8,128)S(1)} %get-tuple-element.97), channel_id=1, source_target_pairs={{0,16},{4,20},{8,24},{12,28},{16,0},{20,4},{24,8},{28,12},{32,48},... | collective-permute-start | bytes 12296 | tf_op jit(solution)/shard_map/ppermute | solution.py:458
  85.8 4.8 %collective-permute-start.13 = (f32[8,128]{1,0:T(8,128)S(1)}, f32[8,128]{1,0:T(8,128)S(1)}, u32[]{:S(2)}, u32[]{:S(2)}) collective-permute-start(f32[8,128]{1,0:T(8,128)S(1)} %get-tuple-element.97), channel_id=1, source_target_pairs={{0,8},{4,12},{8,16},{12,20},{16,24},{20,28},{24,0},{28,4},{32,40},... | collective-permute-start | bytes 12296 | tf_op jit(solution)/shard_map/ppermute | solution.py:458
  90.7 5.6 %collective-permute-start.16 = (f32[8,128]{1,0:T(8,128)S(1)}, f32[8,128]{1,0:T(8,128)S(1)}, u32[]{:S(2)}, u32[]{:S(2)}) collective-permute-start(f32[8,128]{1,0:T(8,128)S(1)} %add_add_fusion.2), channel_id=1, source_target_pairs={{0,4},{4,0},{8,12},{12,8},{16,20},{20,16},{24,28},{28,24},{32,36},... | collective-permute-start | bytes 12296 | tf_op jit(solution)/shard_map/ppermute | solution.py:458
  96.2 2.5 %collective-permute-start.19 = (f32[8,128]{1,0:T(8,128)S(1)}, f32[8,128]{1,0:T(8,128)S(1)}, u32[]{:S(2)}, u32[]{:S(2)}) collective-permute-start(f32[8,128]{1,0:T(8,128)S(1)} %add.33), channel_id=1, source_target_pairs={{0,96},{4,100},{8,104},{12,108},{16,112},{20,116},{24,120},{28,124... | collective-permute-start | bytes 12296 | tf_op jit(solution)/shard_map/ppermute | solution.py:458
  97.7 4.0 %collective-permute-start.18 = (f32[8,128]{1,0:T(8,128)S(1)}, f32[8,128]{1,0:T(8,128)S(1)}, u32[]{:S(2)}, u32[]{:S(2)}) collective-permute-start(f32[8,128]{1,0:T(8,128)S(1)} %add.33), channel_id=1, source_target_pairs={{0,64},{4,68},{8,72},{12,76},{16,80},{20,84},{24,88},{28,92},{32,9... | collective-permute-start | bytes 12296 | tf_op jit(solution)/shard_map/ppermute | solution.py:458
  97.7 4.0 %collective-permute-start.17 = (f32[8,128]{1,0:T(8,128)S(1)}, f32[8,128]{1,0:T(8,128)S(1)}, u32[]{:S(2)}, u32[]{:S(2)}) collective-permute-start(f32[8,128]{1,0:T(8,128)S(1)} %add.33), channel_id=1, source_target_pairs={{0,32},{4,36},{8,40},{12,44},{16,48},{20,52},{24,56},{28,60},{32,6... | collective-permute-start | bytes 12296 | tf_op jit(solution)/shard_map/ppermute | solution.py:458
  102.4 13.9 %collective-permute-start.21 = (f32[688,128]{1,0:T(8,128)S(1)}, f32[688,128]{1,0:T(8,128)S(1)}, u32[]{:S(2)}, u32[]{:S(2)}) collective-permute-start(f32[688,128]{1,0:T(8,128)S(1)} %get-tuple-element.100), channel_id=1, source_target_pairs={{0,124},{1,125},{2,126},{3,127},{4,0},{5,1},{6,2},{7,3},{8,4},{9,5... | collective-permute-start | bytes 1056776 | tf_op jit(solution)/shard_map/ppermute | solution.py:445
  104.2 12.1 %collective-permute-start.20 = (f32[512,128]{1,0:T(8,128)S(1)}, f32[512,128]{1,0:T(8,128)S(1)}, u32[]{:S(2)}, u32[]{:S(2)}) collective-permute-start(f32[512,128]{1,0:T(8,128)S(1)} %get-tuple-element.98), channel_id=1, source_target_pairs={{0,4},{1,5},{2,6},{3,7},{4,8},{5,9},{6,10},{7,11},{8,12},{9,13},{1... | collective-permute-start | bytes 786440 | tf_op jit(solution)/shard_map/ppermute | solution.py:445
  104.3 11.9 %collective-permute-start.22 = (f32[512,128]{1,0:T(8,128)S(1)}, f32[512,128]{1,0:T(8,128)S(1)}, u32[]{:S(2)}, u32[]{:S(2)}) collective-permute-start(f32[512,128]{1,0:T(8,128)S(1)} %get-tuple-element.101), channel_id=1, source_target_pairs={{0,120},{1,121},{2,122},{3,123},{4,124},{5,125},{6,126},{7,127},{8... | collective-permute-start | bytes 786440 | tf_op jit(solution)/shard_map/ppermute | solution.py:445
  109.9 2.8 %collective-permute-start.25 = (f32[8,128]{1,0:T(8,128)S(1)}, f32[8,128]{1,0:T(8,128)S(1)}, u32[]{:S(2)}, u32[]{:S(2)}) collective-permute-start(f32[8,128]{1,0:T(8,128)S(1)} %add_add_fusion.1.token), channel_id=1, source_target_pairs={{0,3},{1,0},{2,1},{3,2},{4,7},{5,4},{6,5},{7,6},{8,11},{9,8},{10,9... | collective-permute-start | bytes 12296 | tf_op jit(solution)/shard_map/ppermute | solution.py:445
  110.8 4.0 %collective-permute-start.24 = (f32[8,128]{1,0:T(8,128)S(1)}, f32[8,128]{1,0:T(8,128)S(1)}, u32[]{:S(2)}, u32[]{:S(2)}) collective-permute-start(f32[8,128]{1,0:T(8,128)S(1)} %add_add_fusion.1.token), channel_id=1, source_target_pairs={{0,2},{1,3},{2,0},{3,1},{4,6},{5,7},{6,4},{7,5},{8,10},{9,11},{10,... | collective-permute-start | bytes 12296 | tf_op jit(solution)/shard_map/ppermute | solution.py:445
  112.6 3.7 %collective-permute-start.23 = (f32[8,128]{1,0:T(8,128)S(1)}, f32[8,128]{1,0:T(8,128)S(1)}, u32[]{:S(2)}, u32[]{:S(2)}) collective-permute-start(f32[8,128]{1,0:T(8,128)S(1)} %add_add_fusion.1.token), channel_id=1, source_target_pairs={{0,1},{1,2},{2,3},{3,0},{4,5},{5,6},{6,7},{7,4},{8,9},{9,10},{10,1... | collective-permute-start | bytes 12296 | tf_op jit(solution)/shard_map/ppermute | solution.py:445

commit v4 on v3

--- a/solution.py
+++ b/solution.py
@@ -24,7 +24,7 @@
 K_PAD = 256
 HOP = 1
 BACK_HOP = 1
-TILE = 480
+TILE = 240
 TILES = NS // TILE
 PIECE = 240
 PIECES = NS // PIECE
@@ -461,8 +461,8 @@
 def total(value):
     value = value + sum(rotated(value, 4, 2, k) for k in (1, 2, 3))
     value = value + rotated(value, 2, 1, 1)
+    token = value
     value = value + sum(rotated(value, 4, 8, k) for k in (1, 2, 3))
-    token = value
     value = value + sent(value, 1, 0) + sent(value, 2, 0) + sent(value, 3, 0)
     return value, token
 

time: 118 us -> 115 us (0.975)
  waiting for transfers between devices: 46 us -> 43 us
  starting transfers between devices: 36.1 us -> 34.8 us
    ppermute x7, waiting for transfers between devices: 7.59 us -> 4.21 us  [rotated(): return lax.ppermute(value, 'sub', pairs)]
    ppermute x19, starting transfers between devices: 27.9 us -> 26.6 us  [sent(): return lax.ppermute(value, ('sub', 'body'), pairs)]
  transfers between devices with their start and end apart: 26 -> 26, of which waited for: 17 -> 16; matrix products, arithmetic and copies ran while one was open for 0% -> 0% of each run, Pallas kernels for 13% -> 14%
where the time goes in v4:
time: 115 us; the launch traced here: 114 us
  waiting for transfers between devices  43 us (37%)
  starting transfers between devices  34.8 us (30%)
  Pallas kernels  34.4 us (30%)
    ppermute x19, waiting for transfers between devices, sent(): return lax.ppermute(value, ('sub', 'body'), pairs)  38.8 us
    ppermute x19, starting transfers between devices, sent(): return lax.ppermute(value, ('sub', 'body'), pairs)  26.6 us
    pallas_call x1, Pallas kernels, per_device(): pl.pallas_call(split_kernel, out_shape=[pltpu.VMEM((NS, KP), bf16)] * 2 +...  10.4 us
    ppermute x7, starting transfers between devices, rotated(): return lax.ppermute(value, 'sub', pairs)  8.23 us
    pallas_call x1, Pallas kernels, per_device(): pl.pallas_call(first_kernel, out_shape=[far_block, seg_block, seg_block,...  7.17 us
    pallas_call x1, Pallas kernels, per_device(): pl.pallas_call(second_kernel, out_shape=[shape(NS, LC), shape(G, LC), sha...  4.72 us
    pallas_call x1, Pallas kernels, per_device(): pl.pallas_call(master_kernel, out_shape=[shape(NS, LC), shape(CR, LC)], i...  4.42 us
    ppermute x7, waiting for transfers between devices, rotated(): return lax.ppermute(value, 'sub', pairs)  4.21 us
  transfers between devices with their start and end apart: 26, of which 16 were waited for; matrix products, arithmetic and copies ran while one was open for 0% of the time, Pallas kernels for 14%

profile of v4, /device:TPU:1, one launch (start us, length us, event | category | flops | bytes accessed | tf_op | source)
XLA Modules:
  0.0 114.1 jit_solution(1835010272682341071)
XLA Ops:
  0.6 2.0 %pack.1 = (f32[1040,128]{1,0:T(8,128)S(1)}, f32[1024,128]{1,0:T(8,128)S(1)}, f32[1024,128]{1,0:T(8,128)S(1)}, f32[176,128]{1,0:T(8,128)S(1)}, f32[16,128]{1,0:T(...) custom-call(s32[1]{0:T(128)} %bitcast.me, s32[16]{0:T(128)} %bitcast.17, ...), custom_call_target="tpu_custom_call" | custom-call | tf_op jit(solution)/shard_map/pack/pallas_call | solution.py:491
  2.7 4.1 %collective-permute-start.1 = (f32[1040,128]{1,0:T(8,128)S(1)}, f32[1040,128]{1,0:T(8,128)S(1)}, u32[]{:S(2)}, u32[]{:S(2)}) collective-permute-start(f32[1040,128]{1,0:T(8,128)S(1)} %get-tuple-element.63), channel_id=1, source_target_pairs={{0,5},{1,6},{2,7},{3,4},{4,9},{5,10},{6,11},{7,8},{8,13},{9,14},{1... | collective-permute-start | bytes 1597448 | tf_op jit(solution)/shard_map/ppermute | solution.py:445
  6.8 1.0 copy-done
  7.8 10.4 %split.1 = (bf16[2400,2560]{1,0:T(8,128)(2,1)S(1)}, bf16[2400,2560]{1,0:T(8,128)(2,1)S(1)}, f32[2400,128]{1,0:T(8,128)S(1)}, bf16[2048,64]{1,0:T(8,128)(2,1)S(1)...) custom-call(s32[8]{0:T(128)S(1)} %get-tuple-element.57.near_source, s32[16]{0:T(128)S(1)} %get-tuple-element.56.position, ...), custom_call_target="tpu_custom_call" | custom-call | flops 6291456000 | bytes 23040000 | tf_op jit(solution)/shard_map/split/pallas_call | solution.py:513
  18.2 0.6 collective-permute-done.1.far
  18.8 1.3 %relay.1 = (f32[536,128]{1,0:T(8,128)S(1)}, f32[696,128]{1,0:T(8,128)S(1)}, f32[520,128]{1,0:T(8,128)S(1)}, s32[32]{0:T(128)}) custom-call(f32[1040,128]{1,0:T(8,128)S(1)} %collective-permute-done.1.far, f32[176,128]{1,0:T(8,128)S(1)} %get-tuple-element.60.pg, f32[2400,128]{1,0:T(8,128)S(1)} %get-tuple-element.64.token.partial), custom_call_target="tpu_custom_call" | custom-call | tf_op jit(solution)/shard_map/relay/pallas_call | solution.py:533
  20.1 2.5 %collective-permute-start.2 = (f32[696,128]{1,0:T(8,128)S(1)}, f32[696,128]{1,0:T(8,128)S(1)}, u32[]{:S(2)}, u32[]{:S(2)}) collective-permute-start(f32[696,128]{1,0:T(8,128)S(1)} %get-tuple-element.66), channel_id=1, source_target_pairs={{0,4},{1,5},{2,6},{3,7},{4,8},{5,9},{6,10},{7,11},{8,12},{9,13},{1... | collective-permute-start | bytes 1069064 | tf_op jit(solution)/shard_map/ppermute | solution.py:445
  22.6 1.6 %collective-permute-start.3 = (f32[520,128]{1,0:T(8,128)S(1)}, f32[520,128]{1,0:T(8,128)S(1)}, u32[]{:S(2)}, u32[]{:S(2)}) collective-permute-start(f32[520,128]{1,0:T(8,128)S(1)} %get-tuple-element.67), channel_id=1, source_target_pairs={{0,8},{1,9},{2,10},{3,11},{4,12},{5,13},{6,14},{7,15},{8,16},{9,17... | collective-permute-start | bytes 798728 | tf_op jit(solution)/shard_map/ppermute | solution.py:445
  24.3 6.7 %collective-permute-done.in0 = f32[520,128]{1,0:T(8,128)S(1)} collective-permute-done((f32[520,128]{1,0:T(8,128)S(1)}, f32[520,128]{1,0:T(8,128)S(1)}, u32[]{:S(2)}, u32[]{:S(2)}) %collective-permute-start) | collective-permute-done | bytes 266272 | tf_op jit(solution)/shard_map/ppermute | solution.py:445
  31.0 6.1 %collective-permute-done.3.in3 = f32[520,128]{1,0:T(8,128)S(1)} collective-permute-done((f32[520,128]{1,0:T(8,128)S(1)}, f32[520,128]{1,0:T(8,128)S(1)}, u32[]{:S(2)}, u32[]{:S(2)}) %collective-permute-start.3) | collective-permute-done | bytes 266272 | tf_op jit(solution)/shard_map/ppermute | solution.py:445
  37.0 7.2 %first.1 = (f32[1024,128]{1,0:T(8,128)S(1)}, f32[512,128]{1,0:T(8,128)S(1)}, f32[512,128]{1,0:T(8,128)S(1)}, f32[688,128]{1,0:T(8,128)S(1)}, f32[512,128]{1,0:T(...) custom-call(s32[1]{0:T(128)} %bitcast.me, ...), custom_call_target="tpu_custom_call" | custom-call | tf_op jit(solution)/shard_map/first/pallas_call | solution.py:544
  44.2 0.1 collective-permute-start.5
  44.3 0.2 collective-permute-start.6
  44.5 2.9 %collective-permute-start.4 = (f32[512,128]{1,0:T(8,128)S(1)}, f32[512,128]{1,0:T(8,128)S(1)}, u32[]{:S(2)}, u32[]{:S(2)}) collective-permute-start(f32[512,128]{1,0:T(8,128)S(1)} %get-tuple-element.76), channel_id=1, source_target_pairs={{0,3},{1,0},{2,1},{3,2},{4,7},{5,4},{6,5},{7,6},{8,11},{9,8},{10,9... | collective-permute-start | bytes 786440 | tf_op jit(solution)/shard_map/ppermute | solution.py:445
  47.3 2.3 %collective-permute-start.7 = (f32[512,128]{1,0:T(8,128)S(1)}, f32[512,128]{1,0:T(8,128)S(1)}, u32[]{:S(2)}, u32[]{:S(2)}) collective-permute-start(f32[512,128]{1,0:T(8,128)S(1)} %get-tuple-element.82), channel_id=1, source_target_pairs={{0,120},{1,121},{2,122},{3,123},{4,124},{5,125},{6,126},{7,127},{8... | collective-permute-start | bytes 786440 | tf_op jit(solution)/shard_map/ppermute | solution.py:445
  49.6 1.0 collective-permute-done.4.token.near
  50.7 5.1 %collective-permute-done.7.r3 = f32[512,128]{1,0:T(8,128)S(1)} collective-permute-done((f32[512,128]{1,0:T(8,128)S(1)}, f32[512,128]{1,0:T(8,128)S(1)}, u32[]{:S(2)}, u32[]{:S(2)}) %collective-permute-start.7) | collective-permute-done | bytes 262176 | tf_op jit(solution)/shard_map/ppermute | solution.py:445
  55.7 0.0 collective-permute-done.6.r2
  55.8 2.0 %collective-permute-done.5.far = f32[1024,128]{1,0:T(8,128)S(1)} collective-permute-done((f32[1024,128]{1,0:T(8,128)S(1)}, f32[1024,128]{1,0:T(8,128)S(1)}, u32[]{:S(2)}, u32[]{:S(2)}) %collective-permute-start.5) | collective-permute-done | bytes 524320 | tf_op jit(solution)/shard_map/ppermute | solution.py:445
  57.7 0.8 exchange.1
  58.5 0.1 collective-permute-start.9
  58.6 1.6 %collective-permute-start.10 = (f32[512,128]{1,0:T(8,128)S(1)}, f32[512,128]{1,0:T(8,128)S(1)}, u32[]{:S(2)}, u32[]{:S(2)}) collective-permute-start(f32[512,128]{1,0:T(8,128)S(1)} %get-tuple-element.86), channel_id=1, source_target_pairs={{0,1},{1,2},{2,3},{3,0},{4,5},{5,6},{6,7},{7,4},{8,9},{9,10},{10,1... | collective-permute-start | bytes 786440 | tf_op jit(solution)/shard_map/ppermute | solution.py:445
  60.2 2.4 %collective-permute-start.8 = (f32[1024,128]{1,0:T(8,128)S(1)}, f32[1024,128]{1,0:T(8,128)S(1)}, u32[]{:S(2)}, u32[]{:S(2)}) collective-permute-start(f32[1024,128]{1,0:T(8,128)S(1)} %get-tuple-element.84), channel_id=1, source_target_pairs={{0,127},{1,124},{2,125},{3,126},{4,3},{5,0},{6,1},{7,2},{8,7},{9,4... | collective-permute-start | bytes 1572872 | tf_op jit(solution)/shard_map/ppermute | solution.py:445
  62.6 3.9 %collective-permute-done.10.f0 = f32[512,128]{1,0:T(8,128)S(1)} collective-permute-done((f32[512,128]{1,0:T(8,128)S(1)}, f32[512,128]{1,0:T(8,128)S(1)}, u32[]{:S(2)}, u32[]{:S(2)}) %collective-permute-start.10) | collective-permute-done | bytes 262176 | tf_op jit(solution)/shard_map/ppermute | solution.py:445
  66.6 8.2 %collective-permute-done.11.f3 = f32[512,128]{1,0:T(8,128)S(1)} collective-permute-done((f32[512,128]{1,0:T(8,128)S(1)}, f32[512,128]{1,0:T(8,128)S(1)}, u32[]{:S(2)}, u32[]{:S(2)}) %collective-permute-start.11) | collective-permute-done | bytes 262176 | tf_op jit(solution)/shard_map/ppermute | solution.py:445
  74.7 0.0 collective-permute-done.9.f2
  74.7 4.4 %master.1 = (f32[2400,128]{1,0:T(8,128)S(1)}, f32[1024,128]{1,0:T(8,128)S(1)}) custom-call(s32[32]{0:T(128)S(1)} %get-tuple-element.74.slots, f32[512,128]{1,0:T(8,128)S(1)} %collective-permute-done.10.f0, f32[512,128]{1,0:T(8,128)S(1)} %get-tuple-element.87.f1, f32[688,128]{1,0:T(8,128)S(1)} %collective-permute-done.9.f2, ...), custom_call_target="tpu_custom_call" | custom-call | flops 2831155200 | bytes 1048576 | tf_op jit(solution)/shard_map/master/pallas_call | solution.py:579
  79.2 4.7 %second.1 = (f32[2400,128]{1,0:T(8,128)S(1)}, f32[176,128]{1,0:T(8,128)S(1)}, f32[1024,128]{1,0:T(8,128)S(1)}, f32[8,128]{1,0:T(8,128)S(1)}) custom-call(s32[1]{0:T(128)} %bitcast.me, s32[16]{0:T(128)S(1)} %get-tuple-element.75.place, f32[512,128]{1,0:T(8,128)S(1)} %collective-permute-done.4.token.near, f32[1024,128]{1,0:T(8,128)S(1)} %collective-permute-done.8.far, ...), custom_call_target="tpu_custom_call" | custom-call | tf_op jit(solution)/shard_map/second/pallas_call | solution.py:590
  83.9 1.0 reply.1
  84.9 1.0 collective-permute-start.12
  85.9 1.5 %collective-permute-start.13 = (f32[8,128]{1,0:T(8,128)S(1)}, f32[8,128]{1,0:T(8,128)S(1)}, u32[]{:S(2)}, u32[]{:S(2)}) collective-permute-start(f32[8,128]{1,0:T(8,128)S(1)} %get-tuple-element.97), channel_id=1, source_target_pairs={{0,8},{4,12},{8,16},{12,20},{16,24},{20,28},{24,0},{28,4},{32,40},... | collective-permute-start | bytes 12296 | tf_op jit(solution)/shard_map/ppermute | solution.py:458
  87.3 1.3 %collective-permute-done.15 = f32[8,128]{1,0:T(8,128)S(1)} collective-permute-done((f32[8,128]{1,0:T(8,128)S(1)}, f32[8,128]{1,0:T(8,128)S(1)}, u32[]{:S(2)}, u32[]{:S(2)}) %collective-permute-start.15) | collective-permute-done | bytes 4128 | tf_op jit(solution)/shard_map/ppermute | solution.py:458
  88.6 1.2 %collective-permute-done.14 = f32[8,128]{1,0:T(8,128)S(1)} collective-permute-done((f32[8,128]{1,0:T(8,128)S(1)}, f32[8,128]{1,0:T(8,128)S(1)}, u32[]{:S(2)}, u32[]{:S(2)}) %collective-permute-start.14) | collective-permute-done | bytes 4128 | tf_op jit(solution)/shard_map/ppermute | solution.py:458
  89.8 0.9 collective-permute-done.13
  90.7 4.7 %collective-permute-start.16 = (f32[8,128]{1,0:T(8,128)S(1)}, f32[8,128]{1,0:T(8,128)S(1)}, u32[]{:S(2)}, u32[]{:S(2)}) collective-permute-start(f32[8,128]{1,0:T(8,128)S(1)} %add_add_fusion.2), channel_id=1, source_target_pairs={{0,4},{4,0},{8,12},{12,8},{16,20},{20,16},{24,28},{28,24},{32,36},... | collective-permute-start | bytes 12296 | tf_op jit(solution)/shard_map/ppermute | solution.py:458
  95.4 0.8 collective-permute-done.16
  96.3 1.5 %collective-permute-start.22 = (f32[8,128]{1,0:T(8,128)S(1)}, f32[8,128]{1,0:T(8,128)S(1)}, u32[]{:S(2)}, u32[]{:S(2)}) collective-permute-start(f32[8,128]{1,0:T(8,128)S(1)} %add.33.token), channel_id=1, source_target_pairs={{0,96},{4,100},{8,104},{12,108},{16,112},{20,116},{24,120},{28,124... | collective-permute-start | bytes 12296 | tf_op jit(solution)/shard_map/ppermute | solution.py:458
  97.7 0.6 collective-permute-start.20
  98.3 0.7 select.1
  99.0 1.0 collective-permute-start.17
  100.0 4.6 %collective-permute-start.19 = (f32[512,128]{1,0:T(8,128)S(1)}, f32[512,128]{1,0:T(8,128)S(1)}, u32[]{:S(2)}, u32[]{:S(2)}) collective-permute-start(f32[512,128]{1,0:T(8,128)S(1)} %get-tuple-element.101), channel_id=1, source_target_pairs={{0,120},{1,121},{2,122},{3,123},{4,124},{5,125},{6,126},{7,127},{8... | collective-permute-start | bytes 786440 | tf_op jit(solution)/shard_map/ppermute | solution.py:445
  104.7 2.1 %collective-permute-start.25 = (f32[8,128]{1,0:T(8,128)S(1)}, f32[8,128]{1,0:T(8,128)S(1)}, u32[]{:S(2)}, u32[]{:S(2)}) collective-permute-start(f32[8,128]{1,0:T(8,128)S(1)} %add_add_fusion.1), channel_id=1, source_target_pairs={{0,3},{1,0},{2,1},{3,2},{4,7},{5,4},{6,5},{7,6},{8,11},{9,8},{10,9... | collective-permute-start | bytes 12296 | tf_op jit(solution)/shard_map/ppermute | solution.py:445
  106.8 0.8 collective-permute-done.25
  107.6 0.1 collective-permute-start.23
  107.6 3.1 %collective-permute-done.24 = f32[8,128]{1,0:T(8,128)S(1)} collective-permute-done((f32[8,128]{1,0:T(8,128)S(1)}, f32[8,128]{1,0:T(8,128)S(1)}, u32[]{:S(2)}, u32[]{:S(2)}) %collective-permute-start.24) | collective-permute-done | bytes 4128 | tf_op jit(solution)/shard_map/ppermute | solution.py:445
  110.8 1.3 %collective-permute-done.23 = f32[8,128]{1,0:T(8,128)S(1)} collective-permute-done((f32[8,128]{1,0:T(8,128)S(1)}, f32[8,128]{1,0:T(8,128)S(1)}, u32[]{:S(2)}, u32[]{:S(2)}) %collective-permute-start.23) | collective-permute-done | bytes 4128 | tf_op jit(solution)/shard_map/ppermute | solution.py:445
  112.1 0.1 collective-permute-done.18.s2
  112.1 2.0 %last.1 = (f32[176,128]{1,0:T(8,128)}, f32[1024,128]{1,0:T(8,128)}, f32[176,128]{1,0:T(8,128)}, f32[1024,128]{1,0:T(8,128)}) custom-call(s32[1]{0:T(128)} %bitcast.me, s32[16]{0:T(128)S(1)} %get-tuple-element.56.position, f32[512,128]{1,0:T(8,128)S(1)} %collective-permute-done.17.s0, f32[512,128]{1,0:T(8,128)S(1)} %get-tuple-element.99.s1, ...), custom_call_target="tpu_custom_call" | custom-call | tf_op jit(solution)/shard_map/last/pallas_call | solution.py:623
  (20 shorter events, 0.1 us)
Async XLA Ops:
  2.7 16.2 %collective-permute-start.1 = (f32[1040,128]{1,0:T(8,128)S(1)}, f32[1040,128]{1,0:T(8,128)S(1)}, u32[]{:S(2)}, u32[]{:S(2)}) collective-permute-start(f32[1040,128]{1,0:T(8,128)S(1)} %get-tuple-element.63), channel_id=1, source_target_pairs={{0,5},{1,6},{2,7},{3,4},{4,9},{5,10},{6,11},{7,8},{8,13},{9,14},{1... | collective-permute-start | bytes 1597448 | tf_op jit(solution)/shard_map/ppermute | solution.py:445
  6.8 1.0 copy-start
  20.1 16.9 %collective-permute-start.2 = (f32[696,128]{1,0:T(8,128)S(1)}, f32[696,128]{1,0:T(8,128)S(1)}, u32[]{:S(2)}, u32[]{:S(2)}) collective-permute-start(f32[696,128]{1,0:T(8,128)S(1)} %get-tuple-element.66), channel_id=1, source_target_pairs={{0,4},{1,5},{2,6},{3,7},{4,8},{5,9},{6,10},{7,11},{8,12},{9,13},{1... | collective-permute-start | bytes 1069064 | tf_op jit(solution)/shard_map/ppermute | solution.py:445
  22.6 8.3 %collective-permute-start = (f32[520,128]{1,0:T(8,128)S(1)}, f32[520,128]{1,0:T(8,128)S(1)}, u32[]{:S(2)}, u32[]{:S(2)}) collective-permute-start(f32[520,128]{1,0:T(8,128)S(1)} %get-tuple-element.62), channel_id=1, source_target_pairs={{0,1},{1,2},{2,3},{3,0},{4,5},{5,6},{6,7},{7,4},{8,9},{9,10},{10,1... | collective-permute-start | bytes 798728 | tf_op jit(solution)/shard_map/ppermute | solution.py:445
  22.6 14.4 %collective-permute-start.3 = (f32[520,128]{1,0:T(8,128)S(1)}, f32[520,128]{1,0:T(8,128)S(1)}, u32[]{:S(2)}, u32[]{:S(2)}) collective-permute-start(f32[520,128]{1,0:T(8,128)S(1)} %get-tuple-element.67), channel_id=1, source_target_pairs={{0,8},{1,9},{2,10},{3,11},{4,12},{5,13},{6,14},{7,15},{8,16},{9,17... | collective-permute-start | bytes 798728 | tf_op jit(solution)/shard_map/ppermute | solution.py:445
  44.2 13.5 %collective-permute-start.5 = (f32[1024,128]{1,0:T(8,128)S(1)}, f32[1024,128]{1,0:T(8,128)S(1)}, u32[]{:S(2)}, u32[]{:S(2)}) collective-permute-start(f32[1024,128]{1,0:T(8,128)S(1)} %get-tuple-element.79), channel_id=1, source_target_pairs={{0,5},{1,6},{2,7},{3,4},{4,9},{5,10},{6,11},{7,8},{8,13},{9,14},{1... | collective-permute-start | bytes 1572872 | tf_op jit(solution)/shard_map/ppermute | solution.py:445
  44.3 11.5 %collective-permute-start.6 = (f32[688,128]{1,0:T(8,128)S(1)}, f32[688,128]{1,0:T(8,128)S(1)}, u32[]{:S(2)}, u32[]{:S(2)}) collective-permute-start(f32[688,128]{1,0:T(8,128)S(1)} %get-tuple-element.81), channel_id=1, source_target_pairs={{0,124},{1,125},{2,126},{3,127},{4,0},{5,1},{6,2},{7,3},{8,4},{9,5... | collective-permute-start | bytes 1056776 | tf_op jit(solution)/shard_map/ppermute | solution.py:445
  44.5 6.2 %collective-permute-start.4 = (f32[512,128]{1,0:T(8,128)S(1)}, f32[512,128]{1,0:T(8,128)S(1)}, u32[]{:S(2)}, u32[]{:S(2)}) collective-permute-start(f32[512,128]{1,0:T(8,128)S(1)} %get-tuple-element.76), channel_id=1, source_target_pairs={{0,3},{1,0},{2,1},{3,2},{4,7},{5,4},{6,5},{7,6},{8,11},{9,8},{10,9... | collective-permute-start | bytes 786440 | tf_op jit(solution)/shard_map/ppermute | solution.py:445
  47.3 8.4 %collective-permute-start.7 = (f32[512,128]{1,0:T(8,128)S(1)}, f32[512,128]{1,0:T(8,128)S(1)}, u32[]{:S(2)}, u32[]{:S(2)}) collective-permute-start(f32[512,128]{1,0:T(8,128)S(1)} %get-tuple-element.82), channel_id=1, source_target_pairs={{0,120},{1,121},{2,122},{3,123},{4,124},{5,125},{6,126},{7,127},{8... | collective-permute-start | bytes 786440 | tf_op jit(solution)/shard_map/ppermute | solution.py:445
  58.5 16.2 %collective-permute-start.9 = (f32[688,128]{1,0:T(8,128)S(1)}, f32[688,128]{1,0:T(8,128)S(1)}, u32[]{:S(2)}, u32[]{:S(2)}) collective-permute-start(f32[688,128]{1,0:T(8,128)S(1)} %get-tuple-element.85), channel_id=1, source_target_pairs={{0,4},{1,5},{2,6},{3,7},{4,8},{5,9},{6,10},{7,11},{8,12},{9,13},{1... | collective-permute-start | bytes 1056776 | tf_op jit(solution)/shard_map/ppermute | solution.py:445
  58.6 8.0 %collective-permute-start.10 = (f32[512,128]{1,0:T(8,128)S(1)}, f32[512,128]{1,0:T(8,128)S(1)}, u32[]{:S(2)}, u32[]{:S(2)}) collective-permute-start(f32[512,128]{1,0:T(8,128)S(1)} %get-tuple-element.86), channel_id=1, source_target_pairs={{0,1},{1,2},{2,3},{3,0},{4,5},{5,6},{6,7},{7,4},{8,9},{9,10},{10,1... | collective-permute-start | bytes 786440 | tf_op jit(solution)/shard_map/ppermute | solution.py:445
  60.2 14.5 %collective-permute-start.11 = (f32[512,128]{1,0:T(8,128)S(1)}, f32[512,128]{1,0:T(8,128)S(1)}, u32[]{:S(2)}, u32[]{:S(2)}) collective-permute-start(f32[512,128]{1,0:T(8,128)S(1)} %get-tuple-element.88), channel_id=1, source_target_pairs={{0,8},{1,9},{2,10},{3,11},{4,12},{5,13},{6,14},{7,15},{8,16},{9,17... | collective-permute-start | bytes 786440 | tf_op jit(solution)/shard_map/ppermute | solution.py:445
  60.2 18.9 %collective-permute-start.8 = (f32[1024,128]{1,0:T(8,128)S(1)}, f32[1024,128]{1,0:T(8,128)S(1)}, u32[]{:S(2)}, u32[]{:S(2)}) collective-permute-start(f32[1024,128]{1,0:T(8,128)S(1)} %get-tuple-element.84), channel_id=1, source_target_pairs={{0,127},{1,124},{2,125},{3,126},{4,3},{5,0},{6,1},{7,2},{8,7},{9,4... | collective-permute-start | bytes 1572872 | tf_op jit(solution)/shard_map/ppermute | solution.py:445
  84.9 13.5 %collective-permute-start.12 = (f32[1032,128]{1,0:T(8,128)S(1)}, f32[1032,128]{1,0:T(8,128)S(1)}, u32[]{:S(2)}, u32[]{:S(2)}) collective-permute-start(f32[1032,128]{1,0:T(8,128)S(1)} %get-tuple-element.96), channel_id=1, source_target_pairs={{0,127},{1,124},{2,125},{3,126},{4,3},{5,0},{6,1},{7,2},{8,7},{9,4... | collective-permute-start | bytes 1585160 | tf_op jit(solution)/shard_map/ppermute | solution.py:445
  85.9 2.8 %collective-permute-start.15 = (f32[8,128]{1,0:T(8,128)S(1)}, f32[8,128]{1,0:T(8,128)S(1)}, u32[]{:S(2)}, u32[]{:S(2)}) collective-permute-start(f32[8,128]{1,0:T(8,128)S(1)} %get-tuple-element.97), channel_id=1, source_target_pairs={{0,24},{4,28},{8,0},{12,4},{16,8},{20,12},{24,16},{28,20},{32,56},... | collective-permute-start | bytes 12296 | tf_op jit(solution)/shard_map/ppermute | solution.py:458
  85.9 4.0 %collective-permute-start.14 = (f32[8,128]{1,0:T(8,128)S(1)}, f32[8,128]{1,0:T(8,128)S(1)}, u32[]{:S(2)}, u32[]{:S(2)}) collective-permute-start(f32[8,128]{1,0:T(8,128)S(1)} %get-tuple-element.97), channel_id=1, source_target_pairs={{0,16},{4,20},{8,24},{12,28},{16,0},{20,4},{24,8},{28,12},{32,48},... | collective-permute-start | bytes 12296 | tf_op jit(solution)/shard_map/ppermute | solution.py:458
  85.9 4.8 %collective-permute-start.13 = (f32[8,128]{1,0:T(8,128)S(1)}, f32[8,128]{1,0:T(8,128)S(1)}, u32[]{:S(2)}, u32[]{:S(2)}) collective-permute-start(f32[8,128]{1,0:T(8,128)S(1)} %get-tuple-element.97), channel_id=1, source_target_pairs={{0,8},{4,12},{8,16},{12,20},{16,24},{20,28},{24,0},{28,4},{32,40},... | collective-permute-start | bytes 12296 | tf_op jit(solution)/shard_map/ppermute | solution.py:458
  90.7 5.5 %collective-permute-start.16 = (f32[8,128]{1,0:T(8,128)S(1)}, f32[8,128]{1,0:T(8,128)S(1)}, u32[]{:S(2)}, u32[]{:S(2)}) collective-permute-start(f32[8,128]{1,0:T(8,128)S(1)} %add_add_fusion.2), channel_id=1, source_target_pairs={{0,4},{4,0},{8,12},{12,8},{16,20},{20,16},{24,28},{28,24},{32,36},... | collective-permute-start | bytes 12296 | tf_op jit(solution)/shard_map/ppermute | solution.py:458
  96.3 8.4 %collective-permute-start.22 = (f32[8,128]{1,0:T(8,128)S(1)}, f32[8,128]{1,0:T(8,128)S(1)}, u32[]{:S(2)}, u32[]{:S(2)}) collective-permute-start(f32[8,128]{1,0:T(8,128)S(1)} %add.33.token), channel_id=1, source_target_pairs={{0,96},{4,100},{8,104},{12,108},{16,112},{20,116},{24,120},{28,124... | collective-permute-start | bytes 12296 | tf_op jit(solution)/shard_map/ppermute | solution.py:458
  97.7 6.9 %collective-permute-start.21 = (f32[8,128]{1,0:T(8,128)S(1)}, f32[8,128]{1,0:T(8,128)S(1)}, u32[]{:S(2)}, u32[]{:S(2)}) collective-permute-start(f32[8,128]{1,0:T(8,128)S(1)} %add.33.token), channel_id=1, source_target_pairs={{0,64},{4,68},{8,72},{12,76},{16,80},{20,84},{24,88},{28,92},{32,9... | collective-permute-start | bytes 12296 | tf_op jit(solution)/shard_map/ppermute | solution.py:458
  97.7 6.9 %collective-permute-start.20 = (f32[8,128]{1,0:T(8,128)S(1)}, f32[8,128]{1,0:T(8,128)S(1)}, u32[]{:S(2)}, u32[]{:S(2)}) collective-permute-start(f32[8,128]{1,0:T(8,128)S(1)} %add.33.token), channel_id=1, source_target_pairs={{0,32},{4,36},{8,40},{12,44},{16,48},{20,52},{24,56},{28,60},{32,6... | collective-permute-start | bytes 12296 | tf_op jit(solution)/shard_map/ppermute | solution.py:458
  99.0 13.0 %collective-permute-start.17 = (f32[512,128]{1,0:T(8,128)S(1)}, f32[512,128]{1,0:T(8,128)S(1)}, u32[]{:S(2)}, u32[]{:S(2)}) collective-permute-start(f32[512,128]{1,0:T(8,128)S(1)} %get-tuple-element.98), channel_id=1, source_target_pairs={{0,4},{1,5},{2,6},{3,7},{4,8},{5,9},{6,10},{7,11},{8,12},{9,13},{1... | collective-permute-start | bytes 786440 | tf_op jit(solution)/shard_map/ppermute | solution.py:445
  100.0 12.0 %collective-permute-start.19 = (f32[512,128]{1,0:T(8,128)S(1)}, f32[512,128]{1,0:T(8,128)S(1)}, u32[]{:S(2)}, u32[]{:S(2)}) collective-permute-start(f32[512,128]{1,0:T(8,128)S(1)} %get-tuple-element.101), channel_id=1, source_target_pairs={{0,120},{1,121},{2,122},{3,123},{4,124},{5,125},{6,126},{7,127},{8... | collective-permute-start | bytes 786440 | tf_op jit(solution)/shard_map/ppermute | solution.py:445
  104.7 7.5 %collective-permute-start.18 = (f32[688,128]{1,0:T(8,128)S(1)}, f32[688,128]{1,0:T(8,128)S(1)}, u32[]{:S(2)}, u32[]{:S(2)}) collective-permute-start(f32[688,128]{1,0:T(8,128)S(1)} %get-tuple-element.100), channel_id=1, source_target_pairs={{0,124},{1,125},{2,126},{3,127},{4,0},{5,1},{6,2},{7,3},{8,4},{9,5... | collective-permute-start | bytes 1056776 | tf_op jit(solution)/shard_map/ppermute | solution.py:445
  104.7 2.9 %collective-permute-start.25 = (f32[8,128]{1,0:T(8,128)S(1)}, f32[8,128]{1,0:T(8,128)S(1)}, u32[]{:S(2)}, u32[]{:S(2)}) collective-permute-start(f32[8,128]{1,0:T(8,128)S(1)} %add_add_fusion.1), channel_id=1, source_target_pairs={{0,3},{1,0},{2,1},{3,2},{4,7},{5,4},{6,5},{7,6},{8,11},{9,8},{10,9... | collective-permute-start | bytes 12296 | tf_op jit(solution)/shard_map/ppermute | solution.py:445
  106.8 4.0 %collective-permute-start.24 = (f32[8,128]{1,0:T(8,128)S(1)}, f32[8,128]{1,0:T(8,128)S(1)}, u32[]{:S(2)}, u32[]{:S(2)}) collective-permute-start(f32[8,128]{1,0:T(8,128)S(1)} %add_add_fusion.1), channel_id=1, source_target_pairs={{0,2},{1,3},{2,0},{3,1},{4,6},{5,7},{6,4},{7,5},{8,10},{9,11},{10,... | collective-permute-start | bytes 12296 | tf_op jit(solution)/shard_map/ppermute | solution.py:445
  107.6 4.5 %collective-permute-start.23 = (f32[8,128]{1,0:T(8,128)S(1)}, f32[8,128]{1,0:T(8,128)S(1)}, u32[]{:S(2)}, u32[]{:S(2)}) collective-permute-start(f32[8,128]{1,0:T(8,128)S(1)} %add_add_fusion.1), channel_id=1, source_target_pairs={{0,1},{1,2},{2,3},{3,0},{4,5},{5,6},{6,7},{7,4},{8,9},{9,10},{10,1... | collective-permute-start | bytes 12296 | tf_op jit(solution)/shard_map/ppermute | solution.py:445

commit v5 on v4

--- a/solution.py
+++ b/solution.py
@@ -23,6 +23,7 @@
 K_RIGHT = 2176
 K_PAD = 256
 HOP = 1
+PAD = 200
 BACK_HOP = 1
 TILE = 240
 TILES = NS // TILE
@@ -213,6 +214,7 @@
     for i in range(DEPTH - 1):
         fetch(i).start()
     put_slots(near, near_source, CAP, pc, act_wide, slot, position)
+    near[NEAR + CAP :, :] = jnp.zeros((PAD, LC), f32)
     both[...] = jnp.zeros_like(both)
     for start, size, ref in ((G, CR, pc), (RIGHT, G, pg)):
         part_high, part_low = halves(ref[...])
@@ -512,7 +514,7 @@
     stacked = shape(2 * CR, SD, dtype=bf16)
     high, low, partial, forth, project, near = pl.pallas_call(
         split_kernel,
-        out_shape=[pltpu.VMEM((NS, KP), bf16)] * 2 + [shape(NS, LC), stacked, stacked, info_block],
+        out_shape=[pltpu.VMEM((NS, KP), bf16)] * 2 + [shape(NS, LC), stacked, stacked, shape(NEAR + CAP + PAD, LC)],
         in_specs=[SM] * 3 + [ANY] + [VM] * 4,
         out_specs=[VM] * 6,
         scratch_shapes=[

time: 115 us -> 114 us (level)
  waiting for transfers between devices: 43 us -> 41.5 us
  transfers between devices with their start and end apart: 26 -> 26, of which waited for: 16 -> 15; matrix products, arithmetic and copies ran while one was open for 0% -> 0% of each run, Pallas kernels for 14% -> 15%
where the time goes in v5:
time: 114 us; the launch traced here: 113 us
  waiting for transfers between devices  41.5 us (36%)
  starting transfers between devices  35.4 us (31%)
  Pallas kernels  34.3 us (30%)
    ppermute x19, waiting for transfers between devices, sent(): return lax.ppermute(value, ('sub', 'body'), pairs)  37.9 us
    ppermute x19, starting transfers between devices, sent(): return lax.ppermute(value, ('sub', 'body'), pairs)  26.7 us
    pallas_call x1, Pallas kernels, per_device(): pl.pallas_call(split_kernel, out_shape=[pltpu.VMEM((NS, KP), bf16)] * 2 +...  10.4 us
    ppermute x7, starting transfers between devices, rotated(): return lax.ppermute(value, 'sub', pairs)  8.79 us
    pallas_call x1, Pallas kernels, per_device(): pl.pallas_call(first_kernel, out_shape=[far_block, seg_block, seg_block,...  7.14 us
    pallas_call x1, Pallas kernels, per_device(): pl.pallas_call(second_kernel, out_shape=[shape(NS, LC), shape(G, LC), sha...  4.66 us
    pallas_call x1, Pallas kernels, per_device(): pl.pallas_call(master_kernel, out_shape=[shape(NS, LC), shape(CR, LC)], i...  4.42 us
    ppermute x7, waiting for transfers between devices, rotated(): return lax.ppermute(value, 'sub', pairs)  3.64 us
  transfers between devices with their start and end apart: 26, of which 15 were waited for; matrix products, arithmetic and copies ran while one was open for 0% of the time, Pallas kernels for 15%

profile of v5, /device:TPU:1, one launch (start us, length us, event | category | flops | bytes accessed | tf_op | source)
XLA Modules:
  0.0 113.1 jit_solution(8411266213159298981)
XLA Ops:
  0.6 2.0 %pack.1 = (f32[1040,128]{1,0:T(8,128)S(1)}, f32[1024,128]{1,0:T(8,128)S(1)}, f32[1024,128]{1,0:T(8,128)S(1)}, f32[176,128]{1,0:T(8,128)S(1)}, f32[16,128]{1,0:T(...) custom-call(s32[1]{0:T(128)} %bitcast.me, s32[16]{0:T(128)} %bitcast.17, ...), custom_call_target="tpu_custom_call" | custom-call | tf_op jit(solution)/shard_map/pack/pallas_call | solution.py:493
  2.7 4.1 %collective-permute-start.1 = (f32[1040,128]{1,0:T(8,128)S(1)}, f32[1040,128]{1,0:T(8,128)S(1)}, u32[]{:S(2)}, u32[]{:S(2)}) collective-permute-start(f32[1040,128]{1,0:T(8,128)S(1)} %get-tuple-element.63), channel_id=1, source_target_pairs={{0,5},{1,6},{2,7},{3,4},{4,9},{5,10},{6,11},{7,8},{8,13},{9,14},{1... | collective-permute-start | bytes 1597448 | tf_op jit(solution)/shard_map/ppermute | solution.py:447
  6.8 1.0 copy-done
  7.8 10.4 %split.1 = (bf16[2400,2560]{1,0:T(8,128)(2,1)S(1)}, bf16[2400,2560]{1,0:T(8,128)(2,1)S(1)}, f32[2400,128]{1,0:T(8,128)S(1)}, bf16[2048,64]{1,0:T(8,128)(2,1)S(1)...) custom-call(s32[8]{0:T(128)S(1)} %get-tuple-element.57.near_source, s32[16]{0:T(128)S(1)} %get-tuple-element.56.position, ...), custom_call_target="tpu_custom_call" | custom-call | flops 6291456000 | bytes 23040000 | tf_op jit(solution)/shard_map/split/pallas_call | solution.py:515
  18.3 1.4 %collective-permute-start = (f32[720,128]{1,0:T(8,128)S(1)}, f32[720,128]{1,0:T(8,128)S(1)}, u32[]{:S(2)}, u32[]{:S(2)}) collective-permute-start(f32[720,128]{1,0:T(8,128)S(1)} %get-tuple-element.62), channel_id=1, source_target_pairs={{0,1},{1,2},{2,3},{3,0},{4,5},{5,6},{6,7},{7,4},{8,9},{9,10},{10,1... | collective-permute-start | bytes 1105928 | tf_op jit(solution)/shard_map/ppermute | solution.py:447
  19.6 0.0 collective-permute-done.1.far
  19.6 1.3 %relay.1 = (f32[536,128]{1,0:T(8,128)S(1)}, f32[696,128]{1,0:T(8,128)S(1)}, f32[520,128]{1,0:T(8,128)S(1)}, s32[32]{0:T(128)}) custom-call(f32[1040,128]{1,0:T(8,128)S(1)} %collective-permute-done.1.far, f32[176,128]{1,0:T(8,128)S(1)} %get-tuple-element.60.pg, f32[2400,128]{1,0:T(8,128)S(1)} %get-tuple-element.64.token.partial), custom_call_target="tpu_custom_call" | custom-call | tf_op jit(solution)/shard_map/relay/pallas_call | solution.py:535
  20.9 1.7 %collective-permute-start.2 = (f32[696,128]{1,0:T(8,128)S(1)}, f32[696,128]{1,0:T(8,128)S(1)}, u32[]{:S(2)}, u32[]{:S(2)}) collective-permute-start(f32[696,128]{1,0:T(8,128)S(1)} %get-tuple-element.66), channel_id=1, source_target_pairs={{0,4},{1,5},{2,6},{3,7},{4,8},{5,9},{6,10},{7,11},{8,12},{9,13},{1... | collective-permute-start | bytes 1069064 | tf_op jit(solution)/shard_map/ppermute | solution.py:447
  22.6 1.6 %collective-permute-start.3 = (f32[520,128]{1,0:T(8,128)S(1)}, f32[520,128]{1,0:T(8,128)S(1)}, u32[]{:S(2)}, u32[]{:S(2)}) collective-permute-start(f32[520,128]{1,0:T(8,128)S(1)} %get-tuple-element.67), channel_id=1, source_target_pairs={{0,8},{1,9},{2,10},{3,11},{4,12},{5,13},{6,14},{7,15},{8,16},{9,17... | collective-permute-start | bytes 798728 | tf_op jit(solution)/shard_map/ppermute | solution.py:447
  24.3 4.8 %collective-permute-done.in0 = f32[720,128]{1,0:T(8,128)S(1)} collective-permute-done((f32[720,128]{1,0:T(8,128)S(1)}, f32[720,128]{1,0:T(8,128)S(1)}, u32[]{:S(2)}, u32[]{:S(2)}) %collective-permute-start) | collective-permute-done | bytes 368672 | tf_op jit(solution)/shard_map/ppermute | solution.py:447
  29.1 7.9 %collective-permute-done.3.in3 = f32[520,128]{1,0:T(8,128)S(1)} collective-permute-done((f32[520,128]{1,0:T(8,128)S(1)}, f32[520,128]{1,0:T(8,128)S(1)}, u32[]{:S(2)}, u32[]{:S(2)}) %collective-permute-start.3) | collective-permute-done | bytes 266272 | tf_op jit(solution)/shard_map/ppermute | solution.py:447
  37.0 7.1 %first.1 = (f32[1024,128]{1,0:T(8,128)S(1)}, f32[512,128]{1,0:T(8,128)S(1)}, f32[512,128]{1,0:T(8,128)S(1)}, f32[688,128]{1,0:T(8,128)S(1)}, f32[512,128]{1,0:T(...) custom-call(s32[1]{0:T(128)} %bitcast.me, ...), custom_call_target="tpu_custom_call" | custom-call | tf_op jit(solution)/shard_map/first/pallas_call | solution.py:546
  44.2 0.1 collective-permute-start.5
  44.3 0.2 collective-permute-start.6
  44.5 2.8 %collective-permute-start.4 = (f32[512,128]{1,0:T(8,128)S(1)}, f32[512,128]{1,0:T(8,128)S(1)}, u32[]{:S(2)}, u32[]{:S(2)}) collective-permute-start(f32[512,128]{1,0:T(8,128)S(1)} %get-tuple-element.76), channel_id=1, source_target_pairs={{0,3},{1,0},{2,1},{3,2},{4,7},{5,4},{6,5},{7,6},{8,11},{9,8},{10,9... | collective-permute-start | bytes 786440 | tf_op jit(solution)/shard_map/ppermute | solution.py:447
  47.3 2.2 %collective-permute-start.7 = (f32[512,128]{1,0:T(8,128)S(1)}, f32[512,128]{1,0:T(8,128)S(1)}, u32[]{:S(2)}, u32[]{:S(2)}) collective-permute-start(f32[512,128]{1,0:T(8,128)S(1)} %get-tuple-element.82), channel_id=1, source_target_pairs={{0,120},{1,121},{2,122},{3,123},{4,124},{5,125},{6,126},{7,127},{8... | collective-permute-start | bytes 786440 | tf_op jit(solution)/shard_map/ppermute | solution.py:447
  49.5 1.1 collective-permute-done.4.token.near
  50.6 5.1 %collective-permute-done.7.r3 = f32[512,128]{1,0:T(8,128)S(1)} collective-permute-done((f32[512,128]{1,0:T(8,128)S(1)}, f32[512,128]{1,0:T(8,128)S(1)}, u32[]{:S(2)}, u32[]{:S(2)}) %collective-permute-start.7) | collective-permute-done | bytes 262176 | tf_op jit(solution)/shard_map/ppermute | solution.py:447
  55.7 2.0 %collective-permute-done.5.far = f32[1024,128]{1,0:T(8,128)S(1)} collective-permute-done((f32[1024,128]{1,0:T(8,128)S(1)}, f32[1024,128]{1,0:T(8,128)S(1)}, u32[]{:S(2)}, u32[]{:S(2)}) %collective-permute-start.5) | collective-permute-done | bytes 524320 | tf_op jit(solution)/shard_map/ppermute | solution.py:447
  57.7 0.7 exchange.1
  58.5 0.1 collective-permute-start.9
  58.5 1.6 %collective-permute-start.10 = (f32[512,128]{1,0:T(8,128)S(1)}, f32[512,128]{1,0:T(8,128)S(1)}, u32[]{:S(2)}, u32[]{:S(2)}) collective-permute-start(f32[512,128]{1,0:T(8,128)S(1)} %get-tuple-element.86), channel_id=1, source_target_pairs={{0,1},{1,2},{2,3},{3,0},{4,5},{5,6},{6,7},{7,4},{8,9},{9,10},{10,1... | collective-permute-start | bytes 786440 | tf_op jit(solution)/shard_map/ppermute | solution.py:447
  60.1 1.8 %collective-permute-start.8 = (f32[1024,128]{1,0:T(8,128)S(1)}, f32[1024,128]{1,0:T(8,128)S(1)}, u32[]{:S(2)}, u32[]{:S(2)}) collective-permute-start(f32[1024,128]{1,0:T(8,128)S(1)} %get-tuple-element.84), channel_id=1, source_target_pairs={{0,127},{1,124},{2,125},{3,126},{4,3},{5,0},{6,1},{7,2},{8,7},{9,4... | collective-permute-start | bytes 1572872 | tf_op jit(solution)/shard_map/ppermute | solution.py:447
  61.9 5.4 %collective-permute-done.10.f0 = f32[512,128]{1,0:T(8,128)S(1)} collective-permute-done((f32[512,128]{1,0:T(8,128)S(1)}, f32[512,128]{1,0:T(8,128)S(1)}, u32[]{:S(2)}, u32[]{:S(2)}) %collective-permute-start.10) | collective-permute-done | bytes 262176 | tf_op jit(solution)/shard_map/ppermute | solution.py:447
  67.3 6.2 %collective-permute-done.11.f3 = f32[512,128]{1,0:T(8,128)S(1)} collective-permute-done((f32[512,128]{1,0:T(8,128)S(1)}, f32[512,128]{1,0:T(8,128)S(1)}, u32[]{:S(2)}, u32[]{:S(2)}) %collective-permute-start.11) | collective-permute-done | bytes 262176 | tf_op jit(solution)/shard_map/ppermute | solution.py:447
  73.5 4.4 %master.1 = (f32[2400,128]{1,0:T(8,128)S(1)}, f32[1024,128]{1,0:T(8,128)S(1)}) custom-call(s32[32]{0:T(128)S(1)} %get-tuple-element.74.slots, f32[512,128]{1,0:T(8,128)S(1)} %collective-permute-done.10.f0, f32[512,128]{1,0:T(8,128)S(1)} %get-tuple-element.87.f1, f32[688,128]{1,0:T(8,128)S(1)} %collective-permute-done.9.f2, ...), custom_call_target="tpu_custom_call" | custom-call | flops 2831155200 | bytes 1048576 | tf_op jit(solution)/shard_map/master/pallas_call | solution.py:581
  77.9 4.7 %second.1 = (f32[2400,128]{1,0:T(8,128)S(1)}, f32[176,128]{1,0:T(8,128)S(1)}, f32[1024,128]{1,0:T(8,128)S(1)}, f32[8,128]{1,0:T(8,128)S(1)}) custom-call(s32[1]{0:T(128)} %bitcast.me, s32[16]{0:T(128)S(1)} %get-tuple-element.75.place, f32[512,128]{1,0:T(8,128)S(1)} %collective-permute-done.4.token.near, f32[1024,128]{1,0:T(8,128)S(1)} %collective-permute-done.8.far, ...), custom_call_target="tpu_custom_call" | custom-call | tf_op jit(solution)/shard_map/second/pallas_call | solution.py:592
  82.6 1.0 reply.1
  83.5 1.0 collective-permute-start.12
  84.6 1.3 %collective-permute-start.14 = (f32[8,128]{1,0:T(8,128)S(1)}, f32[8,128]{1,0:T(8,128)S(1)}, u32[]{:S(2)}, u32[]{:S(2)}) collective-permute-start(f32[8,128]{1,0:T(8,128)S(1)} %get-tuple-element.97), channel_id=1, source_target_pairs={{0,16},{4,20},{8,24},{12,28},{16,0},{20,4},{24,8},{28,12},{32,48},... | collective-permute-start | bytes 12296 | tf_op jit(solution)/shard_map/ppermute | solution.py:460
  85.9 0.9 collective-permute-start.13
  86.7 0.6 collective-permute-done.15
  87.3 1.2 %collective-permute-done.14 = f32[8,128]{1,0:T(8,128)S(1)} collective-permute-done((f32[8,128]{1,0:T(8,128)S(1)}, f32[8,128]{1,0:T(8,128)S(1)}, u32[]{:S(2)}, u32[]{:S(2)}) %collective-permute-start.14) | collective-permute-done | bytes 4128 | tf_op jit(solution)/shard_map/ppermute | solution.py:460
  88.6 1.0 collective-permute-done.13
  89.5 5.1 %collective-permute-start.16 = (f32[8,128]{1,0:T(8,128)S(1)}, f32[8,128]{1,0:T(8,128)S(1)}, u32[]{:S(2)}, u32[]{:S(2)}) collective-permute-start(f32[8,128]{1,0:T(8,128)S(1)} %add_add_fusion.2), channel_id=1, source_target_pairs={{0,4},{4,0},{8,12},{12,8},{16,20},{20,16},{24,28},{28,24},{32,36},... | collective-permute-start | bytes 12296 | tf_op jit(solution)/shard_map/ppermute | solution.py:460
  94.7 0.8 collective-permute-done.16
  95.5 1.0 collective-permute-start.22
  96.4 0.6 collective-permute-start.20
  97.0 0.7 select.1
  97.7 1.5 %collective-permute-start.17 = (f32[512,128]{1,0:T(8,128)S(1)}, f32[512,128]{1,0:T(8,128)S(1)}, u32[]{:S(2)}, u32[]{:S(2)}) collective-permute-start(f32[512,128]{1,0:T(8,128)S(1)} %get-tuple-element.98), channel_id=1, source_target_pairs={{0,4},{1,5},{2,6},{3,7},{4,8},{5,9},{6,10},{7,11},{8,12},{9,13},{1... | collective-permute-start | bytes 786440 | tf_op jit(solution)/shard_map/ppermute | solution.py:447
  99.2 4.1 %collective-permute-start.19 = (f32[512,128]{1,0:T(8,128)S(1)}, f32[512,128]{1,0:T(8,128)S(1)}, u32[]{:S(2)}, u32[]{:S(2)}) collective-permute-start(f32[512,128]{1,0:T(8,128)S(1)} %get-tuple-element.101), channel_id=1, source_target_pairs={{0,120},{1,121},{2,122},{3,123},{4,124},{5,125},{6,126},{7,127},{8... | collective-permute-start | bytes 786440 | tf_op jit(solution)/shard_map/ppermute | solution.py:447
  103.4 2.4 %collective-permute-start.25 = (f32[8,128]{1,0:T(8,128)S(1)}, f32[8,128]{1,0:T(8,128)S(1)}, u32[]{:S(2)}, u32[]{:S(2)}) collective-permute-start(f32[8,128]{1,0:T(8,128)S(1)} %add_add_fusion.1), channel_id=1, source_target_pairs={{0,3},{1,0},{2,1},{3,2},{4,7},{5,4},{6,5},{7,6},{8,11},{9,8},{10,9... | collective-permute-start | bytes 12296 | tf_op jit(solution)/shard_map/ppermute | solution.py:447
  105.8 0.8 collective-permute-done.25
  106.5 0.0 collective-permute-start.23
  106.6 3.2 %collective-permute-done.24 = f32[8,128]{1,0:T(8,128)S(1)} collective-permute-done((f32[8,128]{1,0:T(8,128)S(1)}, f32[8,128]{1,0:T(8,128)S(1)}, u32[]{:S(2)}, u32[]{:S(2)}) %collective-permute-start.24) | collective-permute-done | bytes 4128 | tf_op jit(solution)/shard_map/ppermute | solution.py:447
  109.7 1.3 %collective-permute-done.23 = f32[8,128]{1,0:T(8,128)S(1)} collective-permute-done((f32[8,128]{1,0:T(8,128)S(1)}, f32[8,128]{1,0:T(8,128)S(1)}, u32[]{:S(2)}, u32[]{:S(2)}) %collective-permute-start.23) | collective-permute-done | bytes 4128 | tf_op jit(solution)/shard_map/ppermute | solution.py:447
  111.0 0.1 collective-permute-done.18.s2
  111.2 2.0 %last.1 = (f32[176,128]{1,0:T(8,128)}, f32[1024,128]{1,0:T(8,128)}, f32[176,128]{1,0:T(8,128)}, f32[1024,128]{1,0:T(8,128)}) custom-call(s32[1]{0:T(128)} %bitcast.me, s32[16]{0:T(128)S(1)} %get-tuple-element.56.position, f32[512,128]{1,0:T(8,128)S(1)} %collective-permute-done.17.s0, f32[512,128]{1,0:T(8,128)S(1)} %get-tuple-element.99.s1, ...), custom_call_target="tpu_custom_call" | custom-call | tf_op jit(solution)/shard_map/last/pallas_call | solution.py:625
  (20 shorter events, 0.1 us)
Async XLA Ops:
  2.7 17.0 %collective-permute-start.1 = (f32[1040,128]{1,0:T(8,128)S(1)}, f32[1040,128]{1,0:T(8,128)S(1)}, u32[]{:S(2)}, u32[]{:S(2)}) collective-permute-start(f32[1040,128]{1,0:T(8,128)S(1)} %get-tuple-element.63), channel_id=1, source_target_pairs={{0,5},{1,6},{2,7},{3,4},{4,9},{5,10},{6,11},{7,8},{8,13},{9,14},{1... | collective-permute-start | bytes 1597448 | tf_op jit(solution)/shard_map/ppermute | solution.py:447
  6.8 1.0 copy-start
  18.3 10.8 %collective-permute-start = (f32[720,128]{1,0:T(8,128)S(1)}, f32[720,128]{1,0:T(8,128)S(1)}, u32[]{:S(2)}, u32[]{:S(2)}) collective-permute-start(f32[720,128]{1,0:T(8,128)S(1)} %get-tuple-element.62), channel_id=1, source_target_pairs={{0,1},{1,2},{2,3},{3,0},{4,5},{5,6},{6,7},{7,4},{8,9},{9,10},{10,1... | collective-permute-start | bytes 1105928 | tf_op jit(solution)/shard_map/ppermute | solution.py:447
  20.9 16.1 %collective-permute-start.2 = (f32[696,128]{1,0:T(8,128)S(1)}, f32[696,128]{1,0:T(8,128)S(1)}, u32[]{:S(2)}, u32[]{:S(2)}) collective-permute-start(f32[696,128]{1,0:T(8,128)S(1)} %get-tuple-element.66), channel_id=1, source_target_pairs={{0,4},{1,5},{2,6},{3,7},{4,8},{5,9},{6,10},{7,11},{8,12},{9,13},{1... | collective-permute-start | bytes 1069064 | tf_op jit(solution)/shard_map/ppermute | solution.py:447
  22.6 14.4 %collective-permute-start.3 = (f32[520,128]{1,0:T(8,128)S(1)}, f32[520,128]{1,0:T(8,128)S(1)}, u32[]{:S(2)}, u32[]{:S(2)}) collective-permute-start(f32[520,128]{1,0:T(8,128)S(1)} %get-tuple-element.67), channel_id=1, source_target_pairs={{0,8},{1,9},{2,10},{3,11},{4,12},{5,13},{6,14},{7,15},{8,16},{9,17... | collective-permute-start | bytes 798728 | tf_op jit(solution)/shard_map/ppermute | solution.py:447
  44.2 13.6 %collective-permute-start.5 = (f32[1024,128]{1,0:T(8,128)S(1)}, f32[1024,128]{1,0:T(8,128)S(1)}, u32[]{:S(2)}, u32[]{:S(2)}) collective-permute-start(f32[1024,128]{1,0:T(8,128)S(1)} %get-tuple-element.79), channel_id=1, source_target_pairs={{0,5},{1,6},{2,7},{3,4},{4,9},{5,10},{6,11},{7,8},{8,13},{9,14},{1... | collective-permute-start | bytes 1572872 | tf_op jit(solution)/shard_map/ppermute | solution.py:447
  44.3 11.4 %collective-permute-start.6 = (f32[688,128]{1,0:T(8,128)S(1)}, f32[688,128]{1,0:T(8,128)S(1)}, u32[]{:S(2)}, u32[]{:S(2)}) collective-permute-start(f32[688,128]{1,0:T(8,128)S(1)} %get-tuple-element.81), channel_id=1, source_target_pairs={{0,124},{1,125},{2,126},{3,127},{4,0},{5,1},{6,2},{7,3},{8,4},{9,5... | collective-permute-start | bytes 1056776 | tf_op jit(solution)/shard_map/ppermute | solution.py:447
  44.5 6.1 %collective-permute-start.4 = (f32[512,128]{1,0:T(8,128)S(1)}, f32[512,128]{1,0:T(8,128)S(1)}, u32[]{:S(2)}, u32[]{:S(2)}) collective-permute-start(f32[512,128]{1,0:T(8,128)S(1)} %get-tuple-element.76), channel_id=1, source_target_pairs={{0,3},{1,0},{2,1},{3,2},{4,7},{5,4},{6,5},{7,6},{8,11},{9,8},{10,9... | collective-permute-start | bytes 786440 | tf_op jit(solution)/shard_map/ppermute | solution.py:447
  47.3 8.4 %collective-permute-start.7 = (f32[512,128]{1,0:T(8,128)S(1)}, f32[512,128]{1,0:T(8,128)S(1)}, u32[]{:S(2)}, u32[]{:S(2)}) collective-permute-start(f32[512,128]{1,0:T(8,128)S(1)} %get-tuple-element.82), channel_id=1, source_target_pairs={{0,120},{1,121},{2,122},{3,123},{4,124},{5,125},{6,126},{7,127},{8... | collective-permute-start | bytes 786440 | tf_op jit(solution)/shard_map/ppermute | solution.py:447
  58.5 15.0 %collective-permute-start.9 = (f32[688,128]{1,0:T(8,128)S(1)}, f32[688,128]{1,0:T(8,128)S(1)}, u32[]{:S(2)}, u32[]{:S(2)}) collective-permute-start(f32[688,128]{1,0:T(8,128)S(1)} %get-tuple-element.85), channel_id=1, source_target_pairs={{0,4},{1,5},{2,6},{3,7},{4,8},{5,9},{6,10},{7,11},{8,12},{9,13},{1... | collective-permute-start | bytes 1056776 | tf_op jit(solution)/shard_map/ppermute | solution.py:447
  58.5 8.7 %collective-permute-start.10 = (f32[512,128]{1,0:T(8,128)S(1)}, f32[512,128]{1,0:T(8,128)S(1)}, u32[]{:S(2)}, u32[]{:S(2)}) collective-permute-start(f32[512,128]{1,0:T(8,128)S(1)} %get-tuple-element.86), channel_id=1, source_target_pairs={{0,1},{1,2},{2,3},{3,0},{4,5},{5,6},{6,7},{7,4},{8,9},{9,10},{10,1... | collective-permute-start | bytes 786440 | tf_op jit(solution)/shard_map/ppermute | solution.py:447
  60.1 13.4 %collective-permute-start.11 = (f32[512,128]{1,0:T(8,128)S(1)}, f32[512,128]{1,0:T(8,128)S(1)}, u32[]{:S(2)}, u32[]{:S(2)}) collective-permute-start(f32[512,128]{1,0:T(8,128)S(1)} %get-tuple-element.88), channel_id=1, source_target_pairs={{0,8},{1,9},{2,10},{3,11},{4,12},{5,13},{6,14},{7,15},{8,16},{9,17... | collective-permute-start | bytes 786440 | tf_op jit(solution)/shard_map/ppermute | solution.py:447
  60.1 17.8 %collective-permute-start.8 = (f32[1024,128]{1,0:T(8,128)S(1)}, f32[1024,128]{1,0:T(8,128)S(1)}, u32[]{:S(2)}, u32[]{:S(2)}) collective-permute-start(f32[1024,128]{1,0:T(8,128)S(1)} %get-tuple-element.84), channel_id=1, source_target_pairs={{0,127},{1,124},{2,125},{3,126},{4,3},{5,0},{6,1},{7,2},{8,7},{9,4... | collective-permute-start | bytes 1572872 | tf_op jit(solution)/shard_map/ppermute | solution.py:447
  83.5 13.5 %collective-permute-start.12 = (f32[1032,128]{1,0:T(8,128)S(1)}, f32[1032,128]{1,0:T(8,128)S(1)}, u32[]{:S(2)}, u32[]{:S(2)}) collective-permute-start(f32[1032,128]{1,0:T(8,128)S(1)} %get-tuple-element.96), channel_id=1, source_target_pairs={{0,127},{1,124},{2,125},{3,126},{4,3},{5,0},{6,1},{7,2},{8,7},{9,4... | collective-permute-start | bytes 1585160 | tf_op jit(solution)/shard_map/ppermute | solution.py:447
  84.6 2.8 %collective-permute-start.15 = (f32[8,128]{1,0:T(8,128)S(1)}, f32[8,128]{1,0:T(8,128)S(1)}, u32[]{:S(2)}, u32[]{:S(2)}) collective-permute-start(f32[8,128]{1,0:T(8,128)S(1)} %get-tuple-element.97), channel_id=1, source_target_pairs={{0,24},{4,28},{8,0},{12,4},{16,8},{20,12},{24,16},{28,20},{32,56},... | collective-permute-start | bytes 12296 | tf_op jit(solution)/shard_map/ppermute | solution.py:460
  84.6 4.0 %collective-permute-start.14 = (f32[8,128]{1,0:T(8,128)S(1)}, f32[8,128]{1,0:T(8,128)S(1)}, u32[]{:S(2)}, u32[]{:S(2)}) collective-permute-start(f32[8,128]{1,0:T(8,128)S(1)} %get-tuple-element.97), channel_id=1, source_target_pairs={{0,16},{4,20},{8,24},{12,28},{16,0},{20,4},{24,8},{28,12},{32,48},... | collective-permute-start | bytes 12296 | tf_op jit(solution)/shard_map/ppermute | solution.py:460
  85.9 3.7 %collective-permute-start.13 = (f32[8,128]{1,0:T(8,128)S(1)}, f32[8,128]{1,0:T(8,128)S(1)}, u32[]{:S(2)}, u32[]{:S(2)}) collective-permute-start(f32[8,128]{1,0:T(8,128)S(1)} %get-tuple-element.97), channel_id=1, source_target_pairs={{0,8},{4,12},{8,16},{12,20},{16,24},{20,28},{24,0},{28,4},{32,40},... | collective-permute-start | bytes 12296 | tf_op jit(solution)/shard_map/ppermute | solution.py:460
  89.5 6.0 %collective-permute-start.16 = (f32[8,128]{1,0:T(8,128)S(1)}, f32[8,128]{1,0:T(8,128)S(1)}, u32[]{:S(2)}, u32[]{:S(2)}) collective-permute-start(f32[8,128]{1,0:T(8,128)S(1)} %add_add_fusion.2), channel_id=1, source_target_pairs={{0,4},{4,0},{8,12},{12,8},{16,20},{20,16},{24,28},{28,24},{32,36},... | collective-permute-start | bytes 12296 | tf_op jit(solution)/shard_map/ppermute | solution.py:460
  95.5 7.9 %collective-permute-start.22 = (f32[8,128]{1,0:T(8,128)S(1)}, f32[8,128]{1,0:T(8,128)S(1)}, u32[]{:S(2)}, u32[]{:S(2)}) collective-permute-start(f32[8,128]{1,0:T(8,128)S(1)} %add.33.token), channel_id=1, source_target_pairs={{0,96},{4,100},{8,104},{12,108},{16,112},{20,116},{24,120},{28,124... | collective-permute-start | bytes 12296 | tf_op jit(solution)/shard_map/ppermute | solution.py:460
  96.4 6.9 %collective-permute-start.21 = (f32[8,128]{1,0:T(8,128)S(1)}, f32[8,128]{1,0:T(8,128)S(1)}, u32[]{:S(2)}, u32[]{:S(2)}) collective-permute-start(f32[8,128]{1,0:T(8,128)S(1)} %add.33.token), channel_id=1, source_target_pairs={{0,64},{4,68},{8,72},{12,76},{16,80},{20,84},{24,88},{28,92},{32,9... | collective-permute-start | bytes 12296 | tf_op jit(solution)/shard_map/ppermute | solution.py:460
  96.4 6.9 %collective-permute-start.20 = (f32[8,128]{1,0:T(8,128)S(1)}, f32[8,128]{1,0:T(8,128)S(1)}, u32[]{:S(2)}, u32[]{:S(2)}) collective-permute-start(f32[8,128]{1,0:T(8,128)S(1)} %add.33.token), channel_id=1, source_target_pairs={{0,32},{4,36},{8,40},{12,44},{16,48},{20,52},{24,56},{28,60},{32,6... | collective-permute-start | bytes 12296 | tf_op jit(solution)/shard_map/ppermute | solution.py:460
  97.7 13.3 %collective-permute-start.17 = (f32[512,128]{1,0:T(8,128)S(1)}, f32[512,128]{1,0:T(8,128)S(1)}, u32[]{:S(2)}, u32[]{:S(2)}) collective-permute-start(f32[512,128]{1,0:T(8,128)S(1)} %get-tuple-element.98), channel_id=1, source_target_pairs={{0,4},{1,5},{2,6},{3,7},{4,8},{5,9},{6,10},{7,11},{8,12},{9,13},{1... | collective-permute-start | bytes 786440 | tf_op jit(solution)/shard_map/ppermute | solution.py:447
  99.2 11.8 %collective-permute-start.19 = (f32[512,128]{1,0:T(8,128)S(1)}, f32[512,128]{1,0:T(8,128)S(1)}, u32[]{:S(2)}, u32[]{:S(2)}) collective-permute-start(f32[512,128]{1,0:T(8,128)S(1)} %get-tuple-element.101), channel_id=1, source_target_pairs={{0,120},{1,121},{2,122},{3,123},{4,124},{5,125},{6,126},{7,127},{8... | collective-permute-start | bytes 786440 | tf_op jit(solution)/shard_map/ppermute | solution.py:447
  103.4 7.8 %collective-permute-start.18 = (f32[688,128]{1,0:T(8,128)S(1)}, f32[688,128]{1,0:T(8,128)S(1)}, u32[]{:S(2)}, u32[]{:S(2)}) collective-permute-start(f32[688,128]{1,0:T(8,128)S(1)} %get-tuple-element.100), channel_id=1, source_target_pairs={{0,124},{1,125},{2,126},{3,127},{4,0},{5,1},{6,2},{7,3},{8,4},{9,5... | collective-permute-start | bytes 1056776 | tf_op jit(solution)/shard_map/ppermute | solution.py:447
  103.4 3.1 %collective-permute-start.25 = (f32[8,128]{1,0:T(8,128)S(1)}, f32[8,128]{1,0:T(8,128)S(1)}, u32[]{:S(2)}, u32[]{:S(2)}) collective-permute-start(f32[8,128]{1,0:T(8,128)S(1)} %add_add_fusion.1), channel_id=1, source_target_pairs={{0,3},{1,0},{2,1},{3,2},{4,7},{5,4},{6,5},{7,6},{8,11},{9,8},{10,9... | collective-permute-start | bytes 12296 | tf_op jit(solution)/shard_map/ppermute | solution.py:447
  105.8 4.0 %collective-permute-start.24 = (f32[8,128]{1,0:T(8,128)S(1)}, f32[8,128]{1,0:T(8,128)S(1)}, u32[]{:S(2)}, u32[]{:S(2)}) collective-permute-start(f32[8,128]{1,0:T(8,128)S(1)} %add_add_fusion.1), channel_id=1, source_target_pairs={{0,2},{1,3},{2,0},{3,1},{4,6},{5,7},{6,4},{7,5},{8,10},{9,11},{10,... | collective-permute-start | bytes 12296 | tf_op jit(solution)/shard_map/ppermute | solution.py:447
  106.5 4.5 %collective-permute-start.23 = (f32[8,128]{1,0:T(8,128)S(1)}, f32[8,128]{1,0:T(8,128)S(1)}, u32[]{:S(2)}, u32[]{:S(2)}) collective-permute-start(f32[8,128]{1,0:T(8,128)S(1)} %add_add_fusion.1), channel_id=1, source_target_pairs={{0,1},{1,2},{2,3},{3,0},{4,5},{5,6},{6,7},{7,4},{8,9},{9,10},{10,1... | collective-permute-start | bytes 12296 | tf_op jit(solution)/shard_map/ppermute | solution.py:447
